TPU v7x, 32 devices: a whole 2x2x4 slice. The times are simulated.
32 devices in a mesh: fsdp: 32 (over z, y, x, core).
Axes of the slice: x: 2, y: 2, z: 4, core: 2. Of those that a mesh axis runs over, the one named last changes fastest.
Arguments:
- src_in: bfloat16 [32768, 512], P('fsdp'), may hold values from -6 to 6
- tgt_in: bfloat16 [32768, 512], P('fsdp'), may hold values from -6 to 6
- src_len: int32 [32, 16], P('fsdp'), may hold values from 0 to 250, as said below
- tgt_len: int32 [32, 16], P('fsdp'), may hold values from 0 to 250, as said below
- tgt_mask: int32 [32768], P('fsdp'), may hold values 0 or 1
- enc_cot: bfloat16 [32768, 512], P('fsdp'), may hold values from -6 to 6
- dec_cot: bfloat16 [32768, 512], P('fsdp'), may hold values from -6 to 6
- enc_master: float32 [6144, 512], P('fsdp')
- enc_first: float32 [6144, 512], P('fsdp')
- enc_second: float32 [6144, 512], P('fsdp'), as said below
- dec_master: float32 [8192, 512], P('fsdp')
- dec_first: float32 [8192, 512], P('fsdp')
- dec_second: float32 [8192, 512], P('fsdp'), as said below
- small_master: float32 [11, 512], P(None, 'fsdp')
- small_first: float32 [11, 512], P(None, 'fsdp')
- small_second: float32 [11, 512], P(None, 'fsdp'), as said below
Outputs:
- enc_out: bfloat16 [32768, 512], P('fsdp')
- dec_out: bfloat16 [32768, 512], P('fsdp')
- src_grad: float32 [32768, 512], P('fsdp')
- tgt_grad: float32 [32768, 512], P('fsdp')
- enc_new: float32 [6144, 512], P('fsdp')
- enc_first_new: float32 [6144, 512], P('fsdp')
- encoder_second_moment_updated: float32 [6144, 512], P('fsdp')
- enc_copy_new: bfloat16 [6144, 512], P('fsdp')
- dec_new: float32 [8192, 512], P('fsdp')
- dec_first_new: float32 [8192, 512], P('fsdp')
- dec_second_new: float32 [8192, 512], P('fsdp')
- dec_copy_new: bfloat16 [8192, 512], P('fsdp')
- small_grad: float32 [11, 512], P(None, 'fsdp')
- small_first_new: float32 [11, 512], P(None, 'fsdp')
- small_second_new: float32 [11, 512], P(None, 'fsdp')
Inputs may be any that keep to these rules, and one draw needn't show every extreme that they name: `src_len`: nonzero lengths are at least 5; zeros stand only after all nonzero entries of a row; a row sums to at most 1024; every row holds the length 250. `tgt_len`: zero exactly where src_len is zero; nonzero lengths are at least 5; a row sums to at most 1024; every row holds the length 250. `enc_second`: Positive. `dec_second`: Positive. `small_second`: Positive.
All inputs are finite; a program needn't handle non-finite values. No bound on the sum of `tgt_mask` on one device may be relied on, other than what follows from the above.
Results may differ from a plain program's by a relative error of at most 0.02.
The roundings to bfloat16 on the way count: a program that leaves them out, or rounds other values in their place, can miss the bound.
Values may be sent and summed in bfloat16 or wider, within the bound.
No kernel may reach another device: no remote copies, remote signals or barrier semaphores. Data moves between devices by JAX's collectives and lax.ppermute only.
A program may use at most 256 MiB of HBM per device.

v0:
```python
import jax
import jax.numpy as jnp
from jax import lax
from jax.sharding import PartitionSpec as P

HEADS = 8
QBLOCK = 512
STEPS = 7


rate = 0.02
beta_one = 0.9
beta_two = 0.98
epsilon = 1e-06
decay = 0.01
floor_value = -1000000000.0
root_half = 0.7071067811865476
inverse_root_tau = 0.3989422804014327


def segments(lengths, number):
    bounds = jnp.cumsum(lengths)
    places = jnp.arange(number, dtype=jnp.int32)
    owners = jnp.sum((places[:, None] >= bounds[None, :]).astype(jnp.int32), axis=1)
    return (owners, places < bounds[-1])


def product(former, latter):
    return jnp.dot(former, latter, preferred_element_type=jnp.float32)


def inner_rows(former, latter):
    return lax.dot_general(
        former, latter, (((0,), (0,)), ((), ())), preferred_element_type=jnp.float32
    )


def against(former, latter):
    return lax.dot_general(
        former, latter, (((1,), (1,)), ((), ())), preferred_element_type=jnp.float32
    )


def smooth_gate(values):
    return jax.nn.gelu(values, approximate=False)


def gate_slope(values):
    return (
        0.5 * (1.0 + jax.scipy.special.erf(values * root_half))
        + values * jnp.exp(-0.5 * values * values) * inverse_root_tau
    )


def norm_forward(values, gain_row, shift_row):
    average = jnp.mean(values, axis=-1, keepdims=True)
    centered = values - average
    spread = jnp.mean(centered * centered, axis=-1, keepdims=True)
    inverse = lax.rsqrt(spread + 1e-05)
    normed = centered * inverse
    return (normed * gain_row + shift_row, normed, inverse)


def norm_backward(upstream, normed, inverse, gain_row):
    gain_grad = jnp.sum(upstream * normed, axis=0)
    shift_grad = jnp.sum(upstream, axis=0)
    scaled = upstream * gain_row
    result = inverse * (
        scaled
        - jnp.mean(scaled, axis=-1, keepdims=True)
        - normed * jnp.mean(scaled * normed, axis=-1, keepdims=True)
    )
    return (result, gain_grad, shift_grad)


def attend(queries, key_rows, value_rows, allowed):
    number = queries.shape[0] // QBLOCK
    key_heads = key_rows.reshape(key_rows.shape[0], HEADS, -1)
    value_heads = value_rows.reshape(value_rows.shape[0], HEADS, -1)
    factor = key_heads.shape[2] ** (-0.5)
    query_blocks = queries.reshape(number, QBLOCK, HEADS, -1)
    allowed_blocks = allowed.reshape(number, QBLOCK, -1)

    def attend_one_block(pieces):
        query_block, allowed_block = pieces
        scores = (
            jnp.einsum("qhd,khd->hqk", query_block, key_heads, preferred_element_type=jnp.float32)
            * factor
        )
        scores = jnp.where(allowed_block[None], scores, floor_value)
        row_max = jnp.max(scores, axis=-1, keepdims=True)
        totals = jnp.log(jnp.sum(jnp.exp(scores - row_max), axis=-1, keepdims=True)) + row_max
        weights = jnp.exp(scores - totals).astype(jnp.bfloat16)
        context = jnp.einsum(
            "hqk,khd->qhd", weights, value_heads, preferred_element_type=jnp.float32
        )
        return (context, totals)

    context, totals = lax.map(attend_one_block, (query_blocks, allowed_blocks))
    return (context.reshape(queries.shape[0], -1), totals)


def attention_backward(upstream, queries, key_rows, value_rows, allowed, totals):
    number = queries.shape[0] // QBLOCK
    key_heads = key_rows.reshape(key_rows.shape[0], HEADS, -1)
    value_heads = value_rows.reshape(value_rows.shape[0], HEADS, -1)
    factor = key_heads.shape[2] ** (-0.5)
    query_blocks = queries.reshape(number, QBLOCK, HEADS, -1)
    upstream_blocks = upstream.reshape(number, QBLOCK, HEADS, -1)
    allowed_blocks = allowed.reshape(number, QBLOCK, -1)

    def attention_one_block(carried, pieces):
        key_grad, value_grad = carried
        query_block, allowed_block, upstream_block, total_block = pieces
        scores = (
            jnp.einsum("qhd,khd->hqk", query_block, key_heads, preferred_element_type=jnp.float32)
            * factor
        )
        scores = jnp.where(allowed_block[None], scores, floor_value)
        weights = jnp.exp(scores - total_block)
        weight_grad = jnp.einsum(
            "qhd,khd->hqk", upstream_block, value_heads, preferred_element_type=jnp.float32
        )
        row_dot = jnp.sum(weights * weight_grad, axis=-1, keepdims=True)
        score_grad = (weights * (weight_grad - row_dot)).astype(jnp.bfloat16)
        query_grad = (
            jnp.einsum("hqk,khd->qhd", score_grad, key_heads, preferred_element_type=jnp.float32)
            * factor
        )
        key_grad = (
            key_grad
            + jnp.einsum(
                "hqk,qhd->khd", score_grad, query_block, preferred_element_type=jnp.float32
            )
            * factor
        )
        value_grad = value_grad + jnp.einsum(
            "hqk,qhd->khd",
            weights.astype(jnp.bfloat16),
            upstream_block,
            preferred_element_type=jnp.float32,
        )
        return ((key_grad, value_grad), query_grad)

    zero_heads = jnp.zeros(key_heads.shape, jnp.float32)
    (key_grad, value_grad), query_grad = lax.scan(
        attention_one_block,
        (zero_heads, zero_heads),
        (query_blocks, allowed_blocks, upstream_blocks, totals),
    )
    return (
        query_grad.reshape(queries.shape[0], -1),
        key_grad.reshape(key_rows.shape[0], -1),
        value_grad.reshape(value_rows.shape[0], -1),
    )


def enc_split(rows, model_width):
    inner = (rows.shape[0] - 4 * model_width) // 2
    return (
        rows[: 3 * model_width].reshape(model_width, 3 * model_width),
        rows[3 * model_width : 4 * model_width],
        rows[4 * model_width : 4 * model_width + inner].reshape(model_width, inner),
        rows[4 * model_width + inner :],
    )


def dec_split(rows, model_width):
    inner = (rows.shape[0] - 8 * model_width) // 2
    return (
        rows[: 3 * model_width].reshape(model_width, 3 * model_width),
        rows[3 * model_width : 4 * model_width],
        rows[4 * model_width : 5 * model_width],
        rows[5 * model_width : 7 * model_width].reshape(model_width, 2 * model_width),
        rows[7 * model_width : 8 * model_width],
        rows[8 * model_width : 8 * model_width + inner].reshape(model_width, inner),
        rows[8 * model_width + inner :],
    )


def moments(gradient, first, second):
    first_new = beta_one * first + (1.0 - beta_one) * gradient
    second_new = beta_two * second + (1.0 - beta_two) * gradient * gradient
    return (first_new, second_new)


def adamw(weight, gradient, first, second):
    first_new, second_new = moments(gradient, first, second)
    moved = weight - rate * (
        first_new
        / (1.0 - beta_one**STEPS)
        / (jnp.sqrt(second_new / (1.0 - beta_two**STEPS)) + epsilon)
        + decay * weight
    )
    return (moved, first_new, second_new)


def on_device(
    src_in,
    tgt_in,
    src_len,
    tgt_len,
    tgt_mask,
    enc_cot,
    dec_cot,
    enc_master,
    enc_first,
    enc_second,
    dec_master,
    dec_first,
    dec_second,
    small_master,
    small_first,
    small_second,
):
    model_width = src_in.shape[1]
    brain_float_type = jnp.bfloat16
    src_owners, src_filled = segments(src_len[0], src_in.shape[0])
    tgt_owners, tgt_filled = segments(tgt_len[0], tgt_in.shape[0])
    enc_allowed = (src_owners[:, None] == src_owners[None, :]) & src_filled[None, :]
    self_allowed = (tgt_owners[:, None] == tgt_owners[None, :]) & tgt_filled[None, :]
    cross_allowed = (tgt_owners[:, None] == src_owners[None, :]) & src_filled[None, :]
    src_live = src_filled.astype(jnp.float32)[:, None]
    tgt_live = tgt_filled.astype(jnp.float32)[:, None]
    enc_copy = enc_master.astype(brain_float_type)
    dec_copy = dec_master.astype(brain_float_type)
    small_copy = small_master.astype(brain_float_type)
    enc_rows, small_rows = (
        lax.all_gather(enc_copy, "fsdp", axis=0, tiled=True),
        lax.all_gather(small_copy, "fsdp", axis=1, tiled=True),
    )
    smalls = small_rows.astype(jnp.float32)
    qkv_w, out_w, up_w, down_w = enc_split(enc_rows, model_width)
    src_values = src_in.astype(jnp.float32)
    enc_qkv = product(src_in, qkv_w).astype(brain_float_type)
    enc_query = enc_qkv[:, :model_width]
    enc_keys = enc_qkv[:, model_width : 2 * model_width]
    enc_values = enc_qkv[:, 2 * model_width :]
    enc_context, enc_totals = attend(enc_query, enc_keys, enc_values, enc_allowed)
    enc_context = enc_context.astype(brain_float_type)
    enc_mid, mid_normed, mid_inverse = norm_forward(
        src_values + product(enc_context, out_w) * src_live, smalls[0], smalls[1]
    )
    enc_mid_low = enc_mid.astype(brain_float_type)
    enc_inner = product(enc_mid_low, up_w)
    enc_hidden = smooth_gate(enc_inner).astype(brain_float_type)
    encoded, end_normed, end_inverse = norm_forward(
        enc_mid + product(enc_hidden, down_w), smalls[2], smalls[3]
    )
    memory = encoded.astype(brain_float_type)
    dec_rows = lax.all_gather(dec_copy, "fsdp", axis=0, tiled=True)
    sqkv_w, sout_w, cq_w, ckv_w, cout_w, dup_w, ddown_w = dec_split(dec_rows, model_width)
    masked = tgt_mask[:, None] == 1
    start = jnp.where(masked, smalls[10][None, :], tgt_in.astype(jnp.float32))
    start_low = start.astype(brain_float_type)
    self_qkv = product(start_low, sqkv_w).astype(brain_float_type)
    self_query = self_qkv[:, :model_width]
    self_keys = self_qkv[:, model_width : 2 * model_width]
    self_values = self_qkv[:, 2 * model_width :]
    self_context, self_totals = attend(self_query, self_keys, self_values, self_allowed)
    self_context = self_context.astype(brain_float_type)
    dec_one, one_normed, one_inverse = norm_forward(
        start + product(self_context, sout_w) * tgt_live, smalls[4], smalls[5]
    )
    dec_one_low = dec_one.astype(brain_float_type)
    cross_query = product(dec_one_low, cq_w).astype(brain_float_type)
    cross_pair = product(memory, ckv_w).astype(brain_float_type)
    cross_keys = cross_pair[:, :model_width]
    cross_values = cross_pair[:, model_width:]
    cross_context, cross_totals = attend(cross_query, cross_keys, cross_values, cross_allowed)
    cross_context = cross_context.astype(brain_float_type)
    dec_two, two_normed, two_inverse = norm_forward(
        dec_one + product(cross_context, cout_w) * tgt_live, smalls[6], smalls[7]
    )
    decoder_second_rounded = dec_two.astype(brain_float_type)
    dec_inner = product(decoder_second_rounded, dup_w)
    dec_hidden = smooth_gate(dec_inner).astype(brain_float_type)
    decoded, three_normed, three_inverse = norm_forward(
        dec_two + product(dec_hidden, ddown_w), smalls[8], smalls[9]
    )
    back_sqkv, back_sout, back_cq, back_ckv, back_cout, back_dup, back_ddown = dec_split(
        lax.all_gather(dec_copy, "fsdp", axis=0, tiled=True), model_width
    )
    d_three, gain_five, shift_five = norm_backward(
        dec_cot.astype(jnp.float32), three_normed, three_inverse, smalls[8]
    )
    d_ffn = d_three.astype(brain_float_type)
    grad_ddown = inner_rows(dec_hidden, d_ffn)
    d_inner = (against(d_ffn, back_ddown) * gate_slope(dec_inner)).astype(brain_float_type)
    grad_dup = inner_rows(decoder_second_rounded, d_inner)
    d_two = d_three + against(d_inner, back_dup)
    d_two_sum, gain_four, shift_four = norm_backward(d_two, two_normed, two_inverse, smalls[6])
    d_cross = (d_two_sum * tgt_live).astype(brain_float_type)
    grad_cout = inner_rows(cross_context, d_cross)
    d_cross_context = against(d_cross, back_cout).astype(brain_float_type)
    d_cquery, d_ckeys, d_cvalues = attention_backward(
        d_cross_context, cross_query, cross_keys, cross_values, cross_allowed, cross_totals
    )
    d_cquery = d_cquery.astype(brain_float_type)
    d_cpair = jnp.concatenate([d_ckeys, d_cvalues], axis=1).astype(brain_float_type)
    grad_cq = inner_rows(dec_one_low, d_cquery)
    grad_ckv = inner_rows(memory, d_cpair)
    d_memory = against(d_cpair, back_ckv)
    d_one = d_two_sum + against(d_cquery, back_cq)
    d_one_sum, gain_three, shift_three = norm_backward(d_one, one_normed, one_inverse, smalls[4])
    d_self = (d_one_sum * tgt_live).astype(brain_float_type)
    grad_sout = inner_rows(self_context, d_self)
    d_self_context = against(d_self, back_sout).astype(brain_float_type)
    self_query_gradient, self_key_gradient, self_value_gradient = attention_backward(
        d_self_context, self_query, self_keys, self_values, self_allowed, self_totals
    )
    self_projection_gradient = jnp.concatenate(
        [self_query_gradient, self_key_gradient, self_value_gradient], axis=1
    ).astype(brain_float_type)
    grad_sqkv = inner_rows(start_low, self_projection_gradient)
    d_start = d_one_sum + against(self_projection_gradient, back_sqkv)
    tgt_grad = jnp.where(masked, 0.0, d_start)
    mask_grad = jnp.sum(jnp.where(masked, d_start, 0.0), axis=0)
    dec_grad = jnp.concatenate(
        [
            grad_sqkv.reshape(-1, model_width),
            grad_sout,
            grad_cq,
            grad_ckv.reshape(-1, model_width),
            grad_cout,
            grad_dup.reshape(-1, model_width),
            grad_ddown,
        ],
        axis=0,
    )
    back_qkv, back_out, back_up, back_down = enc_split(
        lax.all_gather(enc_copy, "fsdp", axis=0, tiled=True), model_width
    )
    d_encoded = enc_cot.astype(jnp.float32) + d_memory
    d_end, gain_two, shift_two = norm_backward(d_encoded, end_normed, end_inverse, smalls[2])
    d_effn = d_end.astype(brain_float_type)
    grad_down = inner_rows(enc_hidden, d_effn)
    d_einner = (against(d_effn, back_down) * gate_slope(enc_inner)).astype(brain_float_type)
    grad_up = inner_rows(enc_mid_low, d_einner)
    d_mid = d_end + against(d_einner, back_up)
    d_mid_sum, gain_one, shift_one = norm_backward(d_mid, mid_normed, mid_inverse, smalls[0])
    d_eattn = (d_mid_sum * src_live).astype(brain_float_type)
    grad_out = inner_rows(enc_context, d_eattn)
    d_econtext = against(d_eattn, back_out).astype(brain_float_type)
    d_equery, d_ekeys, d_evalues = attention_backward(
        d_econtext, enc_query, enc_keys, enc_values, enc_allowed, enc_totals
    )
    d_eqkv = jnp.concatenate([d_equery, d_ekeys, d_evalues], axis=1).astype(brain_float_type)
    grad_qkv = inner_rows(src_in, d_eqkv)
    src_grad = d_mid_sum + against(d_eqkv, back_qkv)
    enc_grad = jnp.concatenate(
        [grad_qkv.reshape(-1, model_width), grad_out, grad_up.reshape(-1, model_width), grad_down],
        axis=0,
    )
    small_grad = jnp.stack(
        [
            gain_one,
            shift_one,
            gain_two,
            shift_two,
            gain_three,
            shift_three,
            gain_four,
            shift_four,
            gain_five,
            shift_five,
            mask_grad,
        ]
    )
    dec_summed, enc_summed, small_summed = (
        lax.psum_scatter(dec_grad, "fsdp", scatter_dimension=0, tiled=True),
        lax.psum_scatter(enc_grad, "fsdp", scatter_dimension=0, tiled=True),
        lax.psum_scatter(small_grad, "fsdp", scatter_dimension=1, tiled=True),
    )
    share = 1.0 / lax.axis_size("fsdp")
    enc_summed = enc_summed * share
    dec_summed = dec_summed * share
    small_summed = small_summed * share
    enc_new, enc_first_new, encoder_second_moment_updated = adamw(
        enc_master, enc_summed, enc_first, enc_second
    )
    dec_new, dec_first_new, dec_second_new = adamw(dec_master, dec_summed, dec_first, dec_second)
    small_first_new, small_second_new = moments(small_summed, small_first, small_second)
    return (
        memory,
        decoded.astype(brain_float_type),
        src_grad,
        tgt_grad,
        enc_new,
        enc_first_new,
        encoder_second_moment_updated,
        enc_new.astype(brain_float_type),
        dec_new,
        dec_first_new,
        dec_second_new,
        dec_new.astype(brain_float_type),
        small_summed,
        small_first_new,
        small_second_new,
    )


def solution(mesh):
    placed = (
        P("fsdp", None),
        P("fsdp", None),
        P("fsdp", None),
        P("fsdp", None),
        P("fsdp"),
        P("fsdp", None),
        P("fsdp", None),
        P("fsdp", None),
        P("fsdp", None),
        P("fsdp", None),
        P("fsdp", None),
        P("fsdp", None),
        P("fsdp", None),
        P(None, "fsdp"),
        P(None, "fsdp"),
        P(None, "fsdp"),
    )
    return jax.shard_map(
        on_device,
        mesh=mesh,
        in_specs=placed,
        out_specs=(
            P("fsdp", None),
            P("fsdp", None),
            P("fsdp", None),
            P("fsdp", None),
            P("fsdp", None),
            P("fsdp", None),
            P("fsdp", None),
            P("fsdp", None),
            P("fsdp", None),
            P("fsdp", None),
            P("fsdp", None),
            P("fsdp", None),
            P(None, "fsdp"),
            P(None, "fsdp"),
            P(None, "fsdp"),
        ),
        check_vma=False,
    )
```

profile of v0, /device:TPU:0, one launch (start us, length us, event | category | flops | bytes accessed | tf_op | source)
XLA Modules:
  0.0 1047.1 jit_solution(16476869847142518927)
XLA Ops:
  14.7 43.8 %all_gather.12 = bf16[11,512]{0,1:T(8,128)(2,1)S(1)} all-gather(bf16[11,16]{0,1:T(8,128)(2,1)S(1)} %copy.199), channel_id=1, replica_groups=mesh['fsdp'=32] {'fsdp'}, dimensions={1}, use_global_device_ids=true | all-gather | bytes 11616 | tf_op jit(solution)/shard_map/all_gather | solution.py:230
  73.6 10.3 all-gather.3.cloned.1.call-done
  98.4 28.7 %while.81 = (s32[]{:T(128)}, bf16[2,512,8,64]{1,3,2,0:T(8,128)(2,1)}, f32[2,8,512,1]{2,1,3,0:T(8,128)S(1)}, pred[2,512,1024]{2,1,0:T(8,128)(4,1)}, bf16[2,512,8,...) while((s32[]{:T(128)}, ...), condition=%wide.region_5.6_spmd, body=%wide.region_2.0_spmd.sunk | while | flops 1119875072 | bytes 65142940 | solution.py:99
  102.5 4.2 exponential_reduce_fusion.6
  106.8 4.9 fusion.292
  116.8 4.2 exponential_reduce_fusion.6
  121.1 4.9 fusion.292
  134.6 4.3 reshape.427
  142.0 22.3 %fusion.92 = (bf16[1024,2048]{1,0:T(8,128)(2,1)S(1)}, f32[1024,2048]{1,0:T(8,128)}) fusion(bf16[512,2048]{1,0:T(8,128)(2,1)S(1)} %copy-done.63, f32[1024,512]{0,1:T(8,128)S(1)} %get-tuple-element.912, f32[512]{0:T(512)S(1)} %get-tuple-element.764, f32[512]{0:T(512)S(1)} %get-tuple-element.765, f32[1024]{0:T(1024)S(1)} %add_rsqrt_fusion.4, ...), kind=kOutput, calls=%fused_computation.133 | convolution fusion | flops 2286419968 | bytes 16789504 | tf_op jit(solution)/shard_map/dot_general | solution.py:29
  184.5 28.7 %while.82 = (s32[]{:T(128)}, bf16[2,512,8,64]{1,3,2,0:T(8,128)(2,1)}, f32[2,8,512,1]{2,1,3,0:T(8,128)S(1)}, pred[2,512,1024]{2,1,0:T(8,128)(4,1)}, bf16[2,512,8,...) while((s32[]{:T(128)}, ...), condition=%wide.region_15.16_spmd, body=%wide.region_12.15_spmd.sunk | while | flops 1119875072 | bytes 65142940 | solution.py:99
  193.1 4.9 fusion.296
  207.3 4.9 fusion.296
  232.3 30.7 %while.83 = (s32[]{:T(128)}, bf16[2,512,8,64]{1,3,2,0:T(8,128)(2,1)S(1)}, f32[2,8,512,1]{2,1,3,0:T(8,128)S(1)}, pred[2,512,1024]{2,1,0:T(8,128)(4,1)}, bf16[2,51...) while((s32[]{:T(128)}, ...), condition=%wide.region_21.22_spmd, body=%wide.region_18.21_spmd.sunk | while | flops 1119875072 | bytes 56754784 | solution.py:99
  233.6 4.9 fusion.299
  242.7 5.0 fusion.300
  248.8 4.8 fusion.299
  258.0 5.0 fusion.300
  271.2 4.4 reshape.437
  275.6 23.6 %fusion.95 = (bf16[1024,2048]{1,0:T(8,128)(2,1)S(1)}, f32[1024,2048]{1,0:T(8,128)}) fusion(bf16[512,2048]{1,0:T(8,128)(2,1)} %reshape.437, f32[1024,512]{0,1:T(8,128)S(1)} %get-tuple-element.920, f32[512]{0:T(512)S(1)} %copy-done.158, f32[512]{0:T(512)S(1)} %copy-done.133, f32[1024]{0:T(1024)S(1)} %add_rsqrt_fusion.1, f32[1024]{0:T(1024)S(1)} %broadcast_multiply_fusion.12), kind=kOutput, calls=%fused_computation.136 | convolution fusion | flops 2286419968 | bytes 16789504 | tf_op jit(solution)/shard_map/dot_general | solution.py:29
  299.3 5.7 fusion.192
  308.0 7.4 fusion.101
  329.6 91.1 %while.84 = (s32[]{:T(128)}, f32[1024,8,64]{0,2,1:T(8,128)}, f32[1024,8,64]{0,2,1:T(8,128)}, bf16[2,512,8,64]{1,3,2,0:T(8,128)(2,1)}, bf16[2,512,8,64]{1,3,2,0:T...) while((s32[]{:T(128)}, f32[1024,8,64]{0,2,1:T(8,128)}, ...), condition=%wide.region_32.33_spmd.clone, body=%wide.region_30.32_spmd.clone.sunk | while | flops 2724982784 | bytes 213600496 | solution.py:146
  335.6 11.7 %multiply_reduce_fusion.23 = (f32[8,512]{1,0:T(8,128)}, f32[8,512,1024]{2,1,0:T(8,128)}) fusion(f32[8,512,1024]{2,1,0:T(8,128)S(1)} %fusion.310, f32[8,512]{1,0:T(8,128)} %dynamic-slice_bitcast_fusion.21, bf16[1024,8,64]{0,2,1:T(8,128)(2,1)} %get-tuple-element.1385, bf16[2,512,8,64]{1,3,2,0:T(8,128)(2,1)} %get-tuple-element.1383, ...), kind=kOutput, calls=%fused_computation.52.clone.1 | convolution fusion | flops 557838336 | bytes 35684864 | tf_op jit(solution)/shard_map/while/body/eval_jaxpr/qhd,khd->hqk/dot_general | solution.py:116
  347.3 9.3 multiply_convert_fusion.15
  356.6 6.6 bitcast_add_fusion.12
  363.2 7.9 fusion.311
  380.0 11.7 %multiply_reduce_fusion.23 = (f32[8,512]{1,0:T(8,128)}, f32[8,512,1024]{2,1,0:T(8,128)}) fusion(f32[8,512,1024]{2,1,0:T(8,128)S(1)} %fusion.310, f32[8,512]{1,0:T(8,128)} %dynamic-slice_bitcast_fusion.21, bf16[1024,8,64]{0,2,1:T(8,128)(2,1)} %get-tuple-element.1385, bf16[2,512,8,64]{1,3,2,0:T(8,128)(2,1)} %get-tuple-element.1383, ...), kind=kOutput, calls=%fused_computation.52.clone.1 | convolution fusion | flops 557838336 | bytes 35684864 | tf_op jit(solution)/shard_map/while/body/eval_jaxpr/qhd,khd->hqk/dot_general | solution.py:116
  391.7 9.3 multiply_convert_fusion.15
  401.0 7.2 bitcast_add_fusion.12
  408.2 7.9 fusion.311
  416.1 4.6 bitcast_add_fusion.13
  429.4 5.4 fusion.107
  434.9 4.9 multiply_reduce_fusion.6
  439.8 4.6 fusion.175
  444.4 4.4 fusion.147
  463.3 89.3 %while.86 = (s32[]{:T(128)}, f32[1024,8,64]{0,2,1:T(8,128)}, f32[1024,8,64]{0,2,1:T(8,128)}, bf16[2,512,8,64]{1,3,2,0:T(8,128)(2,1)}, bf16[2,512,8,64]{1,3,2,0:T...) while((s32[]{:T(128)}, f32[1024,8,64]{0,2,1:T(8,128)}, ...), condition=%wide.region_44.45_spmd.clone, body=%wide.region_42.44_spmd.clone.sunk | while | flops 2724982784 | bytes 217794832 | solution.py:146
  468.6 11.5 %multiply_reduce_fusion.25 = (f32[8,512]{1,0:T(8,128)}, f32[8,512,1024]{2,1,0:T(8,128)}) fusion(f32[8,512,1024]{2,1,0:T(8,128)S(1)} %fusion.332, f32[8,512]{1,0:T(8,128)} %dynamic-slice_bitcast_fusion.25, bf16[1024,8,64]{0,2,1:T(8,128)(2,1)S(1)} %get-tuple-element.1457, bf16[2,512,8,64]{1,3,2,0:T(8,128)(2,1)} %get-tuple-element.1455, ...), kind=kOutput, calls=%fused_computation.102.clone.1 | convolution fusion | flops 557838336 | bytes 35684864 | tf_op jit(solution)/shard_map/while/body/eval_jaxpr/qhd,khd->hqk/dot_general | solution.py:116
  480.1 9.4 multiply_convert_fusion.17
  489.4 6.6 bitcast_add_fusion.16
  496.0 7.7 fusion.333
  512.2 11.5 %multiply_reduce_fusion.25 = (f32[8,512]{1,0:T(8,128)}, f32[8,512,1024]{2,1,0:T(8,128)}) fusion(f32[8,512,1024]{2,1,0:T(8,128)S(1)} %fusion.332, f32[8,512]{1,0:T(8,128)} %dynamic-slice_bitcast_fusion.25, bf16[1024,8,64]{0,2,1:T(8,128)(2,1)S(1)} %get-tuple-element.1457, bf16[2,512,8,64]{1,3,2,0:T(8,128)(2,1)} %get-tuple-element.1455, ...), kind=kOutput, calls=%fused_computation.102.clone.1 | convolution fusion | flops 557838336 | bytes 35684864 | tf_op jit(solution)/shard_map/while/body/eval_jaxpr/qhd,khd->hqk/dot_general | solution.py:116
  523.6 9.4 multiply_convert_fusion.17
  533.0 7.2 bitcast_add_fusion.16
  540.2 7.7 fusion.333
  547.9 4.7 bitcast_add_fusion.17
  575.8 89.4 %while.85 = (s32[]{:T(128)}, f32[1024,8,64]{0,2,1:T(8,128)}, f32[1024,8,64]{0,2,1:T(8,128)}, bf16[2,512,8,64]{1,3,2,0:T(8,128)(2,1)}, bf16[2,512,8,64]{1,3,2,0:T...) while((s32[]{:T(128)}, f32[1024,8,64]{0,2,1:T(8,128)}, ...), condition=%wide.region_39.40_spmd.clone, body=%wide.region_37.39_spmd.clone.sunk | while | flops 2724982784 | bytes 217794832 | solution.py:146
  581.1 11.5 %multiply_reduce_fusion.24 = (f32[8,512]{1,0:T(8,128)}, f32[8,512,1024]{2,1,0:T(8,128)}) fusion(f32[8,512,1024]{2,1,0:T(8,128)S(1)} %fusion.321, f32[8,512]{1,0:T(8,128)} %dynamic-slice_bitcast_fusion.23, bf16[1024,8,64]{0,2,1:T(8,128)(2,1)S(1)} %get-tuple-element.1421, bf16[2,512,8,64]{1,3,2,0:T(8,128)(2,1)} %get-tuple-element.1419, ...), kind=kOutput, calls=%fused_computation.77.clone.1 | convolution fusion | flops 557838336 | bytes 35684864 | tf_op jit(solution)/shard_map/while/body/eval_jaxpr/qhd,khd->hqk/dot_general | solution.py:116
  592.5 9.4 multiply_convert_fusion.16
  601.9 6.6 bitcast_add_fusion.14
  608.5 7.7 fusion.322
  624.6 11.5 %multiply_reduce_fusion.24 = (f32[8,512]{1,0:T(8,128)}, f32[8,512,1024]{2,1,0:T(8,128)}) fusion(f32[8,512,1024]{2,1,0:T(8,128)S(1)} %fusion.321, f32[8,512]{1,0:T(8,128)} %dynamic-slice_bitcast_fusion.23, bf16[1024,8,64]{0,2,1:T(8,128)(2,1)S(1)} %get-tuple-element.1421, bf16[2,512,8,64]{1,3,2,0:T(8,128)(2,1)} %get-tuple-element.1419, ...), kind=kOutput, calls=%fused_computation.77.clone.1 | convolution fusion | flops 557838336 | bytes 35684864 | tf_op jit(solution)/shard_map/while/body/eval_jaxpr/qhd,khd->hqk/dot_general | solution.py:116
  636.0 9.4 multiply_convert_fusion.16
  645.4 7.3 bitcast_add_fusion.14
  652.7 7.8 fusion.322
  660.4 4.6 bitcast_add_fusion.15
  676.8 5.2 reshape.450
  682.1 8.7 pad_maximum_fusion
  692.3 6.7 fusion.171
  699.0 5.3 reshape.453
  708.8 6.0 fusion.146
  733.0 4.7 convolution_dynamic-update-slice_fusion
  743.4 5.2 convolution_add_fusion.2
  754.4 99.2 %reduce-scatter.6.cloned.1.call-done = f32[192,512]{1,0:T(8,128)} async-done(((f32[6144,512]{1,0:T(8,128)}), f32[192,512]{1,0:T(8,128)}) %reduce-scatter.6.cloned.1.call-update) | async-done | bytes 393232 | tf_op jit(solution)/shard_map/reduce_scatter | solution.py:372
  856.0 181.6 %reduce-scatter.8.cloned.1.call-done = f32[256,512]{1,0:T(8,128)} async-done(((f32[8192,512]{1,0:T(8,128)}), f32[256,512]{1,0:T(8,128)}) %reduce-scatter.8.cloned.1.call-update) | async-done | bytes 524304 | tf_op jit(solution)/shard_map/reduce_scatter | solution.py:371
  (613 shorter events, 290.6 us)
Async XLA Ops:
  7.2 55.4 %copy-start.146 = (s32[1024]{0:T(1024)S(1)}, s32[1024]{0:T(1024)}, u32[]{:S(2)}) copy-start(s32[1024]{0:T(1024)} %param.32) | copy-start | bytes 12292
  7.2 56.7 %copy-start.77 = (bf16[1024,512]{1,0:T(8,128)(2,1)S(1)}, bf16[1024,512]{1,0:T(8,128)(2,1)}, u32[]{:S(2)}) copy-start(bf16[1024,512]{1,0:T(8,128)(2,1)} %param.29) | copy-start | bytes 3145732
  7.2 76.7 %all-gather.3.cloned.1.call-start = ((), (), s32[]{:S(2)}) async-start(), calls=%async_computation.3 | async-start | bytes 6488064 | tf_op jit(solution)/shard_map/all_gather | solution.py:229
  9.0 160.7 %all-gather.5.cloned.1.call-start = ((), (), s32[]{:S(2)}) async-start(), calls=%async_computation.4 | async-start | bytes 8650752 | tf_op jit(solution)/shard_map/all_gather | solution.py:251
  10.9 56.8 %copy-start.78 = (bf16[1024,512]{1,0:T(8,128)(2,1)S(1)}, bf16[1024,512]{1,0:T(8,128)(2,1)}, u32[]{:S(2)}) copy-start(bf16[1024,512]{1,0:T(8,128)(2,1)} %param.34) | copy-start | bytes 3145732
  10.9 742.1 %reduce-scatter.10.cloned.1.call-start = ((), (), s32[]{:S(2)}) async-start(), calls=%async_computation.7 | async-start | bytes 270336
  58.5 10.4 copy-start.79
  60.6 103.7 %copy-start.135 = (f32[512]{0:T(512)}, f32[512]{0:T(512)S(1)}, u32[]{:S(2)}) copy-start(f32[512]{0:T(512)S(1)} %get-tuple-element.765) | copy-start | bytes 6148
  60.6 103.7 %copy-start.160 = (f32[512]{0:T(512)}, f32[512]{0:T(512)S(1)}, u32[]{:S(2)}) copy-start(f32[512]{0:T(512)S(1)} %get-tuple-element.764) | copy-start | bytes 6148
  61.3 77.7 %copy-start.104 = (f32[1024]{0:T(1024)}, f32[1024]{0:T(1024)S(1)}, u32[]{:S(2)}) copy-start(f32[1024]{0:T(1024)S(1)} %fusion.163) | copy-start | bytes 12292
  127.2 7.4 copy-start.3
  127.2 7.4 copy-start.9
  127.2 7.4 copy-start.11
  127.2 7.4 copy-start.89
  138.9 25.4 %slice-start = ((s8[6291456]{0:T(1024)(128)(4,1)}), s8[4194304]{0:T(1024)(128)(4,1)S(1)}, s32[]{:S(2)}) async-start(s8[6291456]{0:T(1024)(128)(4,1)} %bitcast.360), calls=%async_computation.8 | async-start | bytes 8388608
  141.6 22.7 %copy-start.36 = (f32[1024,512]{0,1:T(8,128)}, f32[1024,512]{0,1:T(8,128)S(1)}, u32[]{:S(2)}) copy-start(f32[1024,512]{0,1:T(8,128)S(1)} %get-tuple-element.912) | copy-start | bytes 6291460
  141.6 22.7 %copy-start.109 = (f32[1024]{0:T(1024)}, f32[1024]{0:T(1024)S(1)}, u32[]{:S(2)}) copy-start(f32[1024]{0:T(1024)S(1)} %broadcast_multiply_fusion.15) | copy-start | bytes 12292
  141.9 22.4 %copy-start.124 = (f32[1024]{0:T(1024)}, f32[1024]{0:T(1024)S(1)}, u32[]{:S(2)}) copy-start(f32[1024]{0:T(1024)S(1)} %add_rsqrt_fusion.4) | copy-start | bytes 12292
  142.0 22.4 %slice-start.1 = ((s8[6291456]{0:T(1024)(128)(4,1)}), s8[2097152]{0:T(1024)(128)(4,1)S(1)}, s32[]{:S(2)}) async-start(s8[6291456]{0:T(1024)(128)(4,1)} %bitcast.360), calls=%async_computation.9 | async-start | bytes 4194304
  219.1 45.9 %copy-start.99 = (f32[1024]{0:T(1024)}, f32[1024]{0:T(1024)S(1)}, u32[]{:S(2)}) copy-start(f32[1024]{0:T(1024)S(1)} %broadcast_multiply_fusion.13) | copy-start | bytes 12292
  219.4 45.6 %copy-start.106 = (f32[1024]{0:T(1024)}, f32[1024]{0:T(1024)S(1)}, u32[]{:S(2)}) copy-start(f32[1024]{0:T(1024)S(1)} %add_rsqrt_fusion.2) | copy-start | bytes 12292
  267.4 52.1 %copy-start.41 = (f32[1024,512]{0,1:T(8,128)}, f32[1024,512]{0,1:T(8,128)S(1)}, u32[]{:S(2)}) copy-start(f32[1024,512]{0,1:T(8,128)S(1)} %get-tuple-element.920) | copy-start | bytes 6291460
  267.4 52.1 %copy-start.114 = (f32[1024]{0:T(1024)}, f32[1024]{0:T(1024)S(1)}, u32[]{:S(2)}) copy-start(f32[1024]{0:T(1024)S(1)} %broadcast_multiply_fusion.12) | copy-start | bytes 12292
  267.8 51.8 %copy-start.129 = (f32[1024]{0:T(1024)}, f32[1024]{0:T(1024)S(1)}, u32[]{:S(2)}) copy-start(f32[1024]{0:T(1024)S(1)} %add_rsqrt_fusion.1) | copy-start | bytes 12292
  267.8 7.8 copy-start.133
  267.8 7.8 copy-start.158
  299.3 8.8 slice-start.5
  299.3 6.1 copy-start.59
  299.3 6.1 copy-start.131
  299.3 6.1 copy-start.138
  299.3 8.7 slice-start.6
  305.0 10.4 copy-start.39
  305.1 10.4 copy-start.112
  305.4 10.1 copy-start.127
  308.0 7.4 copy-start.147
  308.0 7.4 copy-start.149
  308.0 7.4 copy-start.65
  356.6 14.5 %copy-start = (f32[8,512,1024]{2,1,0:T(8,128)S(1)}, f32[8,512,1024]{2,1,0:T(8,128)}, u32[]{:S(2)}) copy-start(f32[8,512,1024]{2,1,0:T(8,128)} %get-tuple-element.1257) | copy-start | bytes 50331652 | tf_op jit(solution)/shard_map/while
  363.2 7.9 copy-start.17
  401.0 15.1 %copy-start = (f32[8,512,1024]{2,1,0:T(8,128)S(1)}, f32[8,512,1024]{2,1,0:T(8,128)}, u32[]{:S(2)}) copy-start(f32[8,512,1024]{2,1,0:T(8,128)} %get-tuple-element.1257) | copy-start | bytes 50331652 | tf_op jit(solution)/shard_map/while
  408.2 7.9 copy-start.17
  423.1 5.9 slice-start.2
  439.8 10.4 slice-start.7
  444.4 5.8 copy-start.107
  444.4 5.8 copy-start.122
  456.7 6.6 copy-start.6
  489.4 14.3 %copy-start.1 = (f32[8,512,1024]{2,1,0:T(8,128)S(1)}, f32[8,512,1024]{2,1,0:T(8,128)}, u32[]{:S(2)}) copy-start(f32[8,512,1024]{2,1,0:T(8,128)} %get-tuple-element.1281) | copy-start | bytes 50331652 | tf_op jit(solution)/shard_map/while
  496.0 7.7 copy-start.18
  533.0 14.9 %copy-start.1 = (f32[8,512,1024]{2,1,0:T(8,128)S(1)}, f32[8,512,1024]{2,1,0:T(8,128)}, u32[]{:S(2)}) copy-start(f32[8,512,1024]{2,1,0:T(8,128)} %get-tuple-element.1281) | copy-start | bytes 50331652 | tf_op jit(solution)/shard_map/while
  540.2 7.7 copy-start.18
  555.4 6.2 copy-start.85
  555.5 6.0 copy-start.72
  562.6 291.0 %reduce-scatter.6.cloned.1.call-start = ((), (), s32[]{:S(2)}) async-start(), calls=%async_computation.5 | async-start | bytes 12976128 | tf_op jit(solution)/shard_map/reduce_scatter | solution.py:372
  569.4 6.3 copy-start.4
  601.9 14.3 %copy-start.2 = (f32[8,512,1024]{2,1,0:T(8,128)S(1)}, f32[8,512,1024]{2,1,0:T(8,128)}, u32[]{:S(2)}) copy-start(f32[8,512,1024]{2,1,0:T(8,128)} %get-tuple-element.1269) | copy-start | bytes 50331652 | tf_op jit(solution)/shard_map/while
  608.5 7.7 copy-start.16
  645.4 15.0 %copy-start.2 = (f32[8,512,1024]{2,1,0:T(8,128)S(1)}, f32[8,512,1024]{2,1,0:T(8,128)}, u32[]{:S(2)}) copy-start(f32[8,512,1024]{2,1,0:T(8,128)} %get-tuple-element.1269) | copy-start | bytes 50331652 | tf_op jit(solution)/shard_map/while
  652.7 7.8 copy-start.16
  690.8 346.9 %reduce-scatter.8.cloned.1.call-start = ((), (), s32[]{:S(2)}) async-start(), calls=%async_computation.6 | async-start | bytes 17301504 | tf_op jit(solution)/shard_map/reduce_scatter | solution.py:371
  748.6 105.0 %copy-start.69 = (f32[192,512]{1,0:T(8,128)S(1)}, f32[192,512]{1,0:T(8,128)}, u32[]{:S(2)}) copy-start(f32[192,512]{1,0:T(8,128)} %param.35) | copy-start | bytes 1179652
  748.6 105.0 %copy-start.95 = (f32[192,512]{1,0:T(8,128)S(1)}, f32[192,512]{1,0:T(8,128)}, u32[]{:S(2)}) copy-start(f32[192,512]{1,0:T(8,128)} %param.36) | copy-start | bytes 1179652
  748.6 289.0 %copy-start.62 = (f32[256,512]{1,0:T(8,128)S(1)}, f32[256,512]{1,0:T(8,128)}, u32[]{:S(2)}) copy-start(f32[256,512]{1,0:T(8,128)} %param.38) | copy-start | bytes 1572868
  748.6 289.0 %copy-start.87 = (f32[256,512]{1,0:T(8,128)S(1)}, f32[256,512]{1,0:T(8,128)}, u32[]{:S(2)}) copy-start(f32[256,512]{1,0:T(8,128)} %param.39) | copy-start | bytes 1572868
  748.6 289.0 %copy-start.88 = (f32[256,512]{1,0:T(8,128)S(1)}, f32[256,512]{1,0:T(8,128)}, u32[]{:S(2)}) copy-start(f32[256,512]{1,0:T(8,128)} %param.40) | copy-start | bytes 1572868
  (144 other events, 493.8 us)
Sparse Core Ops, SparseCore 0:
  11.5 72.3 all-gather.2
  87.3 76.0 all-gather.4
  562.7 132.1 reduce-scatter.9
  701.8 151.7 reduce-scatter.5
  855.8 181.8 reduce-scatter.7
where the time goes:
time: 1060 us; the launch traced here: 1050 us
  matrix products  406 us (38%)
  waiting for transfers between devices  291 us (27%)
  local copies, waits for them, and re-layouts  170 us (16%)
  other arithmetic  118 us (11%)
  blocking collectives  43.8 us (4%)
  between operations  16.3 us (2%)
    reduce_scatter x1, waiting for transfers between devices, on_device(): lax.psum_scatter(dec_grad, 'fsdp', scatter_dimension=0, tiled=True)  182 us
    reduce_scatter x1, waiting for transfers between devices, on_device(): lax.psum_scatter(enc_grad, 'fsdp', scatter_dimension=0, tiled=True)  99.2 us
    dot_general x11, matrix products, product(): return jnp.dot(former, latter, preferred_element_type=jnp.float32)  71.8 us
    dot_general x6, matrix products, attention_one_block(): jnp.einsum('qhd,khd->hqk', query_block, key_heads, preferred_element_type...  69.3 us
    convert_element_type x6, other arithmetic, attention_one_block(): score_grad = (weights * (weight_grad - row_dot)).astype(jnp.bfloat16)  56 us
    unnamed x363, local copies, waits for them, and re-layouts  56 us
    dot_general x6, matrix products, attention_one_block(): jnp.einsum('hqk,khd->qhd', score_grad, key_heads, preferred_element_type=...  46.8 us
    all_gather x1, blocking collectives, on_device(): lax.all_gather(small_copy, 'fsdp', axis=1, tiled=True)  43.8 us
  transfers between devices with their start and end apart: 5, of which 3 were waited for; matrix products, arithmetic and copies ran while one was open for 27% of the time, Pallas kernels for 0%

commit v1 on v0

v1 whole, which is shorter than its diff:
```python
import functools

import jax
import jax.numpy as jnp
from jax import lax
from jax.experimental import pallas as pl
from jax.experimental.pallas import tpu as pltpu
from jax.sharding import PartitionSpec as P

HEADS = 8
HEAD = 64
STEPS = 7
TILE = 256
LANES = 128

rate = 0.02
beta_one = 0.9
beta_two = 0.98
epsilon = 1e-06
decay = 0.01
floor_value = -1000000000.0
root_half = 0.7071067811865476
inverse_root_tau = 0.3989422804014327

F32 = jnp.float32
LOW = jnp.bfloat16
VMEM_BYTES = 56 * 2**20


def nn(former, latter):
    return lax.dot_general(
        former, latter, (((1,), (0,)), ((), ())), preferred_element_type=F32
    )


def nt(former, latter):
    return lax.dot_general(
        former, latter, (((1,), (1,)), ((), ())), preferred_element_type=F32
    )


def turned(values):
    return values.astype(F32).T.astype(LOW)


def column_of(row):
    return jnp.broadcast_to(row, (8, row.shape[1])).T[:, 0:1]


def ln_forward(values, gain, shift):
    centered = values - jnp.mean(values, axis=-1, keepdims=True)
    spread = jnp.mean(centered * centered, axis=-1, keepdims=True)
    inverse = lax.rsqrt(spread + 1e-05)
    normed = centered * inverse
    return normed * gain + shift, normed, inverse


def ln_backward(upstream, normed, inverse, gain):
    scaled = upstream * gain
    first = jnp.mean(scaled, axis=-1, keepdims=True)
    second = jnp.mean(scaled * normed, axis=-1, keepdims=True)
    return inverse * (scaled - first - normed * second)


def phi_and_slope(values):
    size = jnp.abs(values)
    bell = jnp.exp(-0.5 * (values * values))
    part = 1.0 / (1.0 + (0.3275911 * root_half) * size)
    series = part * (
        0.254829592
        + part
        * (-0.284496736 + part * (1.421413741 + part * (-1.453152027 + part * 1.061405429)))
    )
    half_tail = (0.5 * series) * bell
    phi = jnp.where(values >= 0, 1.0 - half_tail, half_tail)
    return phi, phi + values * (bell * inverse_root_tau)


def one_head(pair, head):
    lane = lax.broadcasted_iota(jnp.int32, pair.shape, 1)
    keep = lane < HEAD if head % 2 == 0 else lane >= HEAD
    return jnp.where(keep, pair, jnp.zeros_like(pair))


def pair_columns(head):
    return slice(LANES * (head // 2), LANES * (head // 2) + LANES)


def head_rows(head):
    return slice(HEAD * head, HEAD * head + HEAD)


def block_of(ref, j):
    if len(ref.shape) == 4:
        return ref[:, j].reshape(ref.shape[0] * ref.shape[2], ref.shape[3])
    return ref[j]


def put_block(ref, j, values):
    if len(ref.shape) == 4:
        ref[:, j] = values.reshape(ref.shape[0], ref.shape[2], ref.shape[3])
    else:
        ref[j] = values


def call(kernel, grid, in_specs, out_specs, out_shape, scratch, flops, moved, name):
    return pl.pallas_call(
        kernel,
        grid_spec=pltpu.PrefetchScalarGridSpec(
            num_scalar_prefetch=1,
            grid=grid,
            in_specs=in_specs,
            out_specs=out_specs,
            scratch_shapes=scratch,
        ),
        out_shape=out_shape,
        compiler_params=pltpu.CompilerParams(vmem_limit_bytes=VMEM_BYTES),
        cost_estimate=pl.CostEstimate(
            flops=flops, bytes_accessed=moved, transcendentals=0
        ),
        name=name,
    )


def whole(shape):
    zeros = (0,) * len(shape)
    return pl.BlockSpec(shape, lambda i, *_: zeros)


def rows_of(width):
    return pl.BlockSpec((TILE, width), lambda i, *_: (i, 0))


def at_block(shape, *index):
    return pl.BlockSpec(shape, lambda i, *_: index)


def shaped(shape, kind):
    return jax.ShapeDtypeStruct(shape, kind)


def attend_tile(plan, i, keys, key_cols, query, owner_row, key_owner, vt, sc):
    scores, acc, top, total, masked_q = sc
    query = query * jnp.asarray(HEAD**-0.5, LOW)
    for h in range(HEADS):
        masked_q[h] = one_head(query[:, pair_columns(h)], h)
    top[...] = jnp.full_like(top, -1e30)
    total[...] = jnp.zeros_like(total)
    acc[...] = jnp.zeros_like(acc)
    lo = plan[0, i]
    hi = plan[1, i]

    def score_tile(j, carry):
        rows = pl.ds(pl.multiple_of(j * TILE, TILE), TILE)
        bias = jnp.where(key_owner[rows, 0:1] == owner_row, 0.0, floor_value)
        tops = []
        for h in range(HEADS):
            cols = pl.ds(key_cols + LANES * (h // 2), LANES)
            s = nt(keys[rows, cols], masked_q[h]) + bias
            scores[j, h] = s
            tops.append(jnp.max(s, axis=0, keepdims=True))
        top[...] = jnp.maximum(top[...], jnp.concatenate(tops, axis=0))
        return carry

    lax.fori_loop(lo, hi, score_tile, 0)

    def weigh_tile(j, carry):
        rows = pl.ds(pl.multiple_of(j * TILE, TILE), TILE)
        sums = []
        for h in range(HEADS):
            p = jnp.exp(scores[j, h] - top[h : h + 1, :])
            sums.append(jnp.sum(p, axis=0, keepdims=True))
            acc[head_rows(h), :] += nn(vt[head_rows(h), rows], p.astype(LOW))
        total[...] += jnp.concatenate(sums, axis=0)
        return carry

    lax.fori_loop(lo, hi, weigh_tile, 0)


def fwd_block_kernel(plan, *refs, cross, gain_row):
    if cross:
        (normed_in, memory, wq, wk_a, wk_b, wo, small, owner_q, owner_k,
         q_out, kv_out, ctx_out, lse_out, normed_out, inverse_out,
         kv, vt, mean_v, key_owner, scores, acc, top, total, masked_q) = refs
    else:
        (x_all, wqkv, wo, small, owner_q, owner_k,
         q_out, kv_out, ctx_out, lse_out, normed_out, inverse_out,
         kv, vt, mean_v, key_owner, scores, acc, top, total, masked_q, q_all) = refs
    i = pl.program_id(0)
    width = kv.shape[1] // 2

    @pl.when(i == 0)
    def _():
        key_owner[...] = jnp.broadcast_to(owner_k[...], (8, owner_k.shape[1])).T
        if cross:
            wk = jnp.concatenate([block_of(wk_a, 0), block_of(wk_b, 0)], axis=0)
            wv = jnp.concatenate([block_of(wk_a, 1), block_of(wk_b, 1)], axis=0)
        else:
            wq_all = block_of(wqkv, 0)
            wk = block_of(wqkv, 1)
            wv = block_of(wqkv, 2)
        sums = jnp.zeros((1, width), F32)
        for t in range(kv.shape[0] // TILE):
            rows = slice(t * TILE, t * TILE + TILE)
            x = memory[rows, :] if cross else x_all[rows, :]
            if not cross:
                q_all[rows, :] = nn(x, wq_all).astype(LOW)
            kv[rows, :width] = nn(x, wk).astype(LOW)
            v = nn(x, wv).astype(LOW)
            kv[rows, width:] = v
            v = v.astype(F32)
            vt[:, rows] = v.T.astype(LOW)
            sums = sums + jnp.sum(v, axis=0, keepdims=True)
        mean_v[...] = sums * (1.0 / kv.shape[0])

    mine = pl.ds(pl.multiple_of(i * TILE, TILE), TILE)
    if cross:
        resid = normed_in[...] * small[4:5, :] + small[5:6, :]
        query = nn(resid.astype(LOW), wq[...]).astype(LOW)
        q_out[...] = query
    else:
        resid = x_all[mine, :].astype(F32)
        query = q_all[mine, :]
        q_out[...] = query
    kv_out[...] = kv[mine, :]
    owner_row = owner_q[...]
    attend_tile(plan, i, kv, 0, query, owner_row, key_owner, vt, (scores, acc, top, total, masked_q))
    dead = owner_row < 0
    sums = jnp.where(dead, 1.0, total[...])
    share = 1.0 / sums
    lse_out[...] = jnp.where(dead, 0.0, top[...] + jnp.log(sums))
    for h in range(HEADS):
        acc[head_rows(h), :] = acc[head_rows(h), :] * share[h : h + 1, :]
    live = column_of(owner_row) >= 0
    context = jnp.where(live, acc[...].T, mean_v[...]).astype(LOW)
    ctx_out[...] = context
    added = nn(context, wo[...]) * live.astype(F32)
    _, normed, inverse = ln_forward(
        resid + added, small[gain_row : gain_row + 1, :], small[gain_row + 1 : gain_row + 2, :]
    )
    normed_out[...] = normed
    inverse_out[...] = jnp.broadcast_to(inverse, inverse_out.shape)


def attention_scratch(keys, width):
    return [
        pltpu.VMEM((keys, 2 * width), LOW),
        pltpu.VMEM((width, keys), LOW),
        pltpu.VMEM((1, width), F32),
        pltpu.VMEM((keys, 8), F32),
        pltpu.VMEM((keys // TILE, HEADS, TILE, TILE), F32),
        pltpu.VMEM((width, TILE), F32),
        pltpu.VMEM((HEADS, TILE), F32),
        pltpu.VMEM((HEADS, TILE), F32),
        pltpu.VMEM((HEADS, TILE, LANES), LOW),
    ]


def block_outs(queries, width):
    specs = [
        rows_of(width),
        rows_of(2 * width),
        rows_of(width),
        pl.BlockSpec((HEADS, TILE), lambda i, *_: (0, i)),
        rows_of(width),
        rows_of(LANES),
    ]
    shapes = [
        shaped((queries, width), LOW),
        shaped((queries, 2 * width), LOW),
        shaped((queries, width), LOW),
        shaped((HEADS, queries), F32),
        shaped((queries, width), F32),
        shaped((queries, LANES), F32),
    ]
    return specs, shapes


def owner_specs(keys):
    return [pl.BlockSpec((1, TILE), lambda i, *_: (0, i)), whole((1, keys))]


def self_block(plan, x, wqkv, wqkv_spec, wo, wo_spec, small, gain_row, owner, key_owner, name):
    number, width = x.shape
    specs, shapes = block_outs(number, width)
    return call(
        functools.partial(fwd_block_kernel, cross=False, gain_row=gain_row),
        (number // TILE,),
        [whole(x.shape), wqkv_spec, wo_spec, whole(small.shape)] + owner_specs(number),
        specs,
        shapes,
        attention_scratch(number, width) + [pltpu.VMEM((number, width), LOW)],
        8 * number * width * width + number * number * width * 2,
        16 * number * width,
        name,
    )(plan, x, wqkv, wo, small, owner, key_owner)


def cross_block(plan, normed, memory, dec_rows, wk_two, small, owner, key_owner):
    number, width = normed.shape
    specs, shapes = block_outs(number, width)
    half = (width // 32, 2, 16, width)
    return call(
        functools.partial(fwd_block_kernel, cross=True, gain_row=6),
        (number // TILE,),
        [
            rows_of(width),
            whole(memory.shape),
            at_block((width, width), 4, 0),
            at_block(half, 5, 0, 0, 0),
            at_block(half, 6, 0, 0, 0),
            at_block((width, width), 7, 0),
            whole(small.shape),
        ]
        + owner_specs(number),
        specs,
        shapes,
        attention_scratch(number, width),
        8 * number * width * width + number * number * width * 2,
        16 * number * width,
        "cross_block",
    )(plan, normed, memory, dec_rows, wk_two, wk_two, dec_rows, small, owner, key_owner)


def ffn_kernel(plan, normed, wup, wdown, small, hidden, slope, out, normed_out, inverse_out, *, mid_row, top_row):
    mid = normed[...] * small[mid_row : mid_row + 1, :] + small[mid_row + 1 : mid_row + 2, :]
    low = mid.astype(LOW)
    width = mid.shape[1]
    total = mid
    for j in range(hidden.shape[1] // width):
        cols = slice(j * width, j * width + width)
        inner = nn(low, block_of(wup, j))
        phi, tilt = phi_and_slope(inner)
        made = (inner * phi).astype(LOW)
        hidden[:, cols] = made
        slope[:, cols] = tilt.astype(LOW)
        total = total + nn(made, wdown[cols, :])
    result, normed_two, inverse = ln_forward(
        total, small[top_row : top_row + 1, :], small[top_row + 1 : top_row + 2, :]
    )
    out[...] = result.astype(LOW)
    normed_out[...] = normed_two
    inverse_out[...] = jnp.broadcast_to(inverse, inverse_out.shape)


def ffn_forward(plan, normed, wup, wup_spec, wdown, wdown_spec, small, mid_row, top_row, inner, name):
    number, width = normed.shape
    return call(
        functools.partial(ffn_kernel, mid_row=mid_row, top_row=top_row),
        (number // TILE,),
        [rows_of(width), wup_spec, wdown_spec, whole(small.shape)],
        [rows_of(inner), rows_of(inner), rows_of(width), rows_of(width), rows_of(LANES)],
        [
            shaped((number, inner), LOW),
            shaped((number, inner), LOW),
            shaped((number, width), LOW),
            shaped((number, width), F32),
            shaped((number, LANES), F32),
        ],
        [],
        4 * number * width * inner,
        20 * number * width,
        name,
    )(plan, normed, wup, wdown, small)


def ffn_back_kernel(plan, *refs, summed, mid_row, top_row):
    if summed:
        (cot, extra, normed_top, inverse_top, slope, normed_mid, inverse_mid, wup, wdown, wo, small,
         d_inner, d_down, d_sum, d_product, d_context, sums) = refs
    else:
        (cot, normed_top, inverse_top, slope, normed_mid, inverse_mid, wup, wdown, wo, small,
         d_inner, d_down, d_sum, d_product, d_context, sums) = refs
    i = pl.program_id(0)

    @pl.when(i == 0)
    def _():
        sums[...] = jnp.zeros_like(sums)

    upstream = cot[...].astype(F32)
    if summed:
        upstream = upstream + extra[...]
    width = upstream.shape[1]
    top = normed_top[...]
    sums[2:3, :] += jnp.sum(upstream * top, axis=0, keepdims=True)
    sums[3:4, :] += jnp.sum(upstream, axis=0, keepdims=True)
    d_top = ln_backward(upstream, top, inverse_top[:, 0:1], small[top_row : top_row + 1, :])
    low = d_top.astype(LOW)
    d_down[...] = low
    d_mid = d_top
    for j in range(slope.shape[1] // width):
        cols = slice(j * width, j * width + width)
        part = (nt(low, wdown[cols, :]) * slope[:, cols].astype(F32)).astype(LOW)
        d_inner[:, cols] = part
        d_mid = d_mid + nt(part, block_of(wup, j))
    normed = normed_mid[...]
    sums[0:1, :] += jnp.sum(d_mid * normed, axis=0, keepdims=True)
    sums[1:2, :] += jnp.sum(d_mid, axis=0, keepdims=True)
    total = ln_backward(d_mid, normed, inverse_mid[:, 0:1], small[mid_row : mid_row + 1, :])
    d_sum[...] = total
    place = lax.broadcasted_iota(jnp.int32, (TILE, 1), 0) + i * TILE
    live = (place < plan[2, 0]).astype(F32)
    product = (total * live).astype(LOW)
    d_product[...] = product
    d_context[...] = nt(product, wo[...]).astype(LOW)


def ffn_backward(plan, cots, top, slope, mid, weights, weight_specs, small, mid_row, top_row, name):
    number, width = mid[0].shape
    inner = slope.shape[1]
    return call(
        functools.partial(
            ffn_back_kernel, summed=len(cots) == 2, mid_row=mid_row, top_row=top_row
        ),
        (number // TILE,),
        [rows_of(width)] * len(cots)
        + [rows_of(width), rows_of(LANES), rows_of(inner), rows_of(width), rows_of(LANES)]
        + weight_specs
        + [whole(small.shape)],
        [
            rows_of(inner),
            rows_of(width),
            rows_of(width),
            rows_of(width),
            rows_of(width),
            whole((8, width)),
        ],
        [
            shaped((number, inner), LOW),
            shaped((number, width), LOW),
            shaped((number, width), F32),
            shaped((number, width), LOW),
            shaped((number, width), LOW),
            shaped((8, width), F32),
        ],
        [],
        4 * number * width * inner,
        26 * number * width,
        name,
    )(plan, *cots, *top, slope, *mid, *weights, small)


def ffn_weights_kernel(plan, normed, d_inner, d_down, hidden, context, d_product, small, up, down, wo, turn, *, mid_row):
    i = pl.program_id(0)

    @pl.when(i == 0)
    def _():
        mid = normed[...] * small[mid_row : mid_row + 1, :] + small[mid_row + 1 : mid_row + 2, :]
        turn[...] = mid.T.astype(LOW)
        wo[...] = nn(turned(context[...]), d_product[...]).astype(LOW)

    put_block(up, 0, nn(turn[...], d_inner[...]).astype(LOW))
    down[...] = nn(turned(hidden[...]), d_down[...]).astype(LOW)


def ffn_weights(plan, normed, d_inner, d_down, hidden, context, d_product, small, mid_row, name):
    number, width = normed.shape
    blocks = d_inner.shape[1] // width
    full = whole((number, width))
    column = pl.BlockSpec((number, width), lambda i, *_: (0, i))
    return call(
        functools.partial(ffn_weights_kernel, mid_row=mid_row),
        (blocks,),
        [full, column, full, column, full, full, whole(small.shape)],
        [
            pl.BlockSpec((width // 16, 1, 16, width), lambda i, *_: (0, i, 0, 0)),
            pl.BlockSpec((width, width), lambda i, *_: (i, 0)),
            whole((width, width)),
        ],
        [
            shaped((width // 16, blocks, 16, width), LOW),
            shaped((blocks * width, width), LOW),
            shaped((width, width), LOW),
        ],
        [pltpu.VMEM((width, number), LOW)],
        4 * number * width * width * blocks,
        24 * number * width,
        name,
    )(plan, normed, d_inner, d_down, hidden, context, d_product, small)


def attention_back_kernel(plan, q_ref, k_ref, v_ref, do_ref, lse, owner_q, owner_k, dq, dk, dv,
                          kt, key_owner, masked_q, masked_do, dqt, dk_sum, dv_sum, weights, d_weights, dots):
    i = pl.program_id(0)

    @pl.when(i == 0)
    def _():
        key_owner[...] = jnp.broadcast_to(owner_k[...], (8, owner_k.shape[1])).T
        kt[...] = turned(k_ref[...])
        dk_sum[...] = jnp.zeros_like(dk_sum)
        dv_sum[...] = jnp.zeros_like(dv_sum)

    query = q_ref[...] * jnp.asarray(HEAD**-0.5, LOW)
    upstream = do_ref[...]
    for h in range(HEADS):
        masked_q[h] = one_head(query[:, pair_columns(h)], h)
        masked_do[h] = one_head(upstream[:, pair_columns(h)], h)
    dqt[...] = jnp.zeros_like(dqt)
    dots[...] = jnp.zeros_like(dots)
    owner_row = owner_q[...]
    lo = plan[0, i]
    hi = plan[1, i]

    def weigh_tile(j, carry):
        rows = pl.ds(pl.multiple_of(j * TILE, TILE), TILE)
        bias = jnp.where(key_owner[rows, 0:1] == owner_row, 0.0, floor_value)
        sums = []
        for h in range(HEADS):
            s = nt(k_ref[rows, pair_columns(h)], masked_q[h])
            p = jnp.exp((s - lse[h : h + 1, :]) + bias)
            dp = nt(v_ref[rows, pair_columns(h)], masked_do[h])
            weights[j, h] = p
            d_weights[j, h] = dp
            sums.append(jnp.sum(p * dp, axis=0, keepdims=True))
        dots[...] += jnp.concatenate(sums, axis=0)
        return carry

    lax.fori_loop(lo, hi, weigh_tile, 0)

    def grad_tile(j, carry):
        rows = pl.ds(pl.multiple_of(j * TILE, TILE), TILE)
        for pair in range(HEADS // 2):
            cols = pair_columns(2 * pair)
            dv_part = dv_sum[rows, cols]
            dk_part = dk_sum[rows, cols]
            for h in (2 * pair, 2 * pair + 1):
                p = weights[j, h]
                ds = (p * (d_weights[j, h] - dots[h : h + 1, :])).astype(LOW)
                dv_part = dv_part + nn(p.astype(LOW), masked_do[h])
                dk_part = dk_part + nn(ds, masked_q[h])
                dqt[head_rows(h), :] += nn(kt[head_rows(h), rows], ds)
            dv_sum[rows, cols] = dv_part
            dk_sum[rows, cols] = dk_part
        return carry

    lax.fori_loop(lo, hi, grad_tile, 0)
    dq[...] = (dqt[...] * HEAD**-0.5).T.astype(LOW)

    @pl.when(i == pl.num_programs(0) - 1)
    def _():
        dk[...] = dk_sum[...].astype(LOW)
        dv[...] = dv_sum[...].astype(LOW)


def attention_backward(plan, q, kv, d_context, lse, owner, key_owner, name):
    number, width = q.shape
    keys = kv.shape[0]
    return call(
        attention_back_kernel,
        (number // TILE,),
        [
            rows_of(width),
            at_block((keys, width), 0, 0),
            at_block((keys, width), 0, 1),
            rows_of(width),
            pl.BlockSpec((HEADS, TILE), lambda i, *_: (0, i)),
        ]
        + owner_specs(keys),
        [rows_of(width), whole((keys, width)), whole((keys, width))],
        [shaped((number, width), LOW), shaped((keys, width), LOW), shaped((keys, width), LOW)],
        [
            pltpu.VMEM((width, keys), LOW),
            pltpu.VMEM((keys, 8), F32),
            pltpu.VMEM((HEADS, TILE, LANES), LOW),
            pltpu.VMEM((HEADS, TILE, LANES), LOW),
            pltpu.VMEM((width, TILE), F32),
            pltpu.VMEM((keys, width), F32),
            pltpu.VMEM((keys, width), F32),
            pltpu.VMEM((keys // TILE, HEADS, TILE, TILE), F32),
            pltpu.VMEM((keys // TILE, HEADS, TILE, TILE), F32),
            pltpu.VMEM((HEADS, TILE), F32),
        ],
        number * keys * width * 4,
        12 * number * width,
        name,
    )(plan, q, kv, kv, d_context, lse, owner, key_owner)


def cross_back_kernel(plan, d_query, dk, dv, normed, inverse, d_above, memory, context, wq, wk_a, wk_b, wo, small,
                      d_memory, d_sum, d_context, g_query, g_pair, g_out, sums, d_product):
    i = pl.program_id(0)
    mine = pl.ds(pl.multiple_of(i * TILE, TILE), TILE)

    @pl.when(i == 0)
    def _():
        sums[...] = jnp.zeros_like(sums)
        low = normed[...] * small[4:5, :] + small[5:6, :]
        g_query[...] = nn(low.T.astype(LOW), d_query[...]).astype(LOW)

    wk = jnp.concatenate([block_of(wk_a, 0), block_of(wk_b, 0)], axis=0)
    wv = jnp.concatenate([block_of(wk_a, 1), block_of(wk_b, 1)], axis=0)
    d_memory[...] = nt(dk[mine, :], wk) + nt(dv[mine, :], wv)
    d_one = d_above[...] + nt(d_query[mine, :], wq[...])
    hat = normed[mine, :]
    sums[0:1, :] += jnp.sum(d_one * hat, axis=0, keepdims=True)
    sums[1:2, :] += jnp.sum(d_one, axis=0, keepdims=True)
    total = ln_backward(d_one, hat, inverse[:, 0:1], small[4:5, :])
    d_sum[...] = total
    place = lax.broadcasted_iota(jnp.int32, (TILE, 1), 0) + i * TILE
    live = (place < plan[2, 0]).astype(F32)
    product = (total * live).astype(LOW)
    d_product[mine, :] = product
    d_context[...] = nt(product, wo[...]).astype(LOW)

    @pl.when(i == 1)
    def _():
        turn = turned(memory[...])
        put_block(g_pair, 0, nn(turn, dk[...]).astype(LOW))

    @pl.when(i == 2)
    def _():
        turn = turned(memory[...])
        put_block(g_pair, 1, nn(turn, dv[...]).astype(LOW))

    @pl.when(i == pl.num_programs(0) - 1)
    def _():
        g_out[...] = nn(turned(context[...]), d_product[...]).astype(LOW)


def cross_projections_back(plan, d_query, dk, dv, normed, inverse, d_above, memory, context, dec_rows, wk_two, small):
    number, width = normed.shape
    full = whole((number, width))
    square = whole((width, width))
    half = (width // 32, 2, 16, width)
    return call(
        cross_back_kernel,
        (number // TILE,),
        [full, full, full, full, rows_of(LANES), rows_of(width), full, full,
         at_block((width, width), 4, 0), at_block(half, 5, 0, 0, 0), at_block(half, 6, 0, 0, 0),
         at_block((width, width), 3, 0), whole(small.shape)],
        [rows_of(width), rows_of(width), rows_of(width), square, whole((width // 16, 2, 16, width)), square,
         whole((8, width))],
        [shaped((number, width), F32), shaped((number, width), F32), shaped((number, width), LOW),
         shaped((width, width), LOW), shaped((width // 16, 2, 16, width), LOW), shaped((width, width), LOW),
         shaped((8, width), F32)],
        [pltpu.VMEM((number, width), LOW)],
        16 * number * width * width,
        24 * number * width,
        "cross_projections_back",
    )(plan, d_query, dk, dv, normed, inverse, d_above, memory, context, dec_rows, wk_two, wk_two, dec_rows, small)


def self_back_kernel(plan, *refs, masked):
    if masked:
        dq, dk, dv, d_above, x, wqkv, flags, d_x, g_qkv, mask_sum, turn = refs
    else:
        dq, dk, dv, d_above, x, wqkv, d_x, g_qkv, turn = refs
    i = pl.program_id(0)
    mine = pl.ds(pl.multiple_of(i * TILE, TILE), TILE)

    @pl.when(i == 0)
    def _():
        turn[...] = turned(x[...])
        if masked:
            mask_sum[...] = jnp.zeros_like(mask_sum)

    pieces = jnp.concatenate([ref[mine, :] for ref in (dq, dk, dv)], axis=1)
    weights = jnp.concatenate([block_of(wqkv, j) for j in range(3)], axis=1)
    total = nt(pieces, weights)
    if masked:
        total = total + d_above[...]
    for j, ref in enumerate((dq, dk, dv)):

        @pl.when(i == j)
        def _(ref=ref):
            put_block(g_qkv, 0, nn(turn[...], ref[...]).astype(LOW))

    if masked:
        hit = column_of(flags[...]) == 1.0
        d_x[...] = jnp.where(hit, 0.0, total)
        mask_sum[0:1, :] += jnp.sum(jnp.where(hit, total, 0.0), axis=0, keepdims=True)
    else:
        d_x[...] = d_above[...]
        d_x[...] += total


def self_projections_back(plan, dq, dk, dv, d_above, x, wqkv, wqkv_spec, flags, units, name):
    number, width = x.shape
    full = whole((number, width))
    masked = flags is not None
    if units:
        g_shape = (width // 16, 3, 16, width)
        g_spec = pl.BlockSpec((width // 16, 1, 16, width), lambda i, *_: (0, jnp.minimum(i, 2), 0, 0))
    else:
        g_shape = (3, width, width)
        g_spec = pl.BlockSpec((1, width, width), lambda i, *_: (jnp.minimum(i, 2), 0, 0))
    in_specs = [full, full, full, rows_of(width), full, wqkv_spec]
    out_specs = [rows_of(width), g_spec]
    out_shape = [shaped((number, width), F32), shaped(g_shape, LOW)]
    operands = [dq, dk, dv, d_above, x, wqkv]
    if masked:
        in_specs.append(pl.BlockSpec((1, TILE), lambda i, *_: (0, i)))
        out_specs.append(whole((8, width)))
        out_shape.append(shaped((8, width), F32))
        operands.append(flags)
    return call(
        functools.partial(self_back_kernel, masked=masked),
        (number // TILE,),
        in_specs,
        out_specs,
        out_shape,
        [pltpu.VMEM((width, number), LOW)],
        12 * number * width * width,
        20 * number * width,
        name,
    )(plan, *operands)


def enc_regions(width, inner):
    return ((0, 3 * width, 3), (4 * width, 4 * width + inner, inner // width))


def dec_regions(width, inner):
    return ((5 * width, 7 * width, 2), (8 * width, 8 * width + inner, inner // width))


def to_units(rows, k):
    return rows.reshape(-1, 16, k, rows.shape[1]).transpose(0, 2, 1, 3).reshape(rows.shape)


def from_units(rows, k):
    return rows.reshape(-1, k, 16, rows.shape[1]).transpose(0, 2, 1, 3).reshape(rows.shape)


def fits(size, region):
    return size % (16 * region[2]) == 0


def arrange_own(rows, first, regions, arrange):
    place = first + lax.broadcasted_iota(jnp.int32, (rows.shape[0], 1), 0)
    result = rows
    for region in regions:
        if fits(rows.shape[0], region):
            inside = (place >= region[0]) & (place < region[1])
            result = jnp.where(inside, arrange(rows, region[2]), result)
    return result


def arrange_all(rows, size, regions, arrange):
    for region in regions:
        if not fits(size, region):
            part = arrange(rows[region[0] : region[1]], region[2])
            rows = jnp.concatenate([rows[: region[0]], part, rows[region[1] :]], axis=0)
    return rows


def owners_of(lengths, number):
    bounds = jnp.cumsum(lengths)
    places = jnp.arange(number, dtype=jnp.int32)
    owners = jnp.sum((places[:, None] >= bounds[None, :]).astype(jnp.int32), axis=1)
    filled = places < bounds[-1]
    for_queries = jnp.where(filled, owners, -2).astype(F32)[None, :]
    for_keys = jnp.where(filled, owners, -1).astype(F32)[None, :]
    return for_queries, for_keys, bounds


def plan_of(query_bounds, key_bounds, key_lengths, number):
    firsts = jnp.arange(8, dtype=jnp.int32) * TILE
    filled = query_bounds[-1]
    lasts = jnp.minimum(firsts + TILE, filled) - 1

    def pair_of(places):
        found = jnp.sum((places[:, None] >= query_bounds[None, :]).astype(jnp.int32), axis=1)
        return jnp.minimum(found, key_lengths.shape[0] - 1)

    def pick(values, pairs):
        chosen = pairs[:, None] == jnp.arange(values.shape[0])[None, :]
        return jnp.sum(jnp.where(chosen, values[None, :], 0), axis=1)

    begin = pick(key_bounds - key_lengths, pair_of(firsts))
    end = pick(key_bounds, pair_of(lasts))
    some = firsts < filled
    lo = jnp.where(some, begin // TILE, 0)
    hi = jnp.where(some, (end + TILE - 1) // TILE, 0)
    return jnp.stack([lo, hi, jnp.full_like(lo, filled)]).astype(jnp.int32)


def moments(gradient, first, second):
    first_new = beta_one * first + (1.0 - beta_one) * gradient
    second_new = beta_two * second + (1.0 - beta_two) * gradient * gradient
    return (first_new, second_new)


def adamw(weight, gradient, first, second):
    first_new, second_new = moments(gradient, first, second)
    moved = weight - rate * (
        first_new
        / (1.0 - beta_one**STEPS)
        / (jnp.sqrt(second_new / (1.0 - beta_two**STEPS)) + epsilon)
        + decay * weight
    )
    return (moved, first_new, second_new)


def on_device(
    devices,
    src_in,
    tgt_in,
    src_len,
    tgt_len,
    tgt_mask,
    enc_cot,
    dec_cot,
    enc_master,
    enc_first,
    enc_second,
    dec_master,
    dec_first,
    dec_second,
    small_master,
    small_first,
    small_second,
):
    width = src_in.shape[1]
    number = src_in.shape[0]
    me = lax.axis_index("fsdp")
    enc_size, dec_size = enc_master.shape[0], dec_master.shape[0]
    enc_count, dec_count = enc_size * devices, dec_size * devices
    inner = (enc_count - 4 * width) // 2
    ups = inner // width
    enc_map, dec_map = enc_regions(width, inner), dec_regions(width, inner)

    enc_own = arrange_own(enc_master.astype(LOW), me * enc_size, enc_map, to_units)
    dec_own = arrange_own(dec_master.astype(LOW), me * dec_size, dec_map, to_units)
    enc_rows = lax.all_gather(enc_own, "fsdp", axis=0, tiled=True)
    dec_rows = lax.all_gather(dec_own, "fsdp", axis=0, tiled=True)
    small_rows = lax.all_gather(small_master.astype(LOW), "fsdp", axis=1, tiled=True)

    src_owner, src_key, src_bounds = owners_of(src_len[0], number)
    tgt_owner, tgt_key, tgt_bounds = owners_of(tgt_len[0], number)
    enc_plan = plan_of(src_bounds, src_bounds, src_len[0], number)
    dec_plan = plan_of(tgt_bounds, tgt_bounds, tgt_len[0], number)
    cross_plan = plan_of(tgt_bounds, src_bounds, src_len[0], number)

    smalls = jnp.pad(small_rows.astype(F32), ((0, 5), (0, 0)))
    masked = tgt_mask[:, None] == 1
    start = jnp.where(masked, small_rows[10][None, :], tgt_in)
    flags = tgt_mask.astype(F32)[None, :]

    enc_rows = arrange_all(enc_rows, enc_size, enc_map, to_units)
    dec_rows = arrange_all(dec_rows, dec_size, dec_map, to_units)
    enc_three = enc_rows.reshape(-1, 3, 16, width)
    enc_four = enc_rows.reshape(-1, ups, 16, width)
    dec_two = dec_rows.reshape(-1, 2, 16, width)
    dec_four = dec_rows.reshape(-1, ups, 16, width)
    dec_three = dec_rows[: 3 * width].reshape(width, 3, width).transpose(1, 0, 2)
    units = width // 16
    three_spec = at_block((units, 3, 16, width), 0, 0, 0, 0)
    enc_up = at_block((units, ups, 16, width), 1, 0, 0, 0)
    enc_down = at_block((inner, width), 2, 0)
    enc_wo = at_block((width, width), 3, 0)
    dec_up = at_block((units, ups, 16, width), 2, 0, 0, 0)
    dec_down = at_block((inner, width), 3, 0)

    e_q, e_kv, e_ctx, e_lse, e_hat, e_inv = self_block(
        enc_plan, src_in, enc_three, three_spec, enc_rows, enc_wo, smalls, 0, src_owner, src_key, "enc_block"
    )
    e_hidden, e_slope, memory, t_hat, t_inv = ffn_forward(
        enc_plan, e_hat, enc_four, enc_up, enc_rows, enc_down, smalls, 0, 2, inner, "enc_ffn"
    )
    s_q, s_kv, s_ctx, s_lse, s_hat, s_inv = self_block(
        dec_plan, start, dec_three, whole(dec_three.shape), dec_rows, at_block((width, width), 3, 0), smalls, 4,
        tgt_owner, tgt_key, "dec_block",
    )
    c_q, c_kv, c_ctx, c_lse, c_hat, c_inv = cross_block(
        cross_plan, s_hat, memory, dec_rows, dec_two, smalls, tgt_owner, src_key
    )
    d_hidden, d_slope, decoded, f_hat, f_inv = ffn_forward(
        dec_plan, c_hat, dec_four, dec_up, dec_rows, dec_down, smalls, 6, 8, inner, "dec_ffn"
    )

    dd_inner, dd_down, d_two, d_cross, d_cctx, sums_d = ffn_backward(
        dec_plan, [dec_cot], (f_hat, f_inv), d_slope, (c_hat, c_inv), (dec_four, dec_rows, dec_rows),
        [dec_up, dec_down, at_block((width, width), 7, 0)], smalls, 6, 8, "dec_ffn_back",
    )
    g_dup, g_ddown, g_cout = ffn_weights(
        dec_plan, c_hat, dd_inner, dd_down, d_hidden, c_ctx, d_cross, smalls, 6, "dec_ffn_weights"
    )
    dcq, dck, dcv = attention_backward(cross_plan, c_q, c_kv, d_cctx, c_lse, tgt_owner, src_key, "cross_back")
    d_memory, d_one, d_sctx, g_cq, g_ckv, g_sout, sums_c = cross_projections_back(
        dec_plan, dcq, dck, dcv, s_hat, s_inv, d_two, memory, s_ctx, dec_rows, dec_two, smalls
    )
    dsq, dsk, dsv = attention_backward(dec_plan, s_q, s_kv, d_sctx, s_lse, tgt_owner, tgt_key, "dec_back")
    tgt_grad, g_sqkv, mask_sum = self_projections_back(
        dec_plan, dsq, dsk, dsv, d_one, start, dec_three, whole(dec_three.shape), flags, False, "dec_proj_back"
    )
    de_inner, de_down, d_mid, d_eattn, d_ectx, sums_e = ffn_backward(
        enc_plan, [enc_cot, d_memory], (t_hat, t_inv), e_slope, (e_hat, e_inv), (enc_four, enc_rows, enc_rows),
        [enc_up, enc_down, enc_wo], smalls, 0, 2, "enc_ffn_back",
    )
    g_up, g_down, g_out = ffn_weights(
        enc_plan, e_hat, de_inner, de_down, e_hidden, e_ctx, d_eattn, smalls, 0, "enc_ffn_weights"
    )
    deq, dek, dev = attention_backward(enc_plan, e_q, e_kv, d_ectx, e_lse, src_owner, src_key, "enc_back")
    src_grad, g_qkv = self_projections_back(
        enc_plan, deq, dek, dev, d_mid, src_in, enc_three, three_spec, None, True, "enc_proj_back"
    )

    dec_grad = jnp.concatenate(
        [
            g_sqkv.transpose(1, 0, 2).reshape(-1, width),
            g_sout,
            g_cq,
            g_ckv.reshape(-1, width),
            g_cout,
            g_dup.reshape(-1, width),
            g_ddown,
        ],
        axis=0,
    )
    enc_grad = jnp.concatenate(
        [g_qkv.reshape(-1, width), g_out, g_up.reshape(-1, width), g_down], axis=0
    )
    small_grad = jnp.concatenate([sums_e[:4], sums_c[:2], sums_d[:4], mask_sum[:1]], axis=0)
    dec_grad = arrange_all(dec_grad, dec_size, dec_map, from_units)
    enc_grad = arrange_all(enc_grad, enc_size, enc_map, from_units)
    share = small_master.shape[1]
    small_wire = small_grad.reshape(-1, devices, share).transpose(1, 0, 2).reshape(devices, -1).astype(LOW)
    held = small_wire.shape[1]
    small_wire = jnp.pad(small_wire, ((0, 0), (0, 16 * width - held))).reshape(devices, 16, width)
    enc_wire = jnp.concatenate([enc_grad.reshape(devices, enc_size, width), small_wire], axis=1)
    dec_summed = lax.psum_scatter(dec_grad, "fsdp", scatter_dimension=0, tiled=True)
    enc_summed = lax.psum_scatter(enc_wire.reshape(-1, width), "fsdp", scatter_dimension=0, tiled=True)
    small_summed = enc_summed[enc_size:].reshape(-1)[:held].reshape(-1, share).astype(F32)
    enc_summed = arrange_own(enc_summed[:enc_size].astype(F32), me * enc_size, enc_map, from_units)
    dec_summed = arrange_own(dec_summed.astype(F32), me * dec_size, dec_map, from_units)

    part = 1.0 / devices
    enc_summed = enc_summed * part
    dec_summed = dec_summed * part
    small_summed = small_summed * part
    enc_new, enc_first_new, encoder_second_moment_updated = adamw(
        enc_master, enc_summed, enc_first, enc_second
    )
    dec_new, dec_first_new, dec_second_new = adamw(dec_master, dec_summed, dec_first, dec_second)
    small_first_new, small_second_new = moments(small_summed, small_first, small_second)
    return (
        memory,
        decoded,
        src_grad,
        tgt_grad,
        enc_new,
        enc_first_new,
        encoder_second_moment_updated,
        enc_new.astype(LOW),
        dec_new,
        dec_first_new,
        dec_second_new,
        dec_new.astype(LOW),
        small_summed,
        small_first_new,
        small_second_new,
    )


def solution(mesh):
    rows = P("fsdp", None)
    columns = P(None, "fsdp")
    return jax.shard_map(
        functools.partial(on_device, mesh.shape["fsdp"]),
        mesh=mesh,
        in_specs=(rows,) * 4 + (P("fsdp"),) + (rows,) * 8 + (columns,) * 3,
        out_specs=(rows,) * 12 + (columns,) * 3,
        check_vma=False,
    )
```

time: 1060 us -> 697 us (0.66)
  matrix products: 406 us -> 0 us
  Pallas kernels: 0 us -> 237 us
  local copies, waits for them, and re-layouts: 170 us -> 39 us
  other arithmetic: 118 us -> 35.6 us
  waiting for transfers between devices: 291 us -> 316 us
    dot_general x75 -> x0, matrix products: 406 us -> none  [the longest x11 71.8 us: product(): return jnp.dot(former, latter, preferred_element_type=jnp.float32)]
    pallas_call x0 -> x15, Pallas kernels: none -> 237 us  [the longest x3 62.3 us: attention_backward(): call(attention_back_kernel, (number // TILE,), [rows_of(width), at_block(...]
    convert_element_type x13 -> x9, other arithmetic: 66.6 us -> 12.7 us  [the longest x1 2.93 us: on_device(): dec_new.astype(LOW)]
    all_gather x2, waiting for transfers between devices: 10.3 us -> 57.5 us  [the longest x1 44.2 us: on_device(): dec_rows = lax.all_gather(dec_own, 'fsdp', axis=0, tiled=True)]
    unnamed x363 -> x49, local copies, waits for them, and re-layouts: 56 us -> 13 us
    reduce_scatter x1, waiting for transfers between devices: 182 us -> 142 us  [on_device(): lax.psum_scatter(dec_grad, 'fsdp', scatter_dimension=0, tiled=True)]
    reshape x17, local copies, waits for them, and re-layouts: 43.1 us -> 12 us  [the longest x2 5.53 us: on_device(): dec_three = dec_rows[:3 * width].reshape(width, 3, width).transpose(1, 0, 2)]
    reduce_sum x13 -> x6, other arithmetic: 29.6 us -> 1 us  [the longest x3 0.65 us: pick(): return jnp.sum(jnp.where(chosen, values[None, :], 0), axis=1)]
  transfers between devices with their start and end apart: 5 -> 4, of which waited for: 3 -> 4; matrix products, arithmetic and copies ran while one was open for 27% -> 6% of each run, Pallas kernels for 0% -> 7%
where the time goes in v1:
time: 697 us; the launch traced here: 687 us
  waiting for transfers between devices  316 us (45%)
  Pallas kernels  237 us (34%)
  blocking collectives  43.8 us (6%)
  local copies, waits for them, and re-layouts  39 us (6%)
  other arithmetic  35.6 us (5%)
  between operations  14.6 us (2%)
    reduce_scatter x1, waiting for transfers between devices, on_device(): lax.psum_scatter(dec_grad, 'fsdp', scatter_dimension=0, tiled=True)  142 us
    reduce_scatter x1, waiting for transfers between devices, on_device(): lax.psum_scatter(enc_wire.reshape(-1, width), 'fsdp', scatter_dimension=0...  117 us
    pallas_call x3, Pallas kernels, attention_backward(): call(attention_back_kernel, (number // TILE,), [rows_of(width), at_block(...  62.3 us
    all_gather x1, waiting for transfers between devices, on_device(): dec_rows = lax.all_gather(dec_own, 'fsdp', axis=0, tiled=True)  44.2 us
    all_gather x1, blocking collectives, on_device(): lax.all_gather(small_master.astype(LOW), 'fsdp', axis=1, tiled=True)  43.8 us
    pallas_call x2, Pallas kernels, self_block(): call(functools.partial(fwd_block_kernel, cross=False, gain_row=gain_row),...  36.9 us
    pallas_call x2, Pallas kernels, ffn_forward(): call(functools.partial(ffn_kernel, mid_row=mid_row, top_row=top_row), (nu...  33.6 us
    pallas_call x2, Pallas kernels, ffn_backward(): call(functools.partial(ffn_back_kernel, summed=len(cots) == 2, mid_row=mi...  28.7 us
  transfers between devices with their start and end apart: 4, of which 4 were waited for; matrix products, arithmetic and copies ran while one was open for 6% of the time, Pallas kernels for 7%

profile of v1, /device:TPU:0, one launch (start us, length us, event | category | flops | bytes accessed | tf_op | source)
XLA Modules:
  0.0 686.6 jit_solution(12302464324836484378)
XLA Ops:
  7.3 1.1 convert_element_type.104
  8.7 1.8 fusion.1
  10.6 1.1 convert_element_type.111
  12.1 0.8 fusion
  13.9 0.5 slice.57
  14.6 43.8 %all_gather.10 = bf16[11,512]{0,1:T(8,128)(2,1)S(1)} all-gather(bf16[11,16]{0,1:T(8,128)(2,1)S(1)} %copy.92), channel_id=1, replica_groups=mesh['fsdp'=32] {'fsdp'}, dimensions={1}, use_global_device_ids=true | all-gather | bytes 11616 | tf_op jit(solution)/shard_map/all_gather | solution.py:827
  58.5 0.6 convert_element_type.115
  59.1 0.7 minimum_add_fusion
  59.8 0.7 minimum_add_fusion.1
  61.3 0.7 compare_select_fusion.22
  62.0 0.6 lt.118
  62.7 0.6 pad_add_fusion.2.plan
  63.3 0.7 fusion.11
  63.9 0.7 fusion.13
  64.6 0.6 lt.125
  65.2 0.6 pad_add_fusion
  65.9 0.6 pad_convert_fusion.refs_3_.small.refs_6_.refs_9_.refs_10_
  66.9 1.3 fusion.6
  68.1 1.2 fusion.8
  69.4 1.2 broadcast_select_fusion.refs_0_.refs_4_
  70.6 13.3 %all-gather.3.cloned.1.call-done.refs_2_.wdown.refs_8_.refs_9_ = bf16[6144,512]{1,0:T(8,128)(2,1)} async-done(((bf16[192,512]{1,0:T(8,128)(2,1)}), bf16[6144,512]{1,0:T(8,128)(2,1)}) %all-gather.3.cloned.1.call-update) | async-done | bytes 6291472 | tf_op jit(solution)/shard_map/all_gather | solution.py:825
  83.9 18.4 %enc_block.1 = (bf16[1024,512]{1,0:T(8,128)(2,1)}, bf16[1024,1024]{1,0:T(8,128)(2,1)}, bf16[1024,512]{1,0:T(8,128)(2,1)}, f32[8,1024]{1,0:T(8,128)}, f32[1024,512]{1,0:T(8,128)}, /*index=5*/f32[1024,128]{1,0:T(8,128)}) custom-call(s32[3,8]{1,0:T(4,128)} %pad_add_fusion.2.plan, bf16[1024,512]{1,0:T(8,128)(2,1)} %refs_4_.1, ...), custom_call_target="tpu_custom_call" | custom-call | flops 3221225472 | bytes 8388608 | tf_op jit(solution)/shard_map/enc_block/pallas_call | solution.py:286
  102.4 16.8 %enc_ffn.1 = (bf16[1024,2048]{1,0:T(8,128)(2,1)}, bf16[1024,2048]{1,0:T(8,128)(2,1)}, bf16[1024,512]{1,0:T(8,128)(2,1)}, f32[1024,512]{1,0:T(8,128)}, f32[1024,128]{1,0:T(8,128)}) custom-call(s32[3,8]{1,0:T(4,128)} %pad_add_fusion.2.plan, f32[1024,512]{1,0:T(8,128)} %get-tuple-element.82.normed.refs_5_, bf16[96,4,16,512]{3,2,1,0:T(8,128)(2,1)} %bitcast.135, ...), custom_call_target="tpu_custom_call" | custom-call | flops 4294967296 | bytes 10485760 | tf_op jit(solution)/shard_map/enc_ffn/pallas_call | solution.py:348
  119.2 44.2 %all-gather.5.cloned.1.call-done.refs_2_.refs_5_.wdown.refs_7_.refs_8_.wq.wo = bf16[8192,512]{1,0:T(8,128)(2,1)} async-done(((bf16[256,512]{1,0:T(8,128)(2,1)}), bf16[8192,512]{1,0:T(8,128)(2,1)}) %all-gather.5.cloned.1.call-update) | async-done | bytes 8388624 | tf_op jit(solution)/shard_map/all_gather | solution.py:826
  163.4 2.7 slice.60
  166.0 4.0 reshape.627
  170.0 1.5 copy.110
  171.6 18.4 %dec_block.1 = (bf16[1024,512]{1,0:T(8,128)(2,1)}, bf16[1024,1024]{1,0:T(8,128)(2,1)}, bf16[1024,512]{1,0:T(8,128)(2,1)}, f32[8,1024]{1,0:T(8,128)}, f32[1024,512]{1,0:T(8,128)}, /*index=5*/f32[1024,128]{1,0:T(8,128)}) custom-call(s32[3,8]{1,0:T(4,128)} %get-tuple-element.173.plan, bf16[1024,512]{1,0:T(8,128)(2,1)} %broadcast_select_fusion.refs_0_.refs_4_, ...), custom_call_target="tpu_custom_call" | custom-call | flops 3221225472 | bytes 8388608 | tf_op jit(solution)/shard_map/dec_block/pallas_call | solution.py:286
  190.0 17.1 %cross_block.1 = (bf16[1024,512]{1,0:T(8,128)(2,1)}, bf16[1024,1024]{1,0:T(8,128)(2,1)}, bf16[1024,512]{1,0:T(8,128)(2,1)}, f32[8,1024]{1,0:T(8,128)}, f32[1024,512]{1,0:T(8,128)}, /*index=5*/f32[1024,128]{1,0:T(8,128)}) custom-call(s32[3,8]{1,0:T(4,128)} %get-tuple-element.172.plan, f32[1024,512]{1,0:T(8,128)} %get-tuple-element.84.refs_0_.normed, ...), custom_call_target="tpu_custom_call" | custom-call | flops 3221225472 | bytes 8388608 | tf_op jit(solution)/shard_map/cross_block/pallas_call | solution.py:303
  207.1 16.8 %dec_ffn.1 = (bf16[1024,2048]{1,0:T(8,128)(2,1)}, bf16[1024,2048]{1,0:T(8,128)(2,1)}, bf16[1024,512]{1,0:T(8,128)(2,1)}, f32[1024,512]{1,0:T(8,128)}, f32[1024,128]{1,0:T(8,128)}) custom-call(s32[3,8]{1,0:T(4,128)} %get-tuple-element.173.plan, f32[1024,512]{1,0:T(8,128)} %get-tuple-element.85.normed.refs_4_, bf16[128,4,16,512]{3,2,1,0:T(8,128)(2,1)} %bitcast.130, ...), custom_call_target="tpu_custom_call" | custom-call | flops 4294967296 | bytes 10485760 | tf_op jit(solution)/shard_map/dec_ffn/pallas_call | solution.py:348
  223.9 14.4 %dec_ffn_back.1 = (bf16[1024,2048]{1,0:T(8,128)(2,1)}, bf16[1024,512]{1,0:T(8,128)(2,1)}, f32[1024,512]{1,0:T(8,128)}, bf16[1024,512]{1,0:T(8,128)(2,1)}, bf16[1024,512]{1,0:T(8,128)(2,1)}, /*index=5*/f32[8,512]{1,0:T(8,128)}) custom-call(s32[3,8]{1,0:T(4,128)} %get-tuple-element.173.plan, bf16[1024,512]{1,0:T(8,128)(2,1)} %refs_0_.4, ...), custom_call_target="tpu_custom_call" | custom-call | flops 4294967296 | bytes 13631488 | tf_op jit(solution)/shard_map/dec_ffn_back/pallas_call | solution.py:411
  238.3 18.6 %cross_back.1 = (bf16[1024,512]{1,0:T(8,128)(2,1)}, bf16[1024,512]{1,0:T(8,128)(2,1)}, bf16[1024,512]{1,0:T(8,128)(2,1)}) custom-call(s32[3,8]{1,0:T(4,128)} %get-tuple-element.172.plan, bf16[1024,512]{1,0:T(8,128)(2,1)} %get-tuple-element.89.q_ref, bf16[1024,1024]{1,0:T(8,128)(2,1)} %get-tuple-element.90.k_ref.v_ref, ...), custom_call_target="tpu_custom_call" | custom-call | flops 2147483648 | bytes 6291456 | tf_op jit(solution)/shard_map/cross_back/pallas_call | solution.py:548
  256.9 14.1 %cross_projections_back.1 = (f32[1024,512]{1,0:T(8,128)}, f32[1024,512]{1,0:T(8,128)}, bf16[1024,512]{1,0:T(8,128)(2,1)}, bf16[512,512]{1,0:T(8,128)(2,1)}, bf16...) custom-call(s32[3,8]{1,0:T(4,128)} %get-tuple-element.173.plan, ...), custom_call_target="tpu_custom_call" | custom-call | flops 4294967296 | bytes 12582912 | tf_op jit(solution)/shard_map/cross_projections_back/pallas_call | solution.py:625
  271.0 21.8 %dec_back.1 = (bf16[1024,512]{1,0:T(8,128)(2,1)}, bf16[1024,512]{1,0:T(8,128)(2,1)}, bf16[1024,512]{1,0:T(8,128)(2,1)}) custom-call(s32[3,8]{1,0:T(4,128)} %get-tuple-element.173.plan, bf16[1024,512]{1,0:T(8,128)(2,1)} %get-tuple-element.115.q_ref, bf16[1024,1024]{1,0:T(8,128)(2,1)} %get-tuple-element.116.k_ref.v_ref, ...), custom_call_target="tpu_custom_call" | custom-call | flops 2147483648 | bytes 6291456 | tf_op jit(solution)/shard_map/dec_back/pallas_call | solution.py:548
  292.8 10.5 %dec_proj_back.1 = (f32[1024,512]{1,0:T(8,128)}, bf16[3,512,512]{2,1,0:T(8,128)(2,1)}, f32[8,512]{1,0:T(8,128)}) custom-call(s32[3,8]{1,0:T(4,128)} %get-tuple-element.173.plan, bf16[1024,512]{1,0:T(8,128)(2,1)} %get-tuple-element.119.refs_0_, bf16[1024,512]{1,0:T(8,128)(2,1)} %get-tuple-element.120.refs_1_, bf16[1024,512]{1,0:T(8,128)(2,1)} %get-tuple-element.121.refs_2_, ...), custom_call_target="tpu_custom_call" | custom-call | flops 3221225472 | bytes 10485760 | tf_op jit(solution)/shard_map/dec_proj_back/pallas_call | solution.py:696
  303.3 0.7 slice.86
  304.0 14.4 %enc_ffn_back.1 = (bf16[1024,2048]{1,0:T(8,128)(2,1)}, bf16[1024,512]{1,0:T(8,128)(2,1)}, f32[1024,512]{1,0:T(8,128)}, bf16[1024,512]{1,0:T(8,128)(2,1)}, bf16[1024,512]{1,0:T(8,128)(2,1)}, /*index=5*/f32[8,512]{1,0:T(8,128)}) custom-call(s32[3,8]{1,0:T(4,128)} %pad_add_fusion.2.plan, bf16[1024,512]{1,0:T(8,128)(2,1)} %refs_0_.5, ...), custom_call_target="tpu_custom_call" | custom-call | flops 4294967296 | bytes 13631488 | tf_op jit(solution)/shard_map/enc_ffn_back/pallas_call | solution.py:411
  318.4 0.7 slice.84
  319.1 0.7 slice.85
  319.8 0.7 slice.83
  321.1 1.1 copy.99
  322.2 21.9 %enc_back.1 = (bf16[1024,512]{1,0:T(8,128)(2,1)}, bf16[1024,512]{1,0:T(8,128)(2,1)}, bf16[1024,512]{1,0:T(8,128)(2,1)}) custom-call(s32[3,8]{1,0:T(4,128)} %pad_add_fusion.2.plan, bf16[1024,512]{1,0:T(8,128)(2,1)} %get-tuple-element.87.q_ref, bf16[1024,1024]{1,0:T(8,128)(2,1)} %get-tuple-element.88.k_ref.v_ref, ...), custom_call_target="tpu_custom_call" | custom-call | flops 2147483648 | bytes 6291456 | tf_op jit(solution)/shard_map/enc_back/pallas_call | solution.py:548
  344.1 9.8 %enc_proj_back.1 = (f32[1024,512]{1,0:T(8,128)}, bf16[32,3,16,512]{3,2,1,0:T(8,128)(2,1)}) custom-call(s32[3,8]{1,0:T(4,128)} %pad_add_fusion.2.plan, bf16[1024,512]{1,0:T(8,128)(2,1)} %get-tuple-element.110.refs_0_, bf16[1024,512]{1,0:T(8,128)(2,1)} %get-tuple-element.111.refs_1_, bf16[1024,512]{1,0:T(8,128)(2,1)} %get-tuple-element.112.refs_2_, ...), custom_call_target="tpu_custom_call" | custom-call | flops 3221225472 | bytes 10485760 | tf_op jit(solution)/shard_map/enc_proj_back/pallas_call | solution.py:696
  353.9 12.1 %enc_ffn_weights.1 = (bf16[32,4,16,512]{3,2,1,0:T(8,128)(2,1)}, bf16[2048,512]{1,0:T(8,128)(2,1)}, bf16[512,512]{1,0:T(8,128)(2,1)}) custom-call(s32[3,8]{1,0:T(4,128)} %pad_add_fusion.2.plan, f32[1024,512]{1,0:T(8,128)} %get-tuple-element.82.normed.refs_5_, bf16[1024,2048]{1,0:T(8,128)(2,1)} %get-tuple-element.125.d_inner, ...), custom_call_target="tpu_custom_call" | custom-call | flops 4294967296 | bytes 12582912 | tf_op jit(solution)/shard_map/enc_ffn_weights/pallas_call | solution.py:461
  366.0 5.7 pad_maximum_fusion.1
  371.7 6.2 pad_maximum_fusion
  378.0 2.8 copy.102
  380.8 2.8 reshape.639
  383.5 2.7 constant_dynamic-update-slice_fusion.6
  386.2 1.9 constant_dynamic-update-slice_fusion.5
  388.1 0.8 constant_dynamic-update-slice_fusion.4
  388.9 2.3 constant_dynamic-update-slice_fusion.3
  391.2 11.9 %dec_ffn_weights.1 = (bf16[32,4,16,512]{3,2,1,0:T(8,128)(2,1)}, bf16[2048,512]{1,0:T(8,128)(2,1)}, bf16[512,512]{1,0:T(8,128)(2,1)}) custom-call(s32[3,8]{1,0:T(4,128)} %get-tuple-element.173.plan, f32[1024,512]{1,0:T(8,128)} %get-tuple-element.85.normed.refs_4_, bf16[1024,2048]{1,0:T(8,128)(2,1)} %get-tuple-element.141.d_inner, ...), custom_call_target="tpu_custom_call" | custom-call | flops 4294967296 | bytes 12582912 | tf_op jit(solution)/shard_map/dec_ffn_weights/pallas_call | solution.py:461
  403.1 2.0 constant_dynamic-update-slice_fusion.2
  405.2 3.1 constant_dynamic-update-slice_fusion.1
  408.3 1.4 constant_dynamic-update-slice_fusion
  409.8 117.3 %reduce-scatter.3.cloned.1.call-done = bf16[208,512]{1,0:T(8,128)(2,1)} async-done(((bf16[6656,512]{1,0:T(8,128)(2,1)}), bf16[208,512]{1,0:T(8,128)(2,1)}) %reduce-scatter.3.cloned.1.call-update) | async-done | bytes 213008 | tf_op jit(solution)/shard_map/reduce_scatter | solution.py:923
  527.0 1.0 slice_convert_fusion
  528.9 0.7 slice.66
  529.8 0.6 fusion.4
  530.4 2.4 fusion.17
  532.9 141.7 %reduce-scatter.5.cloned.1.call-done = bf16[256,512]{1,0:T(8,128)(2,1)} async-done(((bf16[8192,512]{1,0:T(8,128)(2,1)}), bf16[256,512]{1,0:T(8,128)(2,1)}) %reduce-scatter.5.cloned.1.call-update) | async-done | bytes 262160 | tf_op jit(solution)/shard_map/reduce_scatter | solution.py:922
  674.5 1.0 convert_element_type.121
  676.9 2.9 fusion.16
  (97 shorter events, 6.1 us)
Async XLA Ops:
  7.2 4.9 copy-start
  7.2 5.8 copy-start.20
  7.2 6.5 copy-start.19
  7.2 7.3 %copy-start.10 = (f32[11,16]{1,0:T(8,128)S(1)}, f32[11,16]{1,0:T(8,128)}, u32[]{:S(2)}) copy-start(f32[11,16]{1,0:T(8,128)} %param.29) | copy-start | bytes 2116
  7.2 51.3 %copy-start.9 = (s32[1024]{0:T(1024)S(1)}, s32[1024]{0:T(1024)}, u32[]{:S(2)}) copy-start(s32[1024]{0:T(1024)} %param.20) | copy-start | bytes 12292
  7.2 62.2 %copy-start.4 = (bf16[1024,512]{1,0:T(8,128)(2,1)S(1)}, bf16[1024,512]{1,0:T(8,128)(2,1)}, u32[]{:S(2)}) copy-start(bf16[1024,512]{1,0:T(8,128)(2,1)} %param.17) | copy-start | bytes 3145732
  7.2 76.7 %all-gather.3.cloned.1.call-start = ((), (), s32[]{:S(2)}) async-start(), calls=%async_computation.2 | async-start | bytes 6488064 | tf_op jit(solution)/shard_map/all_gather | solution.py:825
  8.6 3.3 copy-start.13
  8.6 3.3 copy-start.14
  10.6 152.8 %all-gather.5.cloned.1.call-start = ((), (), s32[]{:S(2)}) async-start(), calls=%async_computation.3 | async-start | bytes 8650752 | tf_op jit(solution)/shard_map/all_gather | solution.py:826
  12.0 90.3 %copy-start.15 = (pred[256]{0:T(512)(128)(4,1)}, pred[256]{0:T(512)(128)(4,1)S(1)}, u32[]{:S(2)}) copy-start(pred[256]{0:T(512)(128)(4,1)S(1)} %get-tuple-element.182) | copy-start | bytes 772
  12.0 90.3 %copy-start.17 = (pred[256]{0:T(512)(128)(4,1)}, pred[256]{0:T(512)(128)(4,1)S(1)}, u32[]{:S(2)}) copy-start(pred[256]{0:T(512)(128)(4,1)S(1)} %get-tuple-element.183) | copy-start | bytes 772
  12.9 514.1 %reduce-scatter.3.cloned.1.call-start = ((), (), s32[]{:S(2)}) async-start(), calls=%async_computation.4 | async-start | bytes 7028736 | tf_op jit(solution)/shard_map/reduce_scatter | solution.py:923
  353.9 12.1 %copy-start.3 = (bf16[32,3,16,512]{3,2,1,0:T(8,128)(2,1)S(1)}, bf16[32,3,16,512]{3,2,1,0:T(8,128)(2,1)}, u32[]{:S(2)}) copy-start(bf16[32,3,16,512]{3,2,1,0:T(8,128)(2,1)} %get-tuple-element.124) | copy-start | bytes 4718596
  377.9 10.2 %copy-start.6 = (bf16[512,512]{1,0:T(8,128)(2,1)S(1)}, bf16[512,512]{1,0:T(8,128)(2,1)}, u32[]{:S(2)}) copy-start(bf16[512,512]{1,0:T(8,128)(2,1)} %get-tuple-element.139) | copy-start | bytes 1572868
  377.9 296.6 %reduce-scatter.5.cloned.1.call-start = ((), (), s32[]{:S(2)}) async-start(), calls=%async_computation.5 | async-start | bytes 8650752 | tf_op jit(solution)/shard_map/reduce_scatter | solution.py:922
  403.1 5.1 copy-start.2
  409.7 120.1 %copy-start.11 = (f32[11,16]{1,0:T(8,128)S(1)}, f32[11,16]{1,0:T(8,128)}, u32[]{:S(2)}) copy-start(f32[11,16]{1,0:T(8,128)} %param.31) | copy-start | bytes 2116
  409.7 120.1 %copy-start.12 = (f32[11,16]{1,0:T(8,128)S(1)}, f32[11,16]{1,0:T(8,128)}, u32[]{:S(2)}) copy-start(f32[11,16]{1,0:T(8,128)} %param.30) | copy-start | bytes 2116
  409.7 120.7 %copy-start.1 = (f32[192,512]{1,0:T(8,128)S(1)}, f32[192,512]{1,0:T(8,128)}, u32[]{:S(2)}) copy-start(f32[192,512]{1,0:T(8,128)} %param.23) | copy-start | bytes 1179652
  409.7 120.7 %copy-start.7 = (f32[192,512]{1,0:T(8,128)S(1)}, f32[192,512]{1,0:T(8,128)}, u32[]{:S(2)}) copy-start(f32[192,512]{1,0:T(8,128)} %param.24) | copy-start | bytes 1179652
  409.7 120.7 %copy-start.8 = (f32[192,512]{1,0:T(8,128)S(1)}, f32[192,512]{1,0:T(8,128)}, u32[]{:S(2)}) copy-start(f32[192,512]{1,0:T(8,128)} %param.25) | copy-start | bytes 1179652
  409.7 267.1 %copy-start.5 = (f32[256,512]{1,0:T(8,128)S(1)}, f32[256,512]{1,0:T(8,128)}, u32[]{:S(2)}) copy-start(f32[256,512]{1,0:T(8,128)} %param.27) | copy-start | bytes 1572868
  530.4 146.5 %copy-start.16 = (pred[256]{0:T(512)(128)(4,1)S(1)}, pred[256]{0:T(512)(128)(4,1)}, u32[]{:S(2)}) copy-start(pred[256]{0:T(512)(128)(4,1)} %copy-done.15) | copy-start | bytes 772
  530.4 146.5 %copy-start.18 = (pred[256]{0:T(512)(128)(4,1)S(1)}, pred[256]{0:T(512)(128)(4,1)}, u32[]{:S(2)}) copy-start(pred[256]{0:T(512)(128)(4,1)} %copy-done.17) | copy-start | bytes 772
Sparse Core Ops, SparseCore 0:
  11.5 72.3 all-gather.2
  87.4 75.9 all-gather.4
  378.0 148.9 reduce-scatter.2
  529.3 145.2 reduce-scatter.4

commit v2 on v1

--- a/solution.py
+++ b/solution.py
@@ -640,32 +640,57 @@
     )(plan, d_query, dk, dv, normed, inverse, d_above, memory, context, dec_rows, wk_two, wk_two, dec_rows, small)
 
 
-def self_back_kernel(plan, *refs, masked):
-    if masked:
-        dq, dk, dv, d_above, x, wqkv, flags, d_x, g_qkv, mask_sum, turn = refs
-    else:
-        dq, dk, dv, d_above, x, wqkv, d_x, g_qkv, turn = refs
+def qkv_weights_kernel(plan, x, dq, dk, dv, g_qkv, turn):
     i = pl.program_id(0)
-    mine = pl.ds(pl.multiple_of(i * TILE, TILE), TILE)
 
     @pl.when(i == 0)
     def _():
         turn[...] = turned(x[...])
-        if masked:
-            mask_sum[...] = jnp.zeros_like(mask_sum)
-
-    pieces = jnp.concatenate([ref[mine, :] for ref in (dq, dk, dv)], axis=1)
+
+    for j, ref in enumerate((dq, dk, dv)):
+
+        @pl.when(i == j)
+        def _(ref=ref):
+            put_block(g_qkv, 0, nn(turn[...], ref[...]).astype(LOW))
+
+
+def qkv_weights(plan, x, dq, dk, dv, units, name):
+    number, width = x.shape
+    full = whole((number, width))
+    if units:
+        shape = (width // 16, 3, 16, width)
+        spec = pl.BlockSpec((width // 16, 1, 16, width), lambda i, *_: (0, i, 0, 0))
+    else:
+        shape = (3, width, width)
+        spec = pl.BlockSpec((1, width, width), lambda i, *_: (i, 0, 0))
+    return call(
+        qkv_weights_kernel,
+        (3,),
+        [full] * 4,
+        spec,
+        shaped(shape, LOW),
+        [pltpu.VMEM((width, number), LOW)],
+        6 * number * width * width,
+        12 * number * width,
+        name,
+    )(plan, x, dq, dk, dv)
+
+
+def qkv_inputs_kernel(plan, *refs, masked):
+    if masked:
+        dq, dk, dv, d_above, wqkv, flags, d_x, mask_sum = refs
+    else:
+        dq, dk, dv, d_above, wqkv, d_x = refs
+    pieces = jnp.concatenate([dq[...], dk[...], dv[...]], axis=1)
     weights = jnp.concatenate([block_of(wqkv, j) for j in range(3)], axis=1)
     total = nt(pieces, weights)
     if masked:
         total = total + d_above[...]
-    for j, ref in enumerate((dq, dk, dv)):
-
-        @pl.when(i == j)
-        def _(ref=ref):
-            put_block(g_qkv, 0, nn(turn[...], ref[...]).astype(LOW))
-
-    if masked:
+
+        @pl.when(pl.program_id(0) == 0)
+        def _():
+            mask_sum[...] = jnp.zeros_like(mask_sum)
+
         hit = column_of(flags[...]) == 1.0
         d_x[...] = jnp.where(hit, 0.0, total)
         mask_sum[0:1, :] += jnp.sum(jnp.where(hit, total, 0.0), axis=0, keepdims=True)
@@ -674,34 +699,27 @@
         d_x[...] += total
 
 
-def self_projections_back(plan, dq, dk, dv, d_above, x, wqkv, wqkv_spec, flags, units, name):
-    number, width = x.shape
-    full = whole((number, width))
+def qkv_inputs(plan, dq, dk, dv, d_above, wqkv, wqkv_spec, flags, name):
+    number, width = dq.shape
     masked = flags is not None
-    if units:
-        g_shape = (width // 16, 3, 16, width)
-        g_spec = pl.BlockSpec((width // 16, 1, 16, width), lambda i, *_: (0, jnp.minimum(i, 2), 0, 0))
-    else:
-        g_shape = (3, width, width)
-        g_spec = pl.BlockSpec((1, width, width), lambda i, *_: (jnp.minimum(i, 2), 0, 0))
-    in_specs = [full, full, full, rows_of(width), full, wqkv_spec]
-    out_specs = [rows_of(width), g_spec]
-    out_shape = [shaped((number, width), F32), shaped(g_shape, LOW)]
-    operands = [dq, dk, dv, d_above, x, wqkv]
+    in_specs = [rows_of(width)] * 4 + [wqkv_spec]
+    out_specs = [rows_of(width)]
+    out_shape = [shaped((number, width), F32)]
+    operands = [dq, dk, dv, d_above, wqkv]
     if masked:
         in_specs.append(pl.BlockSpec((1, TILE), lambda i, *_: (0, i)))
         out_specs.append(whole((8, width)))
         out_shape.append(shaped((8, width), F32))
         operands.append(flags)
     return call(
-        functools.partial(self_back_kernel, masked=masked),
+        functools.partial(qkv_inputs_kernel, masked=masked),
         (number // TILE,),
         in_specs,
         out_specs,
         out_shape,
-        [pltpu.VMEM((width, number), LOW)],
-        12 * number * width * width,
-        20 * number * width,
+        [],
+        6 * number * width * width,
+        16 * number * width,
         name,
     )(plan, *operands)
 
@@ -790,6 +808,126 @@
         + decay * weight
     )
     return (moved, first_new, second_new)
+
+
+CORE, X, Y, Z_LOW, Z_HIGH = 0, 1, 2, 3, 4
+BITS = 5
+
+
+def partner(bit):
+    return [(i, i ^ (1 << bit)) for i in range(1 << BITS)]
+
+
+def bit_of(me, bit):
+    return (me >> bit) & 1
+
+
+def take(values, axis, index):
+    return lax.dynamic_index_in_dim(values, index, axis, keepdims=False)
+
+
+def overlaps(sizes, own):
+    found = []
+    first = 0
+    for piece, size in enumerate(sizes):
+        at = first
+        while at < first + size:
+            owner = at // own
+            end = min(first + size, (owner + 1) * own)
+            found.append((piece, at - first, owner, at - owner * own, end - at))
+            at = end
+        first += size
+    return found
+
+
+def pack_kernel(core, *refs, copies, number):
+    pieces, send, keep, semaphores = refs[:number], refs[number], refs[number + 1], refs[number + 2]
+    for side in (0, 1):
+
+        @pl.when(core[0] == side)
+        def _():
+            handles = []
+            for n, (piece, at, owner, to, rows) in enumerate(copies):
+                target = keep if owner % 2 == side else send
+                handles.append(
+                    pltpu.make_async_copy(
+                        pieces[piece].at[pl.ds(at, rows)],
+                        target.at[owner // 2, pl.ds(to, rows)],
+                        semaphores.at[n],
+                    )
+                )
+            for handle in handles:
+                handle.start()
+            for handle in handles:
+                handle.wait()
+
+
+def pack(core, pieces, copies, block, name):
+    width = pieces[0].shape[1]
+    shape = shaped((1 << (BITS - 1), block, width), LOW)
+    anywhere = pl.BlockSpec(memory_space=pl.ANY)
+    total = sum(piece.size for piece in pieces)
+    return call(
+        functools.partial(pack_kernel, copies=copies, number=len(pieces)),
+        (1,),
+        [whole(piece.shape) for piece in pieces],
+        [anywhere, anywhere],
+        [shape, shape],
+        [pltpu.SemaphoreType.DMA((len(copies),))],
+        0,
+        4 * total,
+        name,
+    )(core, *pieces)
+
+
+def add_low(former, latter):
+    return (former.astype(F32) + latter.astype(F32)).astype(LOW)
+
+
+def swap(values, bit):
+    return lax.ppermute(values, "fsdp", partner(bit))
+
+
+def reduce_owned(me, send, keep, cut):
+    rows, width = send.shape[1:]
+    x, y, low, high = (bit_of(me, b) for b in (X, Y, Z_LOW, Z_HIGH))
+    (send,) = yield (send,)
+    chips = add_low(keep, swap(send, CORE)).reshape(2, 2, 2, 2, rows, width)
+    first, second = chips[..., :cut, :], chips[..., cut:, :]
+    for_y, for_x = yield (take(first, 2, 1 - y), take(second, 3, 1 - x))
+    first = add_low(take(first, 2, y), swap(for_y, Y))
+    second = add_low(take(second, 3, x), swap(for_x, X))
+    for_x, for_y = yield (take(first, 2, 1 - x), take(second, 2, 1 - y))
+    first = add_low(take(first, 2, x), swap(for_x, X))
+    second = add_low(take(second, 2, y), swap(for_y, Y))
+    column = jnp.concatenate([first, second], axis=2)
+    (for_z,) = yield (take(column, 1, 1 - low),)
+    column = add_low(take(column, 1, low), swap(for_z, Z_LOW))
+    (for_z,) = yield (take(column, 0, 1 - high),)
+    return take(column, 0, high).astype(F32) + swap(for_z, Z_HIGH).astype(F32)
+
+
+class Rounds:
+    def __init__(self, steps):
+        self.steps = steps
+        self.sent = next(steps)
+        self.result = None
+
+    def before(self, *operands):
+        sent, operands = lax.optimization_barrier((self.sent, operands))
+        self.move(sent)
+        return operands[0] if len(operands) == 1 else operands
+
+    def move(self, sent):
+        try:
+            self.sent = self.steps.send(sent)
+        except StopIteration as stop:
+            self.sent, self.result = None, stop.value
+
+    def finish(self):
+        while self.result is None:
+            self.move(self.sent)
+        return self.result
 
 
 def on_device(
@@ -881,49 +1019,74 @@
         dec_plan, dcq, dck, dcv, s_hat, s_inv, d_two, memory, s_ctx, dec_rows, dec_two, smalls
     )
     dsq, dsk, dsv = attention_backward(dec_plan, s_q, s_kv, d_sctx, s_lse, tgt_owner, tgt_key, "dec_back")
-    tgt_grad, g_sqkv, mask_sum = self_projections_back(
-        dec_plan, dsq, dsk, dsv, d_one, start, dec_three, whole(dec_three.shape), flags, False, "dec_proj_back"
-    )
+    g_sqkv = qkv_weights(dec_plan, start, dsq, dsk, dsv, False, "dec_qkv_weights")
+    dec_pieces = [
+        g_sqkv.transpose(1, 0, 2).reshape(-1, width),
+        g_sout,
+        g_cq,
+        g_ckv.reshape(-1, width),
+        g_cout,
+        g_dup.reshape(-1, width),
+        g_ddown,
+    ]
+    by_rounds = devices == 1 << BITS
+    rounds = None
+    if by_rounds:
+        core = bit_of(me, CORE)[None].astype(jnp.int32)
+        copies = overlaps([p.shape[0] for p in dec_pieces], dec_size)
+        send, keep = pack(core, dec_pieces, copies, dec_size, "dec_pack")
+        rounds = Rounds(reduce_owned(me, send, keep, dec_size // 2))
+        dsq, dsk, dsv = rounds.before(dsq, dsk, dsv)
+    tgt_grad, mask_sum = qkv_inputs(
+        dec_plan, dsq, dsk, dsv, d_one, dec_three, whole(dec_three.shape), flags, "dec_qkv_inputs"
+    )
+    if by_rounds:
+        d_memory, mask_sum = rounds.before(d_memory, mask_sum)
     de_inner, de_down, d_mid, d_eattn, d_ectx, sums_e = ffn_backward(
         enc_plan, [enc_cot, d_memory], (t_hat, t_inv), e_slope, (e_hat, e_inv), (enc_four, enc_rows, enc_rows),
         [enc_up, enc_down, enc_wo], smalls, 0, 2, "enc_ffn_back",
     )
+    if by_rounds:
+        de_inner, d_ectx = rounds.before(de_inner, d_ectx)
     g_up, g_down, g_out = ffn_weights(
         enc_plan, e_hat, de_inner, de_down, e_hidden, e_ctx, d_eattn, smalls, 0, "enc_ffn_weights"
     )
+    if by_rounds:
+        d_ectx, g_up = rounds.before(d_ectx, g_up)
     deq, dek, dev = attention_backward(enc_plan, e_q, e_kv, d_ectx, e_lse, src_owner, src_key, "enc_back")
-    src_grad, g_qkv = self_projections_back(
-        enc_plan, deq, dek, dev, d_mid, src_in, enc_three, three_spec, None, True, "enc_proj_back"
-    )
-
-    dec_grad = jnp.concatenate(
-        [
-            g_sqkv.transpose(1, 0, 2).reshape(-1, width),
-            g_sout,
-            g_cq,
-            g_ckv.reshape(-1, width),
-            g_cout,
-            g_dup.reshape(-1, width),
-            g_ddown,
-        ],
-        axis=0,
-    )
-    enc_grad = jnp.concatenate(
-        [g_qkv.reshape(-1, width), g_out, g_up.reshape(-1, width), g_down], axis=0
-    )
+    if by_rounds:
+        deq, dek, dev = rounds.before(deq, dek, dev)
+    g_qkv = qkv_weights(enc_plan, src_in, deq, dek, dev, True, "enc_qkv_weights")
+
+    enc_pieces = [g_qkv.reshape(-1, width), g_out, g_up.reshape(-1, width), g_down]
     small_grad = jnp.concatenate([sums_e[:4], sums_c[:2], sums_d[:4], mask_sum[:1]], axis=0)
-    dec_grad = arrange_all(dec_grad, dec_size, dec_map, from_units)
-    enc_grad = arrange_all(enc_grad, enc_size, enc_map, from_units)
     share = small_master.shape[1]
     small_wire = small_grad.reshape(-1, devices, share).transpose(1, 0, 2).reshape(devices, -1).astype(LOW)
     held = small_wire.shape[1]
-    small_wire = jnp.pad(small_wire, ((0, 0), (0, 16 * width - held))).reshape(devices, 16, width)
-    enc_wire = jnp.concatenate([enc_grad.reshape(devices, enc_size, width), small_wire], axis=1)
-    dec_summed = lax.psum_scatter(dec_grad, "fsdp", scatter_dimension=0, tiled=True)
-    enc_summed = lax.psum_scatter(enc_wire.reshape(-1, width), "fsdp", scatter_dimension=0, tiled=True)
-    small_summed = enc_summed[enc_size:].reshape(-1)[:held].reshape(-1, share).astype(F32)
-    enc_summed = arrange_own(enc_summed[:enc_size].astype(F32), me * enc_size, enc_map, from_units)
-    dec_summed = arrange_own(dec_summed.astype(F32), me * dec_size, dec_map, from_units)
+    small_wire = jnp.pad(small_wire, ((0, 0), (0, 16 * width - held))).reshape(devices * 16, width)
+    if by_rounds:
+        dec_summed = rounds.finish()
+        copies = overlaps([p.shape[0] for p in enc_pieces], enc_size)
+        copies += [(len(enc_pieces), 16 * i, i, enc_size, 16) for i in range(devices)]
+        send, keep = pack(core, enc_pieces + [small_wire], copies, enc_size + 16, "enc_pack")
+        rounds = Rounds(reduce_owned(me, send, keep, enc_size // 2 + 16))
+        deq, dek, dev = rounds.before(deq, dek, dev)
+    src_grad = qkv_inputs(enc_plan, deq, dek, dev, d_mid, enc_three, three_spec, None, "enc_qkv_inputs")[0]
+    if by_rounds:
+        enc_summed = rounds.finish()
+    else:
+        dec_grad = arrange_all(jnp.concatenate(dec_pieces, axis=0), dec_size, dec_map, from_units)
+        enc_grad = arrange_all(jnp.concatenate(enc_pieces, axis=0), enc_size, enc_map, from_units)
+        enc_wire = jnp.concatenate(
+            [enc_grad.reshape(devices, enc_size, width), small_wire.reshape(devices, 16, width)], axis=1
+        )
+        dec_summed = lax.psum_scatter(dec_grad, "fsdp", scatter_dimension=0, tiled=True).astype(F32)
+        enc_summed = lax.psum_scatter(
+            enc_wire.reshape(-1, width), "fsdp", scatter_dimension=0, tiled=True
+        ).astype(F32)
+    small_summed = enc_summed[enc_size:].reshape(-1)[:held].reshape(-1, share)
+    enc_summed = arrange_own(enc_summed[:enc_size], me * enc_size, enc_map, from_units)
+    dec_summed = arrange_own(dec_summed, me * dec_size, dec_map, from_units)
 
     part = 1.0 / devices
     enc_summed = enc_summed * part

time: 697 us -> 513 us (0.74)
  waiting for transfers between devices: 316 us -> 111 us
  starting transfers between devices: 0.16 us -> 28 us
  local copies, waits for them, and re-layouts: 39 us -> 26.4 us
  Pallas kernels: 237 us -> 248 us
    reduce_scatter x2 -> x0, waiting for transfers between devices: 259 us -> none  [the longest x1 142 us: on_device(): lax.psum_scatter(dec_grad, 'fsdp', scatter_dimension=0, tiled=True)]
    ppermute x0 -> x14, waiting for transfers between devices: none -> 52.2 us  [swap(): return lax.ppermute(values, 'fsdp', partner(bit))]
    ppermute x0 -> x14, starting transfers between devices: none -> 27.9 us  [swap(): return lax.ppermute(values, 'fsdp', partner(bit))]
    pallas_call x2 -> x6, Pallas kernels: 20.3 us -> 40.8 us  [the longest x2 15.3 us: qkv_inputs(): call(functools.partial(qkv_inputs_kernel, masked=masked), (number // TILE...]
    concatenate x2 -> x0, other arithmetic: 11.9 us -> none  [the longest x1 6.16 us: on_device(): jnp.concatenate([enc_grad.reshape(devices, enc_size, width), small_wire],...]
    unnamed x49 -> x60, local copies, waits for them, and re-layouts: 13 us -> 1.62 us
    convert_element_type x2 -> x12, other arithmetic: 1.96 us -> 9.45 us  [add_low(): return (former.astype(F32) + latter.astype(F32)).astype(LOW)]
  transfers between devices with their start and end apart: 4 -> 16, of which waited for: 4 -> 12; matrix products, arithmetic and copies ran while one was open for 6% -> 6% of each run, Pallas kernels for 7% -> 20%
where the time goes in v2:
time: 513 us; the launch traced here: 503 us
  Pallas kernels  248 us (48%)
  waiting for transfers between devices  111 us (22%)
  blocking collectives  43.9 us (9%)
  other arithmetic  30.2 us (6%)
  starting transfers between devices  28 us (5%)
  local copies, waits for them, and re-layouts  26.4 us (5%)
  between operations  15.4 us (3%)
    pallas_call x3, Pallas kernels, attention_backward(): call(attention_back_kernel, (number // TILE,), [rows_of(width), at_block(...  56 us
    ppermute x14, waiting for transfers between devices, swap(): return lax.ppermute(values, 'fsdp', partner(bit))  52.2 us
    all_gather x1, waiting for transfers between devices, on_device(): dec_rows = lax.all_gather(dec_own, 'fsdp', axis=0, tiled=True)  44.2 us
    all_gather x1, blocking collectives, on_device(): lax.all_gather(small_master.astype(LOW), 'fsdp', axis=1, tiled=True)  43.9 us
    pallas_call x2, Pallas kernels, self_block(): call(functools.partial(fwd_block_kernel, cross=False, gain_row=gain_row),...  34.1 us
    pallas_call x2, Pallas kernels, ffn_forward(): call(functools.partial(ffn_kernel, mid_row=mid_row, top_row=top_row), (nu...  33.6 us
    pallas_call x2, Pallas kernels, ffn_backward(): call(functools.partial(ffn_back_kernel, summed=len(cots) == 2, mid_row=mi...  28.8 us
    ppermute x14, starting transfers between devices, swap(): return lax.ppermute(values, 'fsdp', partner(bit))  27.9 us
  transfers between devices with their start and end apart: 16, of which 12 were waited for; matrix products, arithmetic and copies ran while one was open for 6% of the time, Pallas kernels for 20%

profile of v2, /device:TPU:0, one launch (start us, length us, event | category | flops | bytes accessed | tf_op | source)
XLA Modules:
  0.0 502.5 jit_solution(17799634275655520894)
XLA Ops:
  7.2 1.1 convert_element_type.251
  8.7 0.8 fusion.19
  10.0 0.8 fusion.18
  12.5 43.9 %all_gather.10 = bf16[11,512]{0,1:T(8,128)(2,1)S(1)} all-gather(bf16[11,16]{0,1:T(8,128)(2,1)S(1)} %copy.108), channel_id=1, replica_groups=mesh['fsdp'=32] {'fsdp'}, dimensions={1}, use_global_device_ids=true | all-gather | bytes 11616 | tf_op jit(solution)/shard_map/all_gather | solution.py:965
  65.7 1.3 fusion.21
  66.9 1.2 fusion.23
  68.2 1.2 broadcast_select_fusion.refs_0_.x
  69.3 14.6 %all-gather.3.cloned.1.call-done.refs_2_.wdown.refs_8_.refs_9_ = bf16[6144,512]{1,0:T(8,128)(2,1)} async-done(((bf16[192,512]{1,0:T(8,128)(2,1)}), bf16[6144,512]{1,0:T(8,128)(2,1)}) %all-gather.3.cloned.1.call-update) | async-done | bytes 6291472 | tf_op jit(solution)/shard_map/all_gather | solution.py:963
  83.9 18.5 %enc_block.1 = (bf16[1024,512]{1,0:T(8,128)(2,1)}, bf16[1024,1024]{1,0:T(8,128)(2,1)}, bf16[1024,512]{1,0:T(8,128)(2,1)}, f32[8,1024]{1,0:T(8,128)}, f32[1024,512]{1,0:T(8,128)}, /*index=5*/f32[1024,128]{1,0:T(8,128)}) custom-call(s32[3,8]{1,0:T(4,128)} %get-tuple-element.232.plan, bf16[1024,512]{1,0:T(8,128)(2,1)} %x.5, ...), custom_call_target="tpu_custom_call" | custom-call | flops 3221225472 | bytes 8388608 | tf_op jit(solution)/shard_map/enc_block/pallas_call | solution.py:286
  102.4 16.8 %enc_ffn.1 = (bf16[1024,2048]{1,0:T(8,128)(2,1)}, bf16[1024,2048]{1,0:T(8,128)(2,1)}, bf16[1024,512]{1,0:T(8,128)(2,1)}, f32[1024,512]{1,0:T(8,128)}, f32[1024,128]{1,0:T(8,128)}) custom-call(s32[3,8]{1,0:T(4,128)} %get-tuple-element.232.plan, f32[1024,512]{1,0:T(8,128)} %get-tuple-element.106.normed.refs_5_, bf16[96,4,16,512]{3,2,1,0:T(8,128)(2,1)} %bitcast.210, ...), custom_call_target="tpu_custom_call" | custom-call | flops 4294967296 | bytes 10485760 | tf_op jit(solution)/shard_map/enc_ffn/pallas_call | solution.py:348
  119.2 44.2 %all-gather.5.cloned.1.call-done.refs_2_.refs_5_.wdown.refs_7_.refs_8_.wq.wo = bf16[8192,512]{1,0:T(8,128)(2,1)} async-done(((bf16[256,512]{1,0:T(8,128)(2,1)}), bf16[8192,512]{1,0:T(8,128)(2,1)}) %all-gather.5.cloned.1.call-update) | async-done | bytes 8388624 | tf_op jit(solution)/shard_map/all_gather | solution.py:964
  163.4 1.4 slice-done
  164.8 2.2 reshape.651
  167.0 3.1 copy.158
  170.1 15.6 %dec_block.1 = (bf16[1024,512]{1,0:T(8,128)(2,1)}, bf16[1024,1024]{1,0:T(8,128)(2,1)}, bf16[1024,512]{1,0:T(8,128)(2,1)}, f32[8,1024]{1,0:T(8,128)}, f32[1024,512]{1,0:T(8,128)}, /*index=5*/f32[1024,128]{1,0:T(8,128)}) custom-call(s32[3,8]{1,0:T(4,128)} %get-tuple-element.231.plan, bf16[1024,512]{1,0:T(8,128)(2,1)} %broadcast_select_fusion.refs_0_.x, ...), custom_call_target="tpu_custom_call" | custom-call | flops 3221225472 | bytes 8388608 | tf_op jit(solution)/shard_map/dec_block/pallas_call | solution.py:286
  185.7 16.4 %cross_block.1 = (bf16[1024,512]{1,0:T(8,128)(2,1)}, bf16[1024,1024]{1,0:T(8,128)(2,1)}, bf16[1024,512]{1,0:T(8,128)(2,1)}, f32[8,1024]{1,0:T(8,128)}, f32[1024,512]{1,0:T(8,128)}, /*index=5*/f32[1024,128]{1,0:T(8,128)}) custom-call(s32[3,8]{1,0:T(4,128)} %get-tuple-element.230.plan, f32[1024,512]{1,0:T(8,128)} %get-tuple-element.108.refs_0_.normed, ...), custom_call_target="tpu_custom_call" | custom-call | flops 3221225472 | bytes 8388608 | tf_op jit(solution)/shard_map/cross_block/pallas_call | solution.py:303
  202.2 16.8 %dec_ffn.1 = (bf16[1024,2048]{1,0:T(8,128)(2,1)}, bf16[1024,2048]{1,0:T(8,128)(2,1)}, bf16[1024,512]{1,0:T(8,128)(2,1)}, f32[1024,512]{1,0:T(8,128)}, f32[1024,128]{1,0:T(8,128)}) custom-call(s32[3,8]{1,0:T(4,128)} %get-tuple-element.231.plan, f32[1024,512]{1,0:T(8,128)} %get-tuple-element.109.normed.refs_4_, bf16[128,4,16,512]{3,2,1,0:T(8,128)(2,1)} %bitcast.205, ...), custom_call_target="tpu_custom_call" | custom-call | flops 4294967296 | bytes 10485760 | tf_op jit(solution)/shard_map/dec_ffn/pallas_call | solution.py:348
  219.0 14.4 %dec_ffn_back.1 = (bf16[1024,2048]{1,0:T(8,128)(2,1)}, bf16[1024,512]{1,0:T(8,128)(2,1)}, f32[1024,512]{1,0:T(8,128)}, bf16[1024,512]{1,0:T(8,128)(2,1)}, bf16[1024,512]{1,0:T(8,128)(2,1)}, /*index=5*/f32[8,512]{1,0:T(8,128)}) custom-call(s32[3,8]{1,0:T(4,128)} %get-tuple-element.231.plan, bf16[1024,512]{1,0:T(8,128)(2,1)} %refs_0_.4, ...), custom_call_target="tpu_custom_call" | custom-call | flops 4294967296 | bytes 13631488 | tf_op jit(solution)/shard_map/dec_ffn_back/pallas_call | solution.py:411
  233.3 17.2 %cross_back.1 = (bf16[1024,512]{1,0:T(8,128)(2,1)}, bf16[1024,512]{1,0:T(8,128)(2,1)}, bf16[1024,512]{1,0:T(8,128)(2,1)}) custom-call(s32[3,8]{1,0:T(4,128)} %get-tuple-element.230.plan, bf16[1024,512]{1,0:T(8,128)(2,1)} %get-tuple-element.113.q_ref, bf16[1024,1024]{1,0:T(8,128)(2,1)} %get-tuple-element.114.k_ref.v_ref, ...), custom_call_target="tpu_custom_call" | custom-call | flops 2147483648 | bytes 6291456 | tf_op jit(solution)/shard_map/cross_back/pallas_call | solution.py:548
  250.5 14.1 %cross_projections_back.1 = (f32[1024,512]{1,0:T(8,128)}, f32[1024,512]{1,0:T(8,128)}, bf16[1024,512]{1,0:T(8,128)(2,1)}, bf16[512,512]{1,0:T(8,128)(2,1)}, bf16...) custom-call(s32[3,8]{1,0:T(4,128)} %get-tuple-element.231.plan, ...), custom_call_target="tpu_custom_call" | custom-call | flops 4294967296 | bytes 12582912 | tf_op jit(solution)/shard_map/cross_projections_back/pallas_call | solution.py:625
  264.6 17.1 %dec_back.1 = (bf16[1024,512]{1,0:T(8,128)(2,1)}, bf16[1024,512]{1,0:T(8,128)(2,1)}, bf16[1024,512]{1,0:T(8,128)(2,1)}) custom-call(s32[3,8]{1,0:T(4,128)} %get-tuple-element.231.plan, bf16[1024,512]{1,0:T(8,128)(2,1)} %get-tuple-element.111.q_ref, bf16[1024,1024]{1,0:T(8,128)(2,1)} %get-tuple-element.112.k_ref.v_ref, ...), custom_call_target="tpu_custom_call" | custom-call | flops 2147483648 | bytes 6291456 | tf_op jit(solution)/shard_map/dec_back/pallas_call | solution.py:548
  281.7 6.0 %dec_qkv_weights.1 = bf16[3,512,512]{2,1,0:T(8,128)(2,1)} custom-call(s32[3,8]{1,0:T(4,128)} %get-tuple-element.231.plan, bf16[1024,512]{1,0:T(8,128)(2,1)} %broadcast_select_fusion.refs_0_.x, bf16[1024,512]{1,0:T(8,128)(2,1)} %get-tuple-element.147.dq.refs_0_, bf16[1024,512]{1,0:T(8,128)(2,1)} %get-tuple-element.148.dk.refs_1_, ...), custom_call_target="tpu_custom_call" | custom-call | flops 1610612736 | bytes 6291456 | tf_op jit(solution)/shard_map/dec_qkv_weights/pallas_call | solution.py:666
  287.7 2.8 copy.114
  290.4 2.5 reshape.654.refs_0_
  292.9 11.9 %dec_ffn_weights.1 = (bf16[32,4,16,512]{3,2,1,0:T(8,128)(2,1)}, bf16[2048,512]{1,0:T(8,128)(2,1)}, bf16[512,512]{1,0:T(8,128)(2,1)}) custom-call(s32[3,8]{1,0:T(4,128)} %get-tuple-element.231.plan, f32[1024,512]{1,0:T(8,128)} %get-tuple-element.109.normed.refs_4_, bf16[1024,2048]{1,0:T(8,128)(2,1)} %get-tuple-element.135.d_inner, ...), custom_call_target="tpu_custom_call" | custom-call | flops 4294967296 | bytes 12582912 | tf_op jit(solution)/shard_map/dec_ffn_weights/pallas_call | solution.py:461
  304.8 7.1 %dec_pack.1 = (bf16[16,256,512]{2,1,0:T(8,128)(2,1)}, bf16[16,256,512]{2,1,0:T(8,128)(2,1)}) custom-call(s32[1]{0:T(128)} %bitcast.27.core, bf16[1536,512]{1,0:T(8,128)(2,1)} %reshape.654.refs_0_, bf16[512,512]{1,0:T(8,128)(2,1)} %get-tuple-element.132.refs_1_, bf16[512,512]{1,0:T(8,128)(2,1)} %get-tuple-element.133.refs_2_, bf16[1024,512]{1,0:T(8,128)(2,1)} %bitcast.229, ...), custom_call_target="tpu_custom_call" | custom-call | bytes 16777216 | tf_op jit(solution)/shard_map/dec_pack/pallas_call | solution.py:870
  311.9 10.2 %collective-permute-start = (bf16[16,256,512]{2,1,0:T(8,128)(2,1)}, bf16[16,256,512]{2,1,0:T(8,128)(2,1)}, u32[]{:S(2)}, u32[]{:S(2)}) collective-permute-start(bf16[16,256,512]{2,1,0:T(8,128)(2,1)} %get-tuple-element.145), channel_id=1, source_target_pairs={{0,1},{1,0},{2,3},{3,2},{4,5},{5,4},{6,7},{7,6},{8,9},{9,8},{10,11... | collective-permute-start | bytes 12582920 | tf_op jit(solution)/shard_map/ppermute | solution.py:888
  322.7 8.3 %dec_qkv_inputs.1 = (f32[1024,512]{1,0:T(8,128)}, f32[8,512]{1,0:T(8,128)}) custom-call(s32[3,8]{1,0:T(4,128)} %get-tuple-element.231.plan, bf16[1024,512]{1,0:T(8,128)(2,1)} %get-tuple-element.147.dq.refs_0_, bf16[1024,512]{1,0:T(8,128)(2,1)} %get-tuple-element.148.dk.refs_1_, bf16[1024,512]{1,0:T(8,128)(2,1)} %get-tuple-element.149.dv.refs_2_, ...), custom_call_target="tpu_custom_call" | custom-call | flops 1610612736 | bytes 8388608 | tf_op jit(solution)/shard_map/dec_qkv_inputs/pallas_call | solution.py:714
  331.0 3.5 add_convert_fusion
  335.0 1.2 copy.159
  336.4 1.5 collective-permute-start.2
  337.9 3.1 collective-permute-start.1
  341.0 14.4 %enc_ffn_back.1 = (bf16[1024,2048]{1,0:T(8,128)(2,1)}, bf16[1024,512]{1,0:T(8,128)(2,1)}, f32[1024,512]{1,0:T(8,128)}, bf16[1024,512]{1,0:T(8,128)(2,1)}, bf16[1024,512]{1,0:T(8,128)(2,1)}, /*index=5*/f32[8,512]{1,0:T(8,128)}) custom-call(s32[3,8]{1,0:T(4,128)} %get-tuple-element.232.plan, bf16[1024,512]{1,0:T(8,128)(2,1)} %refs_0_.5, ...), custom_call_target="tpu_custom_call" | custom-call | flops 4294967296 | bytes 13631488 | tf_op jit(solution)/shard_map/enc_ffn_back/pallas_call | solution.py:411
  355.4 6.4 %collective-permute-done.2 = bf16[2,2,2,128,512]{4,3,0,1,2:T(8,128)(2,1)S(1)} collective-permute-done((bf16[2,2,2,128,512]{4,3,0,1,2:T(8,128)(2,1)}, bf16[2,2,2,128,512]{4,3,0,1,2:T(8,128)(2,1)S(1)}, u32[]{:S(2)}, u32[]{:S(2)}) %collective-permute-start.2) | collective-permute-done | bytes 1048608 | tf_op jit(solution)/shard_map/ppermute | solution.py:888
  362.1 1.9 collective-permute-done.1
  364.4 0.8 dynamic-slice_bitcast_fusion.1
  365.2 2.9 collective-permute-start.4
  368.6 12.0 %enc_ffn_weights.1 = (bf16[32,4,16,512]{3,2,1,0:T(8,128)(2,1)}, bf16[2048,512]{1,0:T(8,128)(2,1)}, bf16[512,512]{1,0:T(8,128)(2,1)}) custom-call(s32[3,8]{1,0:T(4,128)} %get-tuple-element.232.plan, f32[1024,512]{1,0:T(8,128)} %get-tuple-element.106.normed.refs_5_, bf16[1024,2048]{1,0:T(8,128)(2,1)} %get-tuple-element.164.d_inner, ...), custom_call_target="tpu_custom_call" | custom-call | flops 4294967296 | bytes 12582912 | tf_op jit(solution)/shard_map/enc_ffn_weights/pallas_call | solution.py:461
  381.5 3.2 collective-permute-start.5
  384.7 0.7 slice.99
  385.4 0.7 slice.97
  386.1 0.7 slice.98
  386.9 0.7 slice.100
  388.0 1.0 reshape.660.refs_4_
  389.0 21.7 %enc_back.1 = (bf16[1024,512]{1,0:T(8,128)(2,1)}, bf16[1024,512]{1,0:T(8,128)(2,1)}, bf16[1024,512]{1,0:T(8,128)(2,1)}) custom-call(s32[3,8]{1,0:T(4,128)} %get-tuple-element.232.plan, bf16[1024,512]{1,0:T(8,128)(2,1)} %get-tuple-element.171.q_ref, bf16[1024,1024]{1,0:T(8,128)(2,1)} %get-tuple-element.172.k_ref.v_ref, ...), custom_call_target="tpu_custom_call" | custom-call | flops 2147483648 | bytes 6291456 | tf_op jit(solution)/shard_map/enc_back/pallas_call | solution.py:548
  410.9 6.2 %enc_qkv_weights.1 = bf16[32,3,16,512]{3,2,1,0:T(8,128)(2,1)} custom-call(s32[3,8]{1,0:T(4,128)} %get-tuple-element.232.plan, bf16[1024,512]{1,0:T(8,128)(2,1)} %x.5, bf16[1024,512]{1,0:T(8,128)(2,1)} %get-tuple-element.189.dq.refs_0_, bf16[1024,512]{1,0:T(8,128)(2,1)} %get-tuple-element.190.dk.refs_1_, bf16[1024,512]{1,0:T(8,128)(2,1)} %get-tuple-element.191.dv.refs_2_), custom_call_target="tpu_custom_call" | custom-call | flops 1610612736 | bytes 6291456 | tf_op jit(solution)/shard_map/enc_qkv_weights/pallas_call | solution.py:666
  417.2 6.2 %enc_pack.1 = (bf16[16,208,512]{2,1,0:T(8,128)(2,1)}, bf16[16,208,512]{2,1,0:T(8,128)(2,1)}) custom-call(s32[1]{0:T(128)} %bitcast.27.core, bf16[1536,512]{1,0:T(8,128)(2,1)} %bitcast.228, bf16[512,512]{1,0:T(8,128)(2,1)} %get-tuple-element.181.refs_1_, bf16[2048,512]{1,0:T(8,128)(2,1)} %bitcast.223, bf16[2048,512]{1,0:T(8,128)(2,1)} %get-tuple-element.183.refs_3_, ...), custom_call_target="tpu_custom_call" | custom-call | bytes 13631488 | tf_op jit(solution)/shard_map/enc_pack/pallas_call | solution.py:870
  423.5 6.2 %collective-permute-done.6 = bf16[16,208,512]{2,1,0:T(8,128)(2,1)S(1)} collective-permute-done((bf16[16,208,512]{2,1,0:T(8,128)(2,1)}, bf16[16,208,512]{2,1,0:T(8,128)(2,1)S(1)}, u32[]{:S(2)}, u32[]{:S(2)}) %collective-permute-start.6) | collective-permute-done | bytes 3407904 | tf_op jit(solution)/shard_map/ppermute | solution.py:888
  429.7 3.1 add_convert_fusion.1
  433.6 2.5 collective-permute-start.7
  436.1 16.7 %collective-permute-done.9 = bf16[2,2,2,96,512]{4,3,0,1,2:T(8,128)(2,1)S(1)} collective-permute-done((bf16[2,2,2,96,512]{4,3,0,1,2:T(8,128)(2,1)S(1)}, bf16[2,2,2,96,512]{4,3,0,1,2:T(8,128)(2,1)S(1)}, u32[]{:S(2)}, u32[]{:S(2)}) %collective-permute-start.9) | collective-permute-done | bytes 786464 | tf_op jit(solution)/shard_map/ppermute | solution.py:888
  453.1 1.8 collective-permute-start.10
  454.9 2.4 collective-permute-done.7
  457.6 1.7 collective-permute-start.8
  459.3 5.6 %collective-permute-done.10 = bf16[2,2,96,512]{3,2,0,1:T(8,128)(2,1)S(1)} collective-permute-done((bf16[2,2,96,512]{3,2,0,1:T(8,128)(2,1)S(1)}, bf16[2,2,96,512]{3,2,0,1:T(8,128)(2,1)S(1)}, u32[]{:S(2)}, u32[]{:S(2)}) %collective-permute-start.10) | collective-permute-done | bytes 393248 | tf_op jit(solution)/shard_map/ppermute | solution.py:888
  465.0 3.6 collective-permute-done.8
  468.7 0.8 fusion.15
  469.5 7.0 %enc_qkv_inputs.1 = f32[1024,512]{1,0:T(8,128)} custom-call(s32[3,8]{1,0:T(4,128)} %get-tuple-element.232.plan, bf16[1024,512]{1,0:T(8,128)(2,1)} %get-tuple-element.189.dq.refs_0_, bf16[1024,512]{1,0:T(8,128)(2,1)} %get-tuple-element.190.dk.refs_1_, bf16[1024,512]{1,0:T(8,128)(2,1)} %get-tuple-element.191.dv.refs_2_, ...), custom_call_target="tpu_custom_call" | custom-call | flops 1610612736 | bytes 8388608 | tf_op jit(solution)/shard_map/enc_qkv_inputs/pallas_call | solution.py:714
  476.5 1.0 convert_add_fusion.10
  478.5 1.2 reshape.669
  480.3 1.1 fusion.8
  481.9 1.8 fusion.31
  483.7 8.2 %collective-permute-done.12 = bf16[208,512]{1,0:T(8,128)(2,1)S(1)} collective-permute-done((bf16[208,512]{1,0:T(8,128)(2,1)S(1)}, bf16[208,512]{1,0:T(8,128)(2,1)S(1)}, u32[]{:S(2)}, u32[]{:S(2)}) %collective-permute-start.12) | collective-permute-done | bytes 213024 | tf_op jit(solution)/shard_map/ppermute | solution.py:888
  493.8 1.5 fusion.32
  (162 shorter events, 20.6 us)
Async XLA Ops:
  7.2 1.5 copy-start.4
  7.2 2.4 copy-start
  7.2 76.7 %all-gather.3.cloned.1.call-start = ((), (), s32[]{:S(2)}) async-start(), calls=%async_computation | async-start | bytes 6488064 | tf_op jit(solution)/shard_map/all_gather | solution.py:963
  8.5 1.0 copy-start.17
  8.6 1.0 copy-start.19
  9.5 1.4 copy-start.26
  9.5 2.1 copy-start.25
  9.5 2.9 copy-start.14
  9.5 153.8 %all-gather.5.cloned.1.call-start = ((), (), s32[]{:S(2)}) async-start(), calls=%async_computation.1 | async-start | bytes 8650752 | tf_op jit(solution)/shard_map/all_gather | solution.py:964
  9.7 56.0 %copy-start.13 = (s32[1024]{0:T(1024)S(1)}, s32[1024]{0:T(1024)}, u32[]{:S(2)}) copy-start(s32[1024]{0:T(1024)} %param.20) | copy-start | bytes 12292
  9.7 58.5 %copy-start.8 = (bf16[1024,512]{1,0:T(8,128)(2,1)S(1)}, bf16[1024,512]{1,0:T(8,128)(2,1)}, u32[]{:S(2)}) copy-start(bf16[1024,512]{1,0:T(8,128)(2,1)} %param.17) | copy-start | bytes 3145732
  10.0 59.4 %copy-start.21 = (pred[256]{0:T(512)(128)(4,1)}, pred[256]{0:T(512)(128)(4,1)S(1)}, u32[]{:S(2)}) copy-start(pred[256]{0:T(512)(128)(4,1)S(1)} %get-tuple-element.235) | copy-start | bytes 772
  10.0 59.4 %copy-start.23 = (pred[256]{0:T(512)(128)(4,1)}, pred[256]{0:T(512)(128)(4,1)S(1)}, u32[]{:S(2)}) copy-start(pred[256]{0:T(512)(128)(4,1)S(1)} %get-tuple-element.236) | copy-start | bytes 772
  163.4 1.4 slice-start
  311.9 19.1 %collective-permute-start = (bf16[16,256,512]{2,1,0:T(8,128)(2,1)}, bf16[16,256,512]{2,1,0:T(8,128)(2,1)}, u32[]{:S(2)}, u32[]{:S(2)}) collective-permute-start(bf16[16,256,512]{2,1,0:T(8,128)(2,1)} %get-tuple-element.145), channel_id=1, source_target_pairs={{0,1},{1,0},{2,3},{3,2},{4,5},{5,4},{6,7},{7,6},{8,9},{9,8},{10,11... | collective-permute-start | bytes 12582920 | tf_op jit(solution)/shard_map/ppermute | solution.py:888
  322.7 8.3 %copy-start.1 = (bf16[16,256,512]{2,1,0:T(8,128)(2,1)S(1)}, bf16[16,256,512]{2,1,0:T(8,128)(2,1)}, u32[]{:S(2)}) copy-start(bf16[16,256,512]{2,1,0:T(8,128)(2,1)} %get-tuple-element.143) | copy-start | bytes 12582916
  336.4 25.4 %collective-permute-start.2 = (bf16[2,2,2,128,512]{4,3,0,1,2:T(8,128)(2,1)}, bf16[2,2,2,128,512]{4,3,0,1,2:T(8,128)(2,1)S(1)}, u32[]{:S(2)}, u32[]{:S(2)}) collective-permute-start(bf16[2,2,2,128,512]{4,3,0,1,2:T(8,128)(2,1)} %bitcast.196), channel_id=1, source_target_pairs={{0,2},{1,3},{2,0},{3,1},{4,6},{5,7},{6,4},{7,5},{8,10},{9,11},{10,... | collective-permute-start | bytes 3145736 | tf_op jit(solution)/shard_map/ppermute | solution.py:888
  337.9 26.1 %collective-permute-start.1 = (bf16[2,2,2,128,512]{4,3,0,1,2:T(8,128)(2,1)S(1)}, bf16[2,2,2,128,512]{4,3,0,1,2:T(8,128)(2,1)S(1)}, u32[]{:S(2)}, u32[]{:S(2)}) collective-permute-start(bf16[2,2,2,128,512]{4,3,0,1,2:T(8,128)(2,1)S(1)} %bitcast.231), channel_id=1, source_target_pairs={{0,4},{1,5},{2,6},{3,7},{4,0},{5,1},{6,2},{7,3},{8,12},{9,13},{10,... | collective-permute-start | bytes 3145736 | tf_op jit(solution)/shard_map/ppermute | solution.py:888
  362.1 2.3 copy-start.2
  365.2 15.4 %collective-permute-start.4 = (bf16[2,2,128,512]{3,2,0,1:T(8,128)(2,1)S(1)}, bf16[2,2,128,512]{3,2,0,1:T(8,128)(2,1)S(1)}, u32[]{:S(2)}, u32[]{:S(2)}) collective-permute-start(bf16[2,2,128,512]{3,2,0,1:T(8,128)(2,1)S(1)} %dynamic-slice_bitcast_fusion), channel_id=1, source_target_pairs={{0,4},{1,5},{2,6},{3,7},{4,0},{5,1},{6,2},{7,3},{8,12},{9,13},{10,... | collective-permute-start | bytes 1572872 | tf_op jit(solution)/shard_map/ppermute | solution.py:888
  368.2 13.2 %collective-permute-start.3 = (bf16[2,2,128,512]{3,2,0,1:T(8,128)(2,1)}, bf16[2,2,128,512]{3,2,0,1:T(8,128)(2,1)S(1)}, u32[]{:S(2)}, u32[]{:S(2)}) collective-permute-start(bf16[2,2,128,512]{3,2,0,1:T(8,128)(2,1)} %dynamic-slice_bitcast_fusion.1), channel_id=1, source_target_pairs={{0,2},{1,3},{2,0},{3,1},{4,6},{5,7},{6,4},{7,5},{8,10},{9,11},{10,... | collective-permute-start | bytes 1572872 | tf_op jit(solution)/shard_map/ppermute | solution.py:888
  368.6 12.0 %copy-start.3 = (bf16[2,2,2,128,512]{4,3,0,1,2:T(8,128)(2,1)S(1)}, bf16[2,2,2,128,512]{4,3,0,1,2:T(8,128)(2,1)}, u32[]{:S(2)}) copy-start(bf16[2,2,2,128,512]{4,3,0,1,2:T(8,128)(2,1)} %copy-done.2) | copy-start | bytes 3145732
  381.5 29.2 %collective-permute-start.5 = (bf16[2,256,512]{2,1,0:T(8,128)(2,1)S(1)}, bf16[2,256,512]{2,1,0:T(8,128)(2,1)S(1)}, u32[]{:S(2)}, u32[]{:S(2)}) collective-permute-start(bf16[2,256,512]{2,1,0:T(8,128)(2,1)S(1)} %fusion.11), channel_id=1, source_target_pairs={{0,8},{1,9},{2,10},{3,11},{4,12},{5,13},{6,14},{7,15},{8,0},{9,1},... | collective-permute-start | bytes 1572872 | tf_op jit(solution)/shard_map/ppermute | solution.py:888
  410.9 6.3 %copy-start.5 = (bf16[2,256,512]{2,1,0:T(8,128)(2,1)}, bf16[2,256,512]{2,1,0:T(8,128)(2,1)S(1)}, u32[]{:S(2)}) copy-start(bf16[2,256,512]{2,1,0:T(8,128)(2,1)S(1)} %fusion.4) | copy-start | bytes 1572868
  423.4 6.3 %collective-permute-start.6 = (bf16[16,208,512]{2,1,0:T(8,128)(2,1)}, bf16[16,208,512]{2,1,0:T(8,128)(2,1)S(1)}, u32[]{:S(2)}, u32[]{:S(2)}) collective-permute-start(bf16[16,208,512]{2,1,0:T(8,128)(2,1)} %get-tuple-element.195), channel_id=1, source_target_pairs={{0,1},{1,0},{2,3},{3,2},{4,5},{5,4},{6,7},{7,6},{8,9},{9,8},{10,11... | collective-permute-start | bytes 10223624 | tf_op jit(solution)/shard_map/ppermute | solution.py:888
  433.2 19.6 %collective-permute-start.9 = (bf16[2,2,2,96,512]{4,3,0,1,2:T(8,128)(2,1)S(1)}, bf16[2,2,2,96,512]{4,3,0,1,2:T(8,128)(2,1)S(1)}, u32[]{:S(2)}, u32[]{:S(2)}) collective-permute-start(bf16[2,2,2,96,512]{4,3,0,1,2:T(8,128)(2,1)S(1)} %bitcast.235), channel_id=1, source_target_pairs={{0,2},{1,3},{2,0},{3,1},{4,6},{5,7},{6,4},{7,5},{8,10},{9,11},{10,... | collective-permute-start | bytes 2359304 | tf_op jit(solution)/shard_map/ppermute | solution.py:888
  433.6 23.7 %collective-permute-start.7 = (bf16[2,2,2,112,512]{4,3,0,1,2:T(8,128)(2,1)S(1)}, bf16[2,2,2,112,512]{4,3,0,1,2:T(8,128)(2,1)S(1)}, u32[]{:S(2)}, u32[]{:S(2)}) collective-permute-start(bf16[2,2,2,112,512]{4,3,0,1,2:T(8,128)(2,1)S(1)} %bitcast.234), channel_id=1, source_target_pairs={{0,4},{1,5},{2,6},{3,7},{4,0},{5,1},{6,2},{7,3},{8,12},{9,13},{10,... | collective-permute-start | bytes 2752520 | tf_op jit(solution)/shard_map/ppermute | solution.py:888
  453.1 11.8 %collective-permute-start.10 = (bf16[2,2,96,512]{3,2,0,1:T(8,128)(2,1)S(1)}, bf16[2,2,96,512]{3,2,0,1:T(8,128)(2,1)S(1)}, u32[]{:S(2)}, u32[]{:S(2)}) collective-permute-start(bf16[2,2,96,512]{3,2,0,1:T(8,128)(2,1)S(1)} %dynamic-slice_bitcast_fusion.3), channel_id=1, source_target_pairs={{0,4},{1,5},{2,6},{3,7},{4,0},{5,1},{6,2},{7,3},{8,12},{9,13},{10,... | collective-permute-start | bytes 1179656 | tf_op jit(solution)/shard_map/ppermute | solution.py:888
  457.6 11.0 %collective-permute-start.8 = (bf16[2,2,112,512]{3,2,0,1:T(8,128)(2,1)S(1)}, bf16[2,2,112,512]{3,2,0,1:T(8,128)(2,1)S(1)}, u32[]{:S(2)}, u32[]{:S(2)}) collective-permute-start(bf16[2,2,112,512]{3,2,0,1:T(8,128)(2,1)S(1)} %dynamic-slice_bitcast_fusion.2), channel_id=1, source_target_pairs={{0,2},{1,3},{2,0},{3,1},{4,6},{5,7},{6,4},{7,5},{8,10},{9,11},{10,... | collective-permute-start | bytes 1376264 | tf_op jit(solution)/shard_map/ppermute | solution.py:888
  459.3 17.3 %collective-permute-start.13 = (bf16[256,512]{1,0:T(8,128)(2,1)S(1)}, bf16[256,512]{1,0:T(8,128)(2,1)}, u32[]{:S(2)}, u32[]{:S(2)}) collective-permute-start(bf16[256,512]{1,0:T(8,128)(2,1)S(1)} %dynamic-slice_bitcast_fusion.4), channel_id=1, source_target_pairs={{0,16},{1,17},{2,18},{3,19},{4,20},{5,21},{6,22},{7,23},{8,24},{9,... | collective-permute-start | bytes 786440 | tf_op jit(solution)/shard_map/ppermute | solution.py:888
  469.5 10.8 %collective-permute-start.11 = (bf16[2,208,512]{2,1,0:T(8,128)(2,1)}, bf16[2,208,512]{2,1,0:T(8,128)(2,1)}, u32[]{:S(2)}, u32[]{:S(2)}) collective-permute-start(bf16[2,208,512]{2,1,0:T(8,128)(2,1)} %fusion.15), channel_id=1, source_target_pairs={{0,8},{1,9},{2,10},{3,11},{4,12},{5,13},{6,14},{7,15},{8,0},{9,1},... | collective-permute-start | bytes 1277960 | tf_op jit(solution)/shard_map/ppermute | solution.py:888
  469.5 7.0 %copy-start.6 = (bf16[2,256,512]{2,1,0:T(8,128)(2,1)S(1)}, bf16[2,256,512]{2,1,0:T(8,128)(2,1)}, u32[]{:S(2)}) copy-start(bf16[2,256,512]{2,1,0:T(8,128)(2,1)} %copy-done.5) | copy-start | bytes 1572868
  478.1 3.7 copy-start.22
  478.1 3.7 copy-start.24
  479.7 2.2 copy-start.7
  479.7 2.2 copy-start.9
  479.7 2.2 copy-start.10
  481.4 10.5 %collective-permute-start.12 = (bf16[208,512]{1,0:T(8,128)(2,1)S(1)}, bf16[208,512]{1,0:T(8,128)(2,1)S(1)}, u32[]{:S(2)}, u32[]{:S(2)}) collective-permute-start(bf16[208,512]{1,0:T(8,128)(2,1)S(1)} %dynamic-slice_bitcast_fusion.5), channel_id=1, source_target_pairs={{0,16},{1,17},{2,18},{3,19},{4,20},{5,21},{6,22},{7,23},{8,24},{9,... | collective-permute-start | bytes 638984 | tf_op jit(solution)/shard_map/ppermute | solution.py:888
  492.0 1.1 copy-start.15
  492.0 1.1 copy-start.16
  492.0 1.7 copy-start.11
  492.0 1.7 copy-start.12
  492.1 1.7 copy-start.18
  492.1 1.7 copy-start.20
Sparse Core Ops, SparseCore 0:
  11.5 72.3 all-gather.2
  87.3 75.9 all-gather.4

commit v3 on v2

--- a/solution.py
+++ b/solution.py
@@ -24,7 +24,7 @@
 
 F32 = jnp.float32
 LOW = jnp.bfloat16
-VMEM_BYTES = 56 * 2**20
+MIB = 2**20
 
 
 def nn(former, latter):
@@ -63,17 +63,8 @@
 
 
 def phi_and_slope(values):
-    size = jnp.abs(values)
-    bell = jnp.exp(-0.5 * (values * values))
-    part = 1.0 / (1.0 + (0.3275911 * root_half) * size)
-    series = part * (
-        0.254829592
-        + part
-        * (-0.284496736 + part * (1.421413741 + part * (-1.453152027 + part * 1.061405429)))
-    )
-    half_tail = (0.5 * series) * bell
-    phi = jnp.where(values >= 0, 1.0 - half_tail, half_tail)
-    return phi, phi + values * (bell * inverse_root_tau)
+    phi = 0.5 + 0.5 * lax.erf(values * root_half)
+    return phi, phi + values * (jnp.exp(-0.5 * (values * values)) * inverse_root_tau)
 
 
 def one_head(pair, head):
@@ -90,21 +81,95 @@
     return slice(HEAD * head, HEAD * head + HEAD)
 
 
-def block_of(ref, j):
-    if len(ref.shape) == 4:
-        return ref[:, j].reshape(ref.shape[0] * ref.shape[2], ref.shape[3])
-    return ref[j]
+def block_of(ref, j, count):
+    if count == 1:
+        return ref[...]
+    return jnp.concatenate(
+        [ref[first + 16 * j : first + 16 * j + 16, :] for first in range(0, ref.shape[0], 16 * count)], axis=0
+    )
+
+
+def spread(wide, values):
+    for n in range(wide.shape[0]):
+        wide[n] = values[:, LANES * n : LANES * n + LANES].astype(F32)
+
+
+def third_rows(wide, j):
+    rows = pl.ds(j, wide.shape[1] // 3, stride=3)
+    return jnp.concatenate([wide[n, rows, :] for n in range(wide.shape[0])], axis=1).astype(LOW)
+
+
+def put_third_rows(wide, j, values):
+    rows = pl.ds(j, wide.shape[1] // 3, stride=3)
+    for n in range(wide.shape[0]):
+        wide[n, rows, :] = values[:, LANES * n : LANES * n + LANES]
+
+
+def wide_scratch(width):
+    return pltpu.VMEM((width // LANES, 3 * width, LANES), F32)
 
 
 def put_block(ref, j, values):
-    if len(ref.shape) == 4:
-        ref[:, j] = values.reshape(ref.shape[0], ref.shape[2], ref.shape[3])
-    else:
-        ref[j] = values
-
-
-def call(kernel, grid, in_specs, out_specs, out_shape, scratch, flops, moved, name):
-    return pl.pallas_call(
+    ref[:, j] = values.reshape(ref.shape[0], ref.shape[2], ref.shape[3])
+
+
+OWNERS = 32
+
+
+def row_copies(first, last, own, base):
+    found = []
+    at = first
+    while at < last:
+        owner = at // own
+        end = min(last, (owner + 1) * own)
+        found.append((owner, base + at - owner * own, end - at, at - first))
+        at = end
+    return found
+
+
+class Fetch:
+    def __init__(self, far, copies, near, semaphores, used):
+        self.handles = [
+            pltpu.make_async_copy(
+                far.at[owner, pl.ds(row, rows)], near.at[pl.ds(to, rows)], semaphores.at[used + n]
+            )
+            for n, (owner, row, rows, to) in enumerate(copies)
+        ]
+
+    def start(self):
+        for handle in self.handles:
+            handle.start()
+
+    def wait(self):
+        for handle in self.handles:
+            handle.wait()
+
+
+def fetches(far, wanted, nears, semaphores):
+    used = 0
+    made = []
+    for copies, near in zip(wanted, nears):
+        made.append(Fetch(far, copies, near, semaphores, used))
+        used += len(copies)
+    return made
+
+
+def fetch_scratch(wanted, width):
+    return [pltpu.VMEM((sum(c[2] for c in copies), width), LOW) for copies in wanted] + [
+        pltpu.SemaphoreType.DMA((sum(len(copies) for copies in wanted),))
+    ]
+
+
+FAR = pl.BlockSpec(memory_space=pl.ANY)
+
+
+def call(kernel, grid, in_specs, out_specs, out_shape, scratch, flops, moved, name, room=24, near=(), keep=()):
+    single = not isinstance(out_shape, list)
+    shapes = [
+        (pltpu.VMEM if keep is True or n in keep else pltpu.HBM)(*made)
+        for n, made in enumerate([out_shape] if single else out_shape)
+    ]
+    made = pl.pallas_call(
         kernel,
         grid_spec=pltpu.PrefetchScalarGridSpec(
             num_scalar_prefetch=1,
@@ -113,14 +178,25 @@
             out_specs=out_specs,
             scratch_shapes=scratch,
         ),
-        out_shape=out_shape,
-        compiler_params=pltpu.CompilerParams(vmem_limit_bytes=VMEM_BYTES),
+        out_shape=shapes[0] if single else shapes,
+        compiler_params=pltpu.CompilerParams(vmem_limit_bytes=room * MIB),
         cost_estimate=pl.CostEstimate(
             flops=flops, bytes_accessed=moved, transcendentals=0
         ),
         name=name,
     )
 
+    def run(plan, *operands):
+        placed = [
+            operand
+            if near is True or n in near
+            else pltpu.with_memory_space_constraint(operand, pltpu.HBM)
+            for n, operand in enumerate(operands)
+        ]
+        return made(plan, *placed)
+
+    return run
+
 
 def whole(shape):
     zeros = (0,) * len(shape)
@@ -136,7 +212,7 @@
 
 
 def shaped(shape, kind):
-    return jax.ShapeDtypeStruct(shape, kind)
+    return (shape, kind)
 
 
 def attend_tile(plan, i, keys, key_cols, query, owner_row, key_owner, vt, sc):
@@ -177,34 +253,48 @@
     lax.fori_loop(lo, hi, weigh_tile, 0)
 
 
-def fwd_block_kernel(plan, *refs, cross, gain_row):
+def fwd_block_kernel(plan, *refs, cross, gain_row, wanted, packed, ffn):
+    refs = list(refs)
+
+    def next_refs(count):
+        taken = refs[:count]
+        del refs[:count]
+        return taken
+
     if cross:
-        (normed_in, memory, wq, wk_a, wk_b, wo, small, owner_q, owner_k,
-         q_out, kv_out, ctx_out, lse_out, normed_out, inverse_out,
-         kv, vt, mean_v, key_owner, scores, acc, top, total, masked_q) = refs
+        normed_in, memory, far, small, owner_q, owner_k = next_refs(6)
     else:
-        (x_all, wqkv, wo, small, owner_q, owner_k,
-         q_out, kv_out, ctx_out, lse_out, normed_out, inverse_out,
-         kv, vt, mean_v, key_owner, scores, acc, top, total, masked_q, q_all) = refs
+        x_all, far, small, owner_q, owner_k = next_refs(5)
+    q_out, kv_out, ctx_out, lse_out, normed_out, inverse_out = next_refs(6)
+    if ffn:
+        out, normed_last, inverse_last = next_refs(3)
+    kv, vt, mean_v, key_owner, scores, acc, top, total, masked_q, q_all = next_refs(10)
+    nears = next_refs(len(wanted))
+    semaphores = refs.pop(0)
+    loads = fetches(far, wanted, nears, semaphores)
     i = pl.program_id(0)
     width = kv.shape[1] // 2
 
     @pl.when(i == 0)
     def _():
+        for load in loads:
+            load.start()
         key_owner[...] = jnp.broadcast_to(owner_k[...], (8, owner_k.shape[1])).T
+        loads[0].wait()
         if cross:
-            wk = jnp.concatenate([block_of(wk_a, 0), block_of(wk_b, 0)], axis=0)
-            wv = jnp.concatenate([block_of(wk_a, 1), block_of(wk_b, 1)], axis=0)
+            wk, wv = block_of(nears[0], 0, 2), block_of(nears[0], 1, 2)
+        elif packed:
+            wq, wk, wv = (block_of(nears[0], j, 3) for j in range(3))
         else:
-            wq_all = block_of(wqkv, 0)
-            wk = block_of(wqkv, 1)
-            wv = block_of(wqkv, 2)
+            wide = refs[0]
+            spread(wide, nears[0][...])
+            wq, wk, wv = (third_rows(wide, j) for j in range(3))
         sums = jnp.zeros((1, width), F32)
         for t in range(kv.shape[0] // TILE):
             rows = slice(t * TILE, t * TILE + TILE)
             x = memory[rows, :] if cross else x_all[rows, :]
             if not cross:
-                q_all[rows, :] = nn(x, wq_all).astype(LOW)
+                q_all[rows, :] = nn(x, wq).astype(LOW)
             kv[rows, :width] = nn(x, wk).astype(LOW)
             v = nn(x, wv).astype(LOW)
             kv[rows, width:] = v
@@ -212,11 +302,14 @@
             vt[:, rows] = v.T.astype(LOW)
             sums = sums + jnp.sum(v, axis=0, keepdims=True)
         mean_v[...] = sums * (1.0 / kv.shape[0])
-
+        for load in loads[1:]:
+            load.wait()
+
+    wo = nears[1]
     mine = pl.ds(pl.multiple_of(i * TILE, TILE), TILE)
     if cross:
         resid = normed_in[...] * small[4:5, :] + small[5:6, :]
-        query = nn(resid.astype(LOW), wq[...]).astype(LOW)
+        query = nn(resid.astype(LOW), nears[2][...]).astype(LOW)
         q_out[...] = query
     else:
         resid = x_all[mine, :].astype(F32)
@@ -235,11 +328,26 @@
     context = jnp.where(live, acc[...].T, mean_v[...]).astype(LOW)
     ctx_out[...] = context
     added = nn(context, wo[...]) * live.astype(F32)
-    _, normed, inverse = ln_forward(
+    mid, normed, inverse = ln_forward(
         resid + added, small[gain_row : gain_row + 1, :], small[gain_row + 1 : gain_row + 2, :]
     )
     normed_out[...] = normed
     inverse_out[...] = jnp.broadcast_to(inverse, inverse_out.shape)
+    if ffn:
+        wup, wdown = nears[-2:]
+        blocks = wdown.shape[0] // width
+        low = mid.astype(LOW)
+        result = mid
+        for j in range(blocks):
+            inner = nn(low, block_of(wup, j, blocks))
+            phi = 0.5 + 0.5 * lax.erf(inner * root_half)
+            result = result + nn((inner * phi).astype(LOW), wdown[j * width : j * width + width, :])
+        result, normed, inverse = ln_forward(
+            result, small[gain_row + 2 : gain_row + 3, :], small[gain_row + 3 : gain_row + 4, :]
+        )
+        out[...] = result.astype(LOW)
+        normed_last[...] = normed
+        inverse_last[...] = jnp.broadcast_to(inverse, inverse_last.shape)
 
 
 def attention_scratch(keys, width):
@@ -253,6 +361,7 @@
         pltpu.VMEM((HEADS, TILE), F32),
         pltpu.VMEM((HEADS, TILE), F32),
         pltpu.VMEM((HEADS, TILE, LANES), LOW),
+        pltpu.VMEM((keys, width), LOW),
     ]
 
 
@@ -280,203 +389,143 @@
     return [pl.BlockSpec((1, TILE), lambda i, *_: (0, i)), whole((1, keys))]
 
 
-def self_block(plan, x, wqkv, wqkv_spec, wo, wo_spec, small, gain_row, owner, key_owner, name):
+def fwd_block(plan, x, memory, far, wanted, packed, small, gain_row, owner, key_owner, ffn, name):
+    cross = memory is not None
     number, width = x.shape
     specs, shapes = block_outs(number, width)
+    if ffn:
+        specs += [rows_of(width), rows_of(width), rows_of(LANES)]
+        shapes += [shaped((number, width), LOW), shaped((number, width), F32), shaped((number, LANES), F32)]
+    scratch = attention_scratch(number, width) + fetch_scratch(wanted, width)
+    if not cross and not packed:
+        scratch.append(wide_scratch(width))
     return call(
-        functools.partial(fwd_block_kernel, cross=False, gain_row=gain_row),
+        functools.partial(
+            fwd_block_kernel, cross=cross, gain_row=gain_row, wanted=wanted, packed=packed, ffn=ffn
+        ),
         (number // TILE,),
-        [whole(x.shape), wqkv_spec, wo_spec, whole(small.shape)] + owner_specs(number),
+        ([rows_of(width), whole(memory.shape)] if cross else [whole(x.shape)])
+        + [FAR, whole(small.shape)]
+        + owner_specs(number),
         specs,
         shapes,
-        attention_scratch(number, width) + [pltpu.VMEM((number, width), LOW)],
+        scratch,
         8 * number * width * width + number * number * width * 2,
         16 * number * width,
         name,
-    )(plan, x, wqkv, wo, small, owner, key_owner)
-
-
-def cross_block(plan, normed, memory, dec_rows, wk_two, small, owner, key_owner):
-    number, width = normed.shape
-    specs, shapes = block_outs(number, width)
-    half = (width // 32, 2, 16, width)
-    return call(
-        functools.partial(fwd_block_kernel, cross=True, gain_row=6),
-        (number // TILE,),
-        [
-            rows_of(width),
-            whole(memory.shape),
-            at_block((width, width), 4, 0),
-            at_block(half, 5, 0, 0, 0),
-            at_block(half, 6, 0, 0, 0),
-            at_block((width, width), 7, 0),
-            whole(small.shape),
-        ]
-        + owner_specs(number),
-        specs,
-        shapes,
-        attention_scratch(number, width),
-        8 * number * width * width + number * number * width * 2,
-        16 * number * width,
-        "cross_block",
-    )(plan, normed, memory, dec_rows, wk_two, wk_two, dec_rows, small, owner, key_owner)
-
-
-def ffn_kernel(plan, normed, wup, wdown, small, hidden, slope, out, normed_out, inverse_out, *, mid_row, top_row):
-    mid = normed[...] * small[mid_row : mid_row + 1, :] + small[mid_row + 1 : mid_row + 2, :]
-    low = mid.astype(LOW)
-    width = mid.shape[1]
-    total = mid
-    for j in range(hidden.shape[1] // width):
-        cols = slice(j * width, j * width + width)
-        inner = nn(low, block_of(wup, j))
-        phi, tilt = phi_and_slope(inner)
-        made = (inner * phi).astype(LOW)
-        hidden[:, cols] = made
-        slope[:, cols] = tilt.astype(LOW)
-        total = total + nn(made, wdown[cols, :])
-    result, normed_two, inverse = ln_forward(
-        total, small[top_row : top_row + 1, :], small[top_row + 1 : top_row + 2, :]
-    )
-    out[...] = result.astype(LOW)
-    normed_out[...] = normed_two
-    inverse_out[...] = jnp.broadcast_to(inverse, inverse_out.shape)
-
-
-def ffn_forward(plan, normed, wup, wup_spec, wdown, wdown_spec, small, mid_row, top_row, inner, name):
-    number, width = normed.shape
-    return call(
-        functools.partial(ffn_kernel, mid_row=mid_row, top_row=top_row),
-        (number // TILE,),
-        [rows_of(width), wup_spec, wdown_spec, whole(small.shape)],
-        [rows_of(inner), rows_of(inner), rows_of(width), rows_of(width), rows_of(LANES)],
-        [
-            shaped((number, inner), LOW),
-            shaped((number, inner), LOW),
-            shaped((number, width), LOW),
-            shaped((number, width), F32),
-            shaped((number, LANES), F32),
-        ],
-        [],
-        4 * number * width * inner,
-        20 * number * width,
-        name,
-    )(plan, normed, wup, wdown, small)
-
-
-def ffn_back_kernel(plan, *refs, summed, mid_row, top_row):
-    if summed:
-        (cot, extra, normed_top, inverse_top, slope, normed_mid, inverse_mid, wup, wdown, wo, small,
-         d_inner, d_down, d_sum, d_product, d_context, sums) = refs
-    else:
-        (cot, normed_top, inverse_top, slope, normed_mid, inverse_mid, wup, wdown, wo, small,
-         d_inner, d_down, d_sum, d_product, d_context, sums) = refs
+        room=44,
+    )(plan, *([x, memory] if cross else [x]), far, small, owner, key_owner)
+
+
+def ffn_back_kernel(plan, *refs, tiles, summed, gain_row, wanted):
+    refs = list(refs)
+    cot = refs.pop(0)
+    extra = refs.pop(0) if summed else None
+    (normed_top, inverse_top, normed_mid, inverse_mid, context, far, small,
+     d_sum, d_context, g_up, g_down, g_out, sums, hidden, d_inner, mid_low, d_down, d_product,
+     wup, wdown, wo, semaphores) = refs
+    loads = fetches(far, wanted, (wup, wdown, wo), semaphores)
     i = pl.program_id(0)
+    width = small.shape[1]
+    blocks = wdown.shape[0] // width
 
     @pl.when(i == 0)
     def _():
+        for load in loads:
+            load.start()
         sums[...] = jnp.zeros_like(sums)
-
-    upstream = cot[...].astype(F32)
-    if summed:
-        upstream = upstream + extra[...]
-    width = upstream.shape[1]
-    top = normed_top[...]
-    sums[2:3, :] += jnp.sum(upstream * top, axis=0, keepdims=True)
-    sums[3:4, :] += jnp.sum(upstream, axis=0, keepdims=True)
-    d_top = ln_backward(upstream, top, inverse_top[:, 0:1], small[top_row : top_row + 1, :])
-    low = d_top.astype(LOW)
-    d_down[...] = low
-    d_mid = d_top
-    for j in range(slope.shape[1] // width):
-        cols = slice(j * width, j * width + width)
-        part = (nt(low, wdown[cols, :]) * slope[:, cols].astype(F32)).astype(LOW)
-        d_inner[:, cols] = part
-        d_mid = d_mid + nt(part, block_of(wup, j))
-    normed = normed_mid[...]
-    sums[0:1, :] += jnp.sum(d_mid * normed, axis=0, keepdims=True)
-    sums[1:2, :] += jnp.sum(d_mid, axis=0, keepdims=True)
-    total = ln_backward(d_mid, normed, inverse_mid[:, 0:1], small[mid_row : mid_row + 1, :])
-    d_sum[...] = total
-    place = lax.broadcasted_iota(jnp.int32, (TILE, 1), 0) + i * TILE
-    live = (place < plan[2, 0]).astype(F32)
-    product = (total * live).astype(LOW)
-    d_product[...] = product
-    d_context[...] = nt(product, wo[...]).astype(LOW)
-
-
-def ffn_backward(plan, cots, top, slope, mid, weights, weight_specs, small, mid_row, top_row, name):
+        for load in loads:
+            load.wait()
+
+    @pl.when(i < tiles)
+    def _():
+        mine = pl.ds(pl.multiple_of(i * TILE, TILE), TILE)
+        upstream = cot[...].astype(F32)
+        if summed:
+            upstream = upstream + extra[...]
+        top = normed_top[...]
+        sums[2:3, :] += jnp.sum(upstream * top, axis=0, keepdims=True)
+        sums[3:4, :] += jnp.sum(upstream, axis=0, keepdims=True)
+        d_mid = ln_backward(upstream, top, inverse_top[:, 0:1], small[gain_row + 2 : gain_row + 3, :])
+        low = d_mid.astype(LOW)
+        d_down[mine, :] = low
+        normed = normed_mid[...]
+        mid = (normed * small[gain_row : gain_row + 1, :] + small[gain_row + 1 : gain_row + 2, :]).astype(LOW)
+        mid_low[mine, :] = mid
+        for j in range(blocks):
+            cols = slice(j * width, j * width + width)
+            up = block_of(wup, j, blocks)
+            inner = nn(mid, up)
+            phi, slope = phi_and_slope(inner)
+            hidden[j, mine, :] = (inner * phi).astype(LOW)
+            part = (nt(low, wdown[cols, :]) * slope).astype(LOW)
+            d_inner[j, mine, :] = part
+            d_mid = d_mid + nt(part, up)
+        sums[0:1, :] += jnp.sum(d_mid * normed, axis=0, keepdims=True)
+        sums[1:2, :] += jnp.sum(d_mid, axis=0, keepdims=True)
+        total = ln_backward(d_mid, normed, inverse_mid[:, 0:1], small[gain_row : gain_row + 1, :])
+        d_sum[...] = total
+        place = lax.broadcasted_iota(jnp.int32, (TILE, 1), 0) + i * TILE
+        live = (place < plan[2, 0]).astype(F32)
+        product = (total * live).astype(LOW)
+        d_product[mine, :] = product
+        d_context[...] = nt(product, wo[...]).astype(LOW)
+
+    @pl.when(i >= tiles)
+    def _():
+        j = i - tiles
+        put_block(g_up, 0, nn(turned(mid_low[...]), d_inner[j]).astype(LOW))
+        g_down[...] = nn(turned(hidden[j]), d_down[...]).astype(LOW)
+
+    @pl.when(i == tiles)
+    def _():
+        g_out[...] = nn(turned(context[...]), d_product[...]).astype(LOW)
+
+
+def ffn_backward(plan, cots, top, mid, context, far, wanted, small, gain_row, inner, name):
     number, width = mid[0].shape
-    inner = slope.shape[1]
+    tiles, blocks = number // TILE, inner // width
+
+    def tile_of(columns):
+        return pl.BlockSpec((TILE, columns), lambda i, *_: (jnp.minimum(i, tiles - 1), 0))
+
     return call(
         functools.partial(
-            ffn_back_kernel, summed=len(cots) == 2, mid_row=mid_row, top_row=top_row
+            ffn_back_kernel, tiles=tiles, summed=len(cots) == 2, gain_row=gain_row, wanted=wanted
         ),
-        (number // TILE,),
-        [rows_of(width)] * len(cots)
-        + [rows_of(width), rows_of(LANES), rows_of(inner), rows_of(width), rows_of(LANES)]
-        + weight_specs
-        + [whole(small.shape)],
+        (tiles + blocks,),
+        [tile_of(width)] * len(cots)
+        + [tile_of(width), tile_of(LANES), tile_of(width), tile_of(LANES), whole((number, width))]
+        + [FAR, whole(small.shape)],
         [
-            rows_of(inner),
-            rows_of(width),
-            rows_of(width),
-            rows_of(width),
-            rows_of(width),
-            whole((8, width)),
+            tile_of(width),
+            tile_of(width),
+            pl.BlockSpec((width // 16, 1, 16, width), lambda i, *_: (0, jnp.maximum(i - tiles, 0), 0, 0)),
+            pl.BlockSpec((width, width), lambda i, *_: (jnp.maximum(i - tiles, 0), 0)),
+            pl.BlockSpec((width, width), lambda i, *_: (0, 0)),
+            pl.BlockSpec((8, width), lambda i, *_: (0, 0)),
         ],
         [
-            shaped((number, inner), LOW),
-            shaped((number, width), LOW),
             shaped((number, width), F32),
             shaped((number, width), LOW),
-            shaped((number, width), LOW),
+            shaped((width // 16, blocks, 16, width), LOW),
+            shaped((inner, width), LOW),
+            shaped((width, width), LOW),
             shaped((8, width), F32),
         ],
-        [],
-        4 * number * width * inner,
-        26 * number * width,
+        [
+            pltpu.VMEM((blocks, number, width), LOW),
+            pltpu.VMEM((blocks, number, width), LOW),
+            pltpu.VMEM((number, width), LOW),
+            pltpu.VMEM((number, width), LOW),
+            pltpu.VMEM((number, width), LOW),
+        ]
+        + fetch_scratch(wanted, width),
+        10 * number * width * inner,
+        30 * number * width,
         name,
-    )(plan, *cots, *top, slope, *mid, *weights, small)
-
-
-def ffn_weights_kernel(plan, normed, d_inner, d_down, hidden, context, d_product, small, up, down, wo, turn, *, mid_row):
-    i = pl.program_id(0)
-
-    @pl.when(i == 0)
-    def _():
-        mid = normed[...] * small[mid_row : mid_row + 1, :] + small[mid_row + 1 : mid_row + 2, :]
-        turn[...] = mid.T.astype(LOW)
-        wo[...] = nn(turned(context[...]), d_product[...]).astype(LOW)
-
-    put_block(up, 0, nn(turn[...], d_inner[...]).astype(LOW))
-    down[...] = nn(turned(hidden[...]), d_down[...]).astype(LOW)
-
-
-def ffn_weights(plan, normed, d_inner, d_down, hidden, context, d_product, small, mid_row, name):
-    number, width = normed.shape
-    blocks = d_inner.shape[1] // width
-    full = whole((number, width))
-    column = pl.BlockSpec((number, width), lambda i, *_: (0, i))
-    return call(
-        functools.partial(ffn_weights_kernel, mid_row=mid_row),
-        (blocks,),
-        [full, column, full, column, full, full, whole(small.shape)],
-        [
-            pl.BlockSpec((width // 16, 1, 16, width), lambda i, *_: (0, i, 0, 0)),
-            pl.BlockSpec((width, width), lambda i, *_: (i, 0)),
-            whole((width, width)),
-        ],
-        [
-            shaped((width // 16, blocks, 16, width), LOW),
-            shaped((blocks * width, width), LOW),
-            shaped((width, width), LOW),
-        ],
-        [pltpu.VMEM((width, number), LOW)],
-        4 * number * width * width * blocks,
-        24 * number * width,
-        name,
-    )(plan, normed, d_inner, d_down, hidden, context, d_product, small)
+        room=44,
+    )(plan, *cots, *top, *mid, context, far, small)
 
 
 def attention_back_kernel(plan, q_ref, k_ref, v_ref, do_ref, lse, owner_q, owner_k, dq, dk, dv,
@@ -573,22 +622,29 @@
         number * keys * width * 4,
         12 * number * width,
         name,
+        room=44,
     )(plan, q, kv, kv, d_context, lse, owner, key_owner)
 
 
-def cross_back_kernel(plan, d_query, dk, dv, normed, inverse, d_above, memory, context, wq, wk_a, wk_b, wo, small,
-                      d_memory, d_sum, d_context, g_query, g_pair, g_out, sums, d_product):
+def cross_back_kernel(plan, d_query, dk, dv, normed, inverse, d_above, memory, context, far, small,
+                      d_memory, d_sum, d_context, g_query, g_pair, g_out, sums, d_product, wkv, wq, wo, semaphores,
+                      *, wanted):
     i = pl.program_id(0)
     mine = pl.ds(pl.multiple_of(i * TILE, TILE), TILE)
 
+    loads = fetches(far, wanted, (wkv, wq, wo), semaphores)
+
     @pl.when(i == 0)
     def _():
+        for load in loads:
+            load.start()
         sums[...] = jnp.zeros_like(sums)
         low = normed[...] * small[4:5, :] + small[5:6, :]
         g_query[...] = nn(low.T.astype(LOW), d_query[...]).astype(LOW)
-
-    wk = jnp.concatenate([block_of(wk_a, 0), block_of(wk_b, 0)], axis=0)
-    wv = jnp.concatenate([block_of(wk_a, 1), block_of(wk_b, 1)], axis=0)
+        for load in loads:
+            load.wait()
+
+    wk, wv = block_of(wkv, 0, 2), block_of(wkv, 1, 2)
     d_memory[...] = nt(dk[mine, :], wk) + nt(dv[mine, :], wv)
     d_one = d_above[...] + nt(d_query[mine, :], wq[...])
     hat = normed[mine, :]
@@ -617,31 +673,29 @@
         g_out[...] = nn(turned(context[...]), d_product[...]).astype(LOW)
 
 
-def cross_projections_back(plan, d_query, dk, dv, normed, inverse, d_above, memory, context, dec_rows, wk_two, small):
+def cross_projections_back(plan, d_query, dk, dv, normed, inverse, d_above, memory, context, far, wanted, small):
     number, width = normed.shape
     full = whole((number, width))
     square = whole((width, width))
-    half = (width // 32, 2, 16, width)
     return call(
-        cross_back_kernel,
+        functools.partial(cross_back_kernel, wanted=wanted),
         (number // TILE,),
-        [full, full, full, full, rows_of(LANES), rows_of(width), full, full,
-         at_block((width, width), 4, 0), at_block(half, 5, 0, 0, 0), at_block(half, 6, 0, 0, 0),
-         at_block((width, width), 3, 0), whole(small.shape)],
+        [full, full, full, full, rows_of(LANES), rows_of(width), full, full, FAR, whole(small.shape)],
         [rows_of(width), rows_of(width), rows_of(width), square, whole((width // 16, 2, 16, width)), square,
          whole((8, width))],
         [shaped((number, width), F32), shaped((number, width), F32), shaped((number, width), LOW),
          shaped((width, width), LOW), shaped((width // 16, 2, 16, width), LOW), shaped((width, width), LOW),
          shaped((8, width), F32)],
-        [pltpu.VMEM((number, width), LOW)],
+        [pltpu.VMEM((number, width), LOW)] + fetch_scratch(wanted, width),
         16 * number * width * width,
         24 * number * width,
         "cross_projections_back",
-    )(plan, d_query, dk, dv, normed, inverse, d_above, memory, context, dec_rows, wk_two, wk_two, dec_rows, small)
-
-
-def qkv_weights_kernel(plan, x, dq, dk, dv, g_qkv, turn):
+    )(plan, d_query, dk, dv, normed, inverse, d_above, memory, context, far, small)
+
+
+def qkv_weights_kernel(plan, x, dq, dk, dv, g_qkv, turn, *wide):
     i = pl.program_id(0)
+    width = turn.shape[0]
 
     @pl.when(i == 0)
     def _():
@@ -650,47 +704,70 @@
     for j, ref in enumerate((dq, dk, dv)):
 
         @pl.when(i == j)
-        def _(ref=ref):
-            put_block(g_qkv, 0, nn(turn[...], ref[...]).astype(LOW))
-
-
-def qkv_weights(plan, x, dq, dk, dv, units, name):
+        def _(j=j, ref=ref):
+            made = nn(turn[...], ref[...])
+            if not wide:
+                put_block(g_qkv, 0, made.astype(LOW))
+            else:
+                put_third_rows(wide[0], j, made)
+
+    if wide:
+
+        @pl.when(i == 2)
+        def _():
+            for n in range(width // LANES):
+                g_qkv[:, LANES * n : LANES * n + LANES] = wide[0][n].astype(LOW)
+
+
+def qkv_weights(plan, x, dq, dk, dv, packed, name):
     number, width = x.shape
     full = whole((number, width))
-    if units:
+    scratch = [pltpu.VMEM((width, number), LOW)]
+    if packed:
         shape = (width // 16, 3, 16, width)
         spec = pl.BlockSpec((width // 16, 1, 16, width), lambda i, *_: (0, i, 0, 0))
     else:
-        shape = (3, width, width)
-        spec = pl.BlockSpec((1, width, width), lambda i, *_: (i, 0, 0))
+        shape = (3 * width, width)
+        spec = whole(shape)
+        scratch.append(wide_scratch(width))
     return call(
         qkv_weights_kernel,
         (3,),
         [full] * 4,
         spec,
         shaped(shape, LOW),
-        [pltpu.VMEM((width, number), LOW)],
+        scratch,
         6 * number * width * width,
         12 * number * width,
         name,
     )(plan, x, dq, dk, dv)
 
 
-def qkv_inputs_kernel(plan, *refs, masked):
+def qkv_inputs_kernel(plan, *refs, masked, wanted):
     if masked:
-        dq, dk, dv, d_above, wqkv, flags, d_x, mask_sum = refs
+        dq, dk, dv, d_above, far, flags, d_x, mask_sum, near, semaphores, blocks, wide = refs
     else:
-        dq, dk, dv, d_above, wqkv, d_x = refs
+        dq, dk, dv, d_above, far, d_x, near, semaphores, blocks = refs
+    width = dq.shape[1]
+
+    @pl.when(pl.program_id(0) == 0)
+    def _():
+        (load,) = fetches(far, wanted, (near,), semaphores)
+        load.start()
+        load.wait()
+        if masked:
+            mask_sum[...] = jnp.zeros_like(mask_sum)
+            spread(wide, near[...])
+        for j in range(3):
+            if masked:
+                blocks[:, j * width : j * width + width] = third_rows(wide, j)
+            else:
+                blocks[:, j * width : j * width + width] = block_of(near, j, 3)
+
     pieces = jnp.concatenate([dq[...], dk[...], dv[...]], axis=1)
-    weights = jnp.concatenate([block_of(wqkv, j) for j in range(3)], axis=1)
-    total = nt(pieces, weights)
+    total = nt(pieces, blocks[...])
     if masked:
         total = total + d_above[...]
-
-        @pl.when(pl.program_id(0) == 0)
-        def _():
-            mask_sum[...] = jnp.zeros_like(mask_sum)
-
         hit = column_of(flags[...]) == 1.0
         d_x[...] = jnp.where(hit, 0.0, total)
         mask_sum[0:1, :] += jnp.sum(jnp.where(hit, total, 0.0), axis=0, keepdims=True)
@@ -699,25 +776,27 @@
         d_x[...] += total
 
 
-def qkv_inputs(plan, dq, dk, dv, d_above, wqkv, wqkv_spec, flags, name):
+def qkv_inputs(plan, dq, dk, dv, d_above, far, wanted, flags, name):
     number, width = dq.shape
     masked = flags is not None
-    in_specs = [rows_of(width)] * 4 + [wqkv_spec]
+    in_specs = [rows_of(width)] * 4 + [FAR]
     out_specs = [rows_of(width)]
     out_shape = [shaped((number, width), F32)]
-    operands = [dq, dk, dv, d_above, wqkv]
+    operands = [dq, dk, dv, d_above, far]
+    scratch = fetch_scratch(wanted, width) + [pltpu.VMEM((width, 3 * width), LOW)]
     if masked:
         in_specs.append(pl.BlockSpec((1, TILE), lambda i, *_: (0, i)))
         out_specs.append(whole((8, width)))
         out_shape.append(shaped((8, width), F32))
         operands.append(flags)
+        scratch.append(wide_scratch(width))
     return call(
-        functools.partial(qkv_inputs_kernel, masked=masked),
+        functools.partial(qkv_inputs_kernel, masked=masked, wanted=wanted),
         (number // TILE,),
         in_specs,
         out_specs,
         out_shape,
-        [],
+        scratch,
         6 * number * width * width,
         16 * number * width,
         name,
@@ -870,13 +949,14 @@
     return call(
         functools.partial(pack_kernel, copies=copies, number=len(pieces)),
         (1,),
-        [whole(piece.shape) for piece in pieces],
+        [pl.BlockSpec(memory_space=pltpu.VMEM)] * len(pieces),
         [anywhere, anywhere],
         [shape, shape],
         [pltpu.SemaphoreType.DMA((len(copies),))],
         0,
         4 * total,
         name,
+        near=True,
     )(core, *pieces)
 
 
@@ -960,9 +1040,38 @@
 
     enc_own = arrange_own(enc_master.astype(LOW), me * enc_size, enc_map, to_units)
     dec_own = arrange_own(dec_master.astype(LOW), me * dec_size, dec_map, to_units)
-    enc_rows = lax.all_gather(enc_own, "fsdp", axis=0, tiled=True)
-    dec_rows = lax.all_gather(dec_own, "fsdp", axis=0, tiled=True)
-    small_rows = lax.all_gather(small_master.astype(LOW), "fsdp", axis=1, tiled=True)
+    by_rounds = devices == 1 << BITS
+    share = small_master.shape[1]
+    held = small_master.size
+    own = jnp.pad(small_master.astype(LOW).reshape(-1), (0, 16 * width - held)).reshape(16, width)
+    far = lax.all_gather(jnp.concatenate([enc_own, dec_own, own], axis=0), "fsdp", axis=0, tiled=False)
+    small_rows = far[:, enc_size + dec_size, :held].reshape(devices, -1, share)
+    small_rows = small_rows.transpose(1, 0, 2).reshape(-1, width)
+    if devices != OWNERS:
+        enc_rows = arrange_all(far[:, :enc_size].reshape(-1, width), enc_size, enc_map, to_units)
+        dec_rows = arrange_all(far[:, enc_size : enc_size + dec_size].reshape(-1, width), dec_size, dec_map, to_units)
+        far = jnp.concatenate(
+            [enc_rows.reshape(OWNERS, -1, width), dec_rows.reshape(OWNERS, -1, width)], axis=1
+        )
+    enc_share, dec_share = enc_count // OWNERS, dec_count // OWNERS
+
+    def enc_part(first, last):
+        return row_copies(first, last, enc_share, 0)
+
+    def dec_part(first, last):
+        return row_copies(first, last, dec_share, enc_share)
+
+    enc_qkv = enc_part(0, 3 * width)
+    enc_wo = enc_part(3 * width, 4 * width)
+    enc_up = enc_part(4 * width, 4 * width + inner)
+    enc_down = enc_part(4 * width + inner, enc_count)
+    self_qkv = dec_part(0, 3 * width)
+    self_wo = dec_part(3 * width, 4 * width)
+    cross_q = dec_part(4 * width, 5 * width)
+    cross_kv = dec_part(5 * width, 7 * width)
+    cross_wo = dec_part(7 * width, 8 * width)
+    dec_up = dec_part(8 * width, 8 * width + inner)
+    dec_down = dec_part(8 * width + inner, dec_count)
 
     src_owner, src_key, src_bounds = owners_of(src_len[0], number)
     tgt_owner, tgt_key, tgt_bounds = owners_of(tgt_len[0], number)
@@ -975,53 +1084,30 @@
     start = jnp.where(masked, small_rows[10][None, :], tgt_in)
     flags = tgt_mask.astype(F32)[None, :]
 
-    enc_rows = arrange_all(enc_rows, enc_size, enc_map, to_units)
-    dec_rows = arrange_all(dec_rows, dec_size, dec_map, to_units)
-    enc_three = enc_rows.reshape(-1, 3, 16, width)
-    enc_four = enc_rows.reshape(-1, ups, 16, width)
-    dec_two = dec_rows.reshape(-1, 2, 16, width)
-    dec_four = dec_rows.reshape(-1, ups, 16, width)
-    dec_three = dec_rows[: 3 * width].reshape(width, 3, width).transpose(1, 0, 2)
-    units = width // 16
-    three_spec = at_block((units, 3, 16, width), 0, 0, 0, 0)
-    enc_up = at_block((units, ups, 16, width), 1, 0, 0, 0)
-    enc_down = at_block((inner, width), 2, 0)
-    enc_wo = at_block((width, width), 3, 0)
-    dec_up = at_block((units, ups, 16, width), 2, 0, 0, 0)
-    dec_down = at_block((inner, width), 3, 0)
-
-    e_q, e_kv, e_ctx, e_lse, e_hat, e_inv = self_block(
-        enc_plan, src_in, enc_three, three_spec, enc_rows, enc_wo, smalls, 0, src_owner, src_key, "enc_block"
-    )
-    e_hidden, e_slope, memory, t_hat, t_inv = ffn_forward(
-        enc_plan, e_hat, enc_four, enc_up, enc_rows, enc_down, smalls, 0, 2, inner, "enc_ffn"
-    )
-    s_q, s_kv, s_ctx, s_lse, s_hat, s_inv = self_block(
-        dec_plan, start, dec_three, whole(dec_three.shape), dec_rows, at_block((width, width), 3, 0), smalls, 4,
-        tgt_owner, tgt_key, "dec_block",
-    )
-    c_q, c_kv, c_ctx, c_lse, c_hat, c_inv = cross_block(
-        cross_plan, s_hat, memory, dec_rows, dec_two, smalls, tgt_owner, src_key
-    )
-    d_hidden, d_slope, decoded, f_hat, f_inv = ffn_forward(
-        dec_plan, c_hat, dec_four, dec_up, dec_rows, dec_down, smalls, 6, 8, inner, "dec_ffn"
-    )
-
-    dd_inner, dd_down, d_two, d_cross, d_cctx, sums_d = ffn_backward(
-        dec_plan, [dec_cot], (f_hat, f_inv), d_slope, (c_hat, c_inv), (dec_four, dec_rows, dec_rows),
-        [dec_up, dec_down, at_block((width, width), 7, 0)], smalls, 6, 8, "dec_ffn_back",
-    )
-    g_dup, g_ddown, g_cout = ffn_weights(
-        dec_plan, c_hat, dd_inner, dd_down, d_hidden, c_ctx, d_cross, smalls, 6, "dec_ffn_weights"
+    e_q, e_kv, e_ctx, e_lse, e_hat, e_inv, memory, t_hat, t_inv = fwd_block(
+        enc_plan, src_in, None, far, (enc_qkv, enc_wo, enc_up, enc_down), True, smalls, 0, src_owner, src_key, True,
+        "enc_layer",
+    )
+    s_q, s_kv, s_ctx, s_lse, s_hat, s_inv = fwd_block(
+        dec_plan, start, None, far, (self_qkv, self_wo), False, smalls, 4, tgt_owner, tgt_key, False, "dec_block"
+    )
+    c_q, c_kv, c_ctx, c_lse, c_hat, c_inv, decoded, f_hat, f_inv = fwd_block(
+        cross_plan, s_hat, memory, far, (cross_kv, cross_wo, cross_q, dec_up, dec_down), True, smalls, 6,
+        tgt_owner, src_key, True, "cross_layer",
+    )
+
+    d_two, d_cctx, g_dup, g_ddown, g_cout, sums_d = ffn_backward(
+        dec_plan, [dec_cot], (f_hat, f_inv), (c_hat, c_inv), c_ctx, far, (dec_up, dec_down, cross_wo), smalls, 6,
+        inner, "dec_ffn_back",
     )
     dcq, dck, dcv = attention_backward(cross_plan, c_q, c_kv, d_cctx, c_lse, tgt_owner, src_key, "cross_back")
     d_memory, d_one, d_sctx, g_cq, g_ckv, g_sout, sums_c = cross_projections_back(
-        dec_plan, dcq, dck, dcv, s_hat, s_inv, d_two, memory, s_ctx, dec_rows, dec_two, smalls
+        dec_plan, dcq, dck, dcv, s_hat, s_inv, d_two, memory, s_ctx, far, (cross_kv, cross_q, self_wo), smalls,
     )
     dsq, dsk, dsv = attention_backward(dec_plan, s_q, s_kv, d_sctx, s_lse, tgt_owner, tgt_key, "dec_back")
     g_sqkv = qkv_weights(dec_plan, start, dsq, dsk, dsv, False, "dec_qkv_weights")
     dec_pieces = [
-        g_sqkv.transpose(1, 0, 2).reshape(-1, width),
+        g_sqkv,
         g_sout,
         g_cq,
         g_ckv.reshape(-1, width),
@@ -1029,8 +1115,6 @@
         g_dup.reshape(-1, width),
         g_ddown,
     ]
-    by_rounds = devices == 1 << BITS
-    rounds = None
     if by_rounds:
         core = bit_of(me, CORE)[None].astype(jnp.int32)
         copies = overlaps([p.shape[0] for p in dec_pieces], dec_size)
@@ -1038,18 +1122,13 @@
         rounds = Rounds(reduce_owned(me, send, keep, dec_size // 2))
         dsq, dsk, dsv = rounds.before(dsq, dsk, dsv)
     tgt_grad, mask_sum = qkv_inputs(
-        dec_plan, dsq, dsk, dsv, d_one, dec_three, whole(dec_three.shape), flags, "dec_qkv_inputs"
+        dec_plan, dsq, dsk, dsv, d_one, far, (self_qkv,), flags, "dec_qkv_inputs"
     )
     if by_rounds:
         d_memory, mask_sum = rounds.before(d_memory, mask_sum)
-    de_inner, de_down, d_mid, d_eattn, d_ectx, sums_e = ffn_backward(
-        enc_plan, [enc_cot, d_memory], (t_hat, t_inv), e_slope, (e_hat, e_inv), (enc_four, enc_rows, enc_rows),
-        [enc_up, enc_down, enc_wo], smalls, 0, 2, "enc_ffn_back",
-    )
-    if by_rounds:
-        de_inner, d_ectx = rounds.before(de_inner, d_ectx)
-    g_up, g_down, g_out = ffn_weights(
-        enc_plan, e_hat, de_inner, de_down, e_hidden, e_ctx, d_eattn, smalls, 0, "enc_ffn_weights"
+    d_mid, d_ectx, g_up, g_down, g_out, sums_e = ffn_backward(
+        enc_plan, [enc_cot, d_memory], (t_hat, t_inv), (e_hat, e_inv), e_ctx, far,
+        (enc_up, enc_down, enc_wo), smalls, 0, inner, "enc_ffn_back",
     )
     if by_rounds:
         d_ectx, g_up = rounds.before(d_ectx, g_up)
@@ -1060,9 +1139,7 @@
 
     enc_pieces = [g_qkv.reshape(-1, width), g_out, g_up.reshape(-1, width), g_down]
     small_grad = jnp.concatenate([sums_e[:4], sums_c[:2], sums_d[:4], mask_sum[:1]], axis=0)
-    share = small_master.shape[1]
     small_wire = small_grad.reshape(-1, devices, share).transpose(1, 0, 2).reshape(devices, -1).astype(LOW)
-    held = small_wire.shape[1]
     small_wire = jnp.pad(small_wire, ((0, 0), (0, 16 * width - held))).reshape(devices * 16, width)
     if by_rounds:
         dec_summed = rounds.finish()
@@ -1071,7 +1148,7 @@
         send, keep = pack(core, enc_pieces + [small_wire], copies, enc_size + 16, "enc_pack")
         rounds = Rounds(reduce_owned(me, send, keep, enc_size // 2 + 16))
         deq, dek, dev = rounds.before(deq, dek, dev)
-    src_grad = qkv_inputs(enc_plan, deq, dek, dev, d_mid, enc_three, three_spec, None, "enc_qkv_inputs")[0]
+    src_grad = qkv_inputs(enc_plan, deq, dek, dev, d_mid, far, (enc_qkv,), None, "enc_qkv_inputs")[0]
     if by_rounds:
         enc_summed = rounds.finish()
     else:

time: 513 us -> 473 us (0.922)
  blocking collectives: 43.9 us -> 0 us
  waiting for transfers between devices: 111 us -> 137 us
  starting transfers between devices: 28 us -> 16.6 us
  local copies, waits for them, and re-layouts: 26.4 us -> 20.6 us
    all_gather x1 -> x0, blocking collectives: 43.9 us -> none  [on_device(): lax.all_gather(small_master.astype(LOW), 'fsdp', axis=1, tiled=True)]
    all_gather x2 -> x1, waiting for transfers between devices: 58.8 us -> 100 us  [on_device(): lax.all_gather(jnp.concatenate([enc_own, dec_own, own], axis=0), 'fsdp',...]
    ppermute x14, waiting for transfers between devices: 52.2 us -> 37.4 us  [swap(): return lax.ppermute(values, 'fsdp', partner(bit))]
    ppermute x14, starting transfers between devices: 27.9 us -> 16.6 us  [swap(): return lax.ppermute(values, 'fsdp', partner(bit))]
    reshape x4 -> x3, local copies, waits for them, and re-layouts: 7.94 us -> 0.19 us  [the longest x1 0.09 us: on_device(): small_master.astype(LOW).reshape(-1)]
    pallas_call x19 -> x15, Pallas kernels: 248 us -> 243 us  [run(): return made(plan, *placed)]
  transfers between devices with their start and end apart: 16 -> 15, of which waited for: 12 -> 7; matrix products, arithmetic and copies ran while one was open for 6% -> 6% of each run, Pallas kernels for 20% -> 14%
where the time goes in v3:
time: 473 us; the launch traced here: 464 us
  Pallas kernels  243 us (51%)
  waiting for transfers between devices  137 us (29%)
  other arithmetic  31.5 us (7%)
  local copies, waits for them, and re-layouts  20.6 us (4%)
  starting transfers between devices  16.6 us (4%)
  between operations  15.5 us (3%)
    pallas_call x15, Pallas kernels, run(): return made(plan, *placed)  243 us
    all_gather x1, waiting for transfers between devices, on_device(): lax.all_gather(jnp.concatenate([enc_own, dec_own, own], axis=0), 'fsdp',...  100 us
    ppermute x14, waiting for transfers between devices, swap(): return lax.ppermute(values, 'fsdp', partner(bit))  37.4 us
    ppermute x14, starting transfers between devices, swap(): return lax.ppermute(values, 'fsdp', partner(bit))  16.6 us
    convert_element_type x12, other arithmetic, add_low(): return (former.astype(F32) + latter.astype(F32)).astype(LOW)  12.7 us
  transfers between devices with their start and end apart: 15, of which 7 were waited for; matrix products, arithmetic and copies ran while one was open for 6% of the time, Pallas kernels for 14%

profile of v3, /device:TPU:0, one launch (start us, length us, event | category | flops | bytes accessed | tf_op | source)
XLA Modules:
  0.0 464.2 jit_solution(13869103646027994972)
XLA Ops:
  7.2 1.1 convert_element_type.257
  9.8 0.8 pad_maximum_fusion
  12.8 0.7 minimum_add_fusion.1
  14.4 0.7 fusion.27
  15.0 0.7 fusion.25
  15.7 0.7 compare_select_fusion.23
  16.3 0.7 compare_select_fusion.22
  17.0 0.7 fusion.26
  17.7 0.7 fusion.24
  19.9 1.9 fusion.19
  21.8 100.1 %all-gather.3.cloned.1.call-done = bf16[14848,512]{1,0:T(8,128)(2,1)} async-done(((bf16[464,512]{1,0:T(8,128)(2,1)}), bf16[14848,512]{1,0:T(8,128)(2,1)}) %all-gather.3.cloned.1.call-update) | async-done | bytes 15204368 | tf_op jit(solution)/shard_map/all_gather | solution.py:1047
  121.9 0.9 slice.75
  124.0 1.2 broadcast_select_fusion.refs_0_.x
  125.2 19.4 %dec_block.1 = (bf16[1024,512]{1,0:T(8,128)(2,1)}, bf16[1024,1024]{1,0:T(8,128)(2,1)}, bf16[1024,512]{1,0:T(8,128)(2,1)}, f32[8,1024]{1,0:T(8,128)}, f32[1024,512]{1,0:T(8,128)}, /*index=5*/f32[1024,128]{1,0:T(8,128)}) custom-call(s32[3,8]{1,0:T(4,128)S(1)} %get-tuple-element.204.plan, bf16[1024,512]{1,0:T(8,128)(2,1)} %broadcast_select_fusion.refs_0_.x, ...), custom_call_target="tpu_custom_call" | custom-call | flops 3221225472 | bytes 8388608 | tf_op jit(solution)/shard_map/dec_block/pallas_call | solution.py:196
  144.6 27.0 %enc_layer.1 = (bf16[1024,512]{1,0:T(8,128)(2,1)}, bf16[1024,1024]{1,0:T(8,128)(2,1)}, bf16[1024,512]{1,0:T(8,128)(2,1)}, f32[8,1024]{1,0:T(8,128)}, f32[1024,51...) custom-call(s32[3,8]{1,0:T(4,128)S(1)} %get-tuple-element.206.plan, ...), custom_call_target="tpu_custom_call" | custom-call | flops 3221225472 | bytes 8388608 | tf_op jit(solution)/shard_map/enc_layer/pallas_call | solution.py:196
  171.6 26.8 %cross_layer.1 = (bf16[1024,512]{1,0:T(8,128)(2,1)}, bf16[1024,1024]{1,0:T(8,128)(2,1)}, bf16[1024,512]{1,0:T(8,128)(2,1)}, f32[8,1024]{1,0:T(8,128)}, f32[1024,...) custom-call(s32[3,8]{1,0:T(4,128)S(1)} %get-tuple-element.205.plan, ...), custom_call_target="tpu_custom_call" | custom-call | flops 3221225472 | bytes 8388608 | tf_op jit(solution)/shard_map/cross_layer/pallas_call | solution.py:196
  198.4 25.7 %dec_ffn_back.1 = (f32[1024,512]{1,0:T(8,128)}, bf16[1024,512]{1,0:T(8,128)(2,1)}, bf16[32,4,16,512]{3,2,1,0:T(8,128)(2,1)}, bf16[2048,512]{1,0:T(8,128)(2,1)}, ...) custom-call(s32[3,8]{1,0:T(4,128)S(1)} %get-tuple-element.204.plan, bf16[1024,512]{1,0:T(8,128)(2,1)} %refs_0_.4, ...), custom_call_target="tpu_custom_call" | custom-call | flops 10737418240 | bytes 15728640 | tf_op jit(solution)/shard_map/dec_ffn_back/pallas_call | solution.py:196
  224.1 21.3 %cross_back.1 = (bf16[1024,512]{1,0:T(8,128)(2,1)}, bf16[1024,512]{1,0:T(8,128)(2,1)}, bf16[1024,512]{1,0:T(8,128)(2,1)}) custom-call(s32[3,8]{1,0:T(4,128)S(1)} %get-tuple-element.205.plan, bf16[1024,512]{1,0:T(8,128)(2,1)} %get-tuple-element.98.q_ref, bf16[1024,1024]{1,0:T(8,128)(2,1)} %get-tuple-element.99.k_ref.v_ref, ...), custom_call_target="tpu_custom_call" | custom-call | flops 2147483648 | bytes 6291456 | tf_op jit(solution)/shard_map/cross_back/pallas_call | solution.py:196
  245.4 14.1 %cross_projections_back.1 = (f32[1024,512]{1,0:T(8,128)}, f32[1024,512]{1,0:T(8,128)}, bf16[1024,512]{1,0:T(8,128)(2,1)}, bf16[512,512]{1,0:T(8,128)(2,1)}, bf16...) custom-call(s32[3,8]{1,0:T(4,128)S(1)} %get-tuple-element.204.plan, ...), custom_call_target="tpu_custom_call" | custom-call | flops 4294967296 | bytes 12582912 | tf_op jit(solution)/shard_map/cross_projections_back/pallas_call | solution.py:196
  259.5 23.0 %dec_back.1 = (bf16[1024,512]{1,0:T(8,128)(2,1)}, bf16[1024,512]{1,0:T(8,128)(2,1)}, bf16[1024,512]{1,0:T(8,128)(2,1)}) custom-call(s32[3,8]{1,0:T(4,128)S(1)} %get-tuple-element.204.plan, bf16[1024,512]{1,0:T(8,128)(2,1)} %get-tuple-element.96.q_ref, bf16[1024,1024]{1,0:T(8,128)(2,1)} %get-tuple-element.97.k_ref.v_ref, ...), custom_call_target="tpu_custom_call" | custom-call | flops 2147483648 | bytes 6291456 | tf_op jit(solution)/shard_map/dec_back/pallas_call | solution.py:196
  282.5 6.7 %dec_qkv_weights.1.refs_0_ = bf16[1536,512]{1,0:T(8,128)(2,1)} custom-call(s32[3,8]{1,0:T(4,128)S(1)} %get-tuple-element.204.plan, bf16[1024,512]{1,0:T(8,128)(2,1)} %broadcast_select_fusion.refs_0_.x, bf16[1024,512]{1,0:T(8,128)(2,1)} %get-tuple-element.128.dq.refs_0_, bf16[1024,512]{1,0:T(8,128)(2,1)} %get-tuple-element.129.dk.refs_1_, ...), custom_call_target="tpu_custom_call" | custom-call | flops 1610612736 | bytes 6291456 | tf_op jit(solution)/shard_map/dec_qkv_weights/pallas_call | solution.py:196
  289.2 1.4 copy-done.4
  290.6 3.5 dec_pack.1
  294.8 8.7 %dec_qkv_inputs.1 = (f32[1024,512]{1,0:T(8,128)}, f32[8,512]{1,0:T(8,128)}) custom-call(s32[3,8]{1,0:T(4,128)S(1)} %get-tuple-element.204.plan, bf16[1024,512]{1,0:T(8,128)(2,1)} %get-tuple-element.128.dq.refs_0_, bf16[1024,512]{1,0:T(8,128)(2,1)} %get-tuple-element.129.dk.refs_1_, bf16[1024,512]{1,0:T(8,128)(2,1)} %get-tuple-element.130.dv.refs_2_, ...), custom_call_target="tpu_custom_call" | custom-call | flops 1610612736 | bytes 8388608 | tf_op jit(solution)/shard_map/dec_qkv_inputs/pallas_call | solution.py:196
  303.5 3.2 add_convert_fusion
  307.6 1.5 collective-permute-start.2
  309.7 26.0 %enc_ffn_back.1 = (f32[1024,512]{1,0:T(8,128)}, bf16[1024,512]{1,0:T(8,128)(2,1)}, bf16[32,4,16,512]{3,2,1,0:T(8,128)(2,1)}, bf16[2048,512]{1,0:T(8,128)(2,1)}, ...) custom-call(s32[3,8]{1,0:T(4,128)S(1)} %get-tuple-element.206.plan, bf16[1024,512]{1,0:T(8,128)(2,1)} %refs_0_.5, ...), custom_call_target="tpu_custom_call" | custom-call | flops 10737418240 | bytes 15728640 | tf_op jit(solution)/shard_map/enc_ffn_back/pallas_call | solution.py:196
  336.0 0.9 dynamic-slice_bitcast_fusion
  337.3 0.8 dynamic-slice_bitcast_fusion.1
  338.1 1.5 collective-permute-start.4
  339.6 0.7 slice.99
  340.3 0.7 slice.97
  341.0 0.7 slice.98
  341.7 0.7 slice.100
  343.7 23.0 %enc_back.1 = (bf16[1024,512]{1,0:T(8,128)(2,1)}, bf16[1024,512]{1,0:T(8,128)(2,1)}, bf16[1024,512]{1,0:T(8,128)(2,1)}) custom-call(s32[3,8]{1,0:T(4,128)S(1)} %get-tuple-element.206.plan, bf16[1024,512]{1,0:T(8,128)(2,1)} %get-tuple-element.145.q_ref, bf16[1024,1024]{1,0:T(8,128)(2,1)} %get-tuple-element.146.k_ref.v_ref, ...), custom_call_target="tpu_custom_call" | custom-call | flops 2147483648 | bytes 6291456 | tf_op jit(solution)/shard_map/enc_back/pallas_call | solution.py:196
  366.8 1.2 fusion.6
  368.1 0.8 fusion.13
  368.9 6.5 %enc_qkv_weights.1 = bf16[32,3,16,512]{3,2,1,0:T(8,128)(2,1)} custom-call(s32[3,8]{1,0:T(4,128)S(1)} %get-tuple-element.206.plan, bf16[1024,512]{1,0:T(8,128)(2,1)} %x.7, bf16[1024,512]{1,0:T(8,128)(2,1)} %get-tuple-element.163.dq.refs_0_, bf16[1024,512]{1,0:T(8,128)(2,1)} %get-tuple-element.164.dk.refs_1_, bf16[1024,512]{1,0:T(8,128)(2,1)} %get-tuple-element.165.dv.refs_2_), custom_call_target="tpu_custom_call" | custom-call | flops 1610612736 | bytes 6291456 | tf_op jit(solution)/shard_map/enc_qkv_weights/pallas_call | solution.py:196
  375.4 1.4 copy-done.5
  376.8 3.4 enc_pack.1
  380.3 6.2 %collective-permute-done.5 = bf16[16,208,512]{2,1,0:T(8,128)(2,1)S(1)} collective-permute-done((bf16[16,208,512]{2,1,0:T(8,128)(2,1)}, bf16[16,208,512]{2,1,0:T(8,128)(2,1)S(1)}, u32[]{:S(2)}, u32[]{:S(2)}) %collective-permute-start.5) | collective-permute-done | bytes 3407904 | tf_op jit(solution)/shard_map/ppermute | solution.py:968
  386.5 2.7 add_convert_fusion.1
  389.4 1.1 constant_dynamic-slice_fusion.1
  390.6 0.9 copy.136
  391.8 1.0 copy.135
  392.8 2.0 collective-permute-start.6
  394.8 1.2 collective-permute-start.12
  396.1 15.4 %collective-permute-done.8 = bf16[2,2,2,96,512]{4,3,0,1,2:T(8,128)(2,1)} collective-permute-done((bf16[2,2,2,96,512]{4,3,0,1,2:T(8,128)(2,1)}, bf16[2,2,2,96,512]{4,3,0,1,2:T(8,128)(2,1)}, u32[]{:S(2)}, u32[]{:S(2)}) %collective-permute-start.8) | collective-permute-done | bytes 786464 | tf_op jit(solution)/shard_map/ppermute | solution.py:968
  411.4 1.6 fusion.3
  413.0 1.5 collective-permute-start.9
  414.6 1.3 collective-permute-done.6
  415.8 1.5 fusion.2
  417.4 2.6 collective-permute-start.7
  420.2 3.6 collective-permute-done.9
  423.9 4.9 %collective-permute-done.7 = bf16[2,2,112,512]{3,2,0,1:T(8,128)(2,1)S(1)} collective-permute-done((bf16[2,2,112,512]{3,2,0,1:T(8,128)(2,1)S(1)}, bf16[2,2,112,512]{3,2,0,1:T(8,128)(2,1)S(1)}, u32[]{:S(2)}, u32[]{:S(2)}) %collective-permute-start.7) | collective-permute-done | bytes 458784 | tf_op jit(solution)/shard_map/ppermute | solution.py:968
  429.0 0.8 fusion.15
  429.8 3.1 collective-permute-start.10
  432.9 7.7 %enc_qkv_inputs.1 = f32[1024,512]{1,0:T(8,128)} custom-call(s32[3,8]{1,0:T(4,128)S(1)} %get-tuple-element.206.plan, bf16[1024,512]{1,0:T(8,128)(2,1)} %get-tuple-element.163.dq.refs_0_, bf16[1024,512]{1,0:T(8,128)(2,1)} %get-tuple-element.164.dk.refs_1_, bf16[1024,512]{1,0:T(8,128)(2,1)} %get-tuple-element.165.dv.refs_2_, ...), custom_call_target="tpu_custom_call" | custom-call | flops 1610612736 | bytes 8388608 | tf_op jit(solution)/shard_map/enc_qkv_inputs/pallas_call | solution.py:196
  441.6 1.2 reshape.658
  442.8 1.3 fusion.8
  444.1 1.7 collective-permute-start.11
  445.8 1.8 fusion.29
  447.6 6.0 %collective-permute-done.11 = bf16[208,512]{1,0:T(8,128)(2,1)S(1)} collective-permute-done((bf16[208,512]{1,0:T(8,128)(2,1)S(1)}, bf16[208,512]{1,0:T(8,128)(2,1)S(1)}, u32[]{:S(2)}, u32[]{:S(2)}) %collective-permute-start.11) | collective-permute-done | bytes 213024 | tf_op jit(solution)/shard_map/ppermute | solution.py:968
  455.4 1.5 fusion.30
  (164 shorter events, 15.0 us)
Async XLA Ops:
  7.2 1.4 copy-start.15
  7.2 114.7 %all-gather.3.cloned.1.call-start = ((), (), s32[]{:S(2)}) async-start(), calls=%async_computation | async-start | bytes 15679488 | tf_op jit(solution)/shard_map/all_gather | solution.py:1047
  8.4 0.7 copy-start.24
  8.4 1.0 copy-start.11
  8.8 1.0 copy-start.27
  9.0 1.6 copy-start.30
  9.0 2.4 copy-start.29
  9.0 10.8 %copy-start.23 = (s32[1024]{0:T(1024)S(1)}, s32[1024]{0:T(1024)}, u32[]{:S(2)}) copy-start(s32[1024]{0:T(1024)} %param.20) | copy-start | bytes 12292
  9.5 114.5 %copy-start.17 = (bf16[1024,512]{1,0:T(8,128)(2,1)S(1)}, bf16[1024,512]{1,0:T(8,128)(2,1)}, u32[]{:S(2)}) copy-start(bf16[1024,512]{1,0:T(8,128)(2,1)} %param.17) | copy-start | bytes 3145732
  259.5 29.7 %copy-start.8 = (bf16[512,512]{1,0:T(8,128)(2,1)S(1)}, bf16[512,512]{1,0:T(8,128)(2,1)}, u32[]{:S(2)}) copy-start(bf16[512,512]{1,0:T(8,128)(2,1)} %get-tuple-element.119.refs_2_) | copy-start | bytes 1572868
  259.5 29.7 %copy-start.9 = (bf16[512,512]{1,0:T(8,128)(2,1)S(1)}, bf16[512,512]{1,0:T(8,128)(2,1)}, u32[]{:S(2)}) copy-start(bf16[512,512]{1,0:T(8,128)(2,1)} %get-tuple-element.118.refs_1_) | copy-start | bytes 1572868
  282.5 6.7 %copy-start.2 = (bf16[32,4,16,512]{3,2,1,0:T(8,128)(2,1)S(1)}, bf16[32,4,16,512]{3,2,1,0:T(8,128)(2,1)}, u32[]{:S(2)}) copy-start(bf16[32,4,16,512]{3,2,1,0:T(8,128)(2,1)} %get-tuple-element.122) | copy-start | bytes 6291460
  282.5 6.7 %copy-start.3 = (bf16[2048,512]{1,0:T(8,128)(2,1)S(1)}, bf16[2048,512]{1,0:T(8,128)(2,1)}, u32[]{:S(2)}) copy-start(bf16[2048,512]{1,0:T(8,128)(2,1)} %get-tuple-element.123.refs_6_) | copy-start | bytes 6291460
  282.5 6.7 %copy-start.6 = (bf16[32,2,16,512]{3,2,1,0:T(8,128)(2,1)S(1)}, bf16[32,2,16,512]{3,2,1,0:T(8,128)(2,1)}, u32[]{:S(2)}) copy-start(bf16[32,2,16,512]{3,2,1,0:T(8,128)(2,1)} %get-tuple-element.120) | copy-start | bytes 3145732
  282.5 6.7 %copy-start.7 = (bf16[512,512]{1,0:T(8,128)(2,1)S(1)}, bf16[512,512]{1,0:T(8,128)(2,1)}, u32[]{:S(2)}) copy-start(bf16[512,512]{1,0:T(8,128)(2,1)} %get-tuple-element.121.refs_4_) | copy-start | bytes 1572868
  289.2 1.4 copy-start.4
  294.1 9.3 %collective-permute-start = (bf16[16,256,512]{2,1,0:T(8,128)(2,1)}, bf16[16,256,512]{2,1,0:T(8,128)(2,1)}, u32[]{:S(2)}, u32[]{:S(2)}) collective-permute-start(bf16[16,256,512]{2,1,0:T(8,128)(2,1)} %get-tuple-element.126), channel_id=1, source_target_pairs={{0,1},{1,0},{2,3},{3,2},{4,5},{5,4},{6,7},{7,6},{8,9},{9,8},{10,11... | collective-permute-start | bytes 12582920 | tf_op jit(solution)/shard_map/ppermute | solution.py:968
  294.8 8.7 %copy-start.12 = (bf16[16,256,512]{2,1,0:T(8,128)(2,1)S(1)}, bf16[16,256,512]{2,1,0:T(8,128)(2,1)}, u32[]{:S(2)}) copy-start(bf16[16,256,512]{2,1,0:T(8,128)(2,1)} %get-tuple-element.124) | copy-start | bytes 12582916
  307.6 28.1 %collective-permute-start.2 = (bf16[2,2,2,128,512]{4,3,0,1,2:T(8,128)(2,1)S(1)}, bf16[2,2,2,128,512]{4,3,0,1,2:T(8,128)(2,1)S(1)}, u32[]{:S(2)}, u32[]{:S(2)}) collective-permute-start(bf16[2,2,2,128,512]{4,3,0,1,2:T(8,128)(2,1)S(1)} %bitcast.222), channel_id=1, source_target_pairs={{0,2},{1,3},{2,0},{3,1},{4,6},{5,7},{6,4},{7,5},{8,10},{9,11},{10,... | collective-permute-start | bytes 3145736 | tf_op jit(solution)/shard_map/ppermute | solution.py:968
  309.1 27.8 %collective-permute-start.1 = (bf16[2,2,2,128,512]{4,3,0,1,2:T(8,128)(2,1)S(1)}, bf16[2,2,2,128,512]{4,3,0,1,2:T(8,128)(2,1)S(1)}, u32[]{:S(2)}, u32[]{:S(2)}) collective-permute-start(bf16[2,2,2,128,512]{4,3,0,1,2:T(8,128)(2,1)S(1)} %bitcast.221), channel_id=1, source_target_pairs={{0,4},{1,5},{2,6},{3,7},{4,0},{5,1},{6,2},{7,3},{8,12},{9,13},{10,... | collective-permute-start | bytes 3145736 | tf_op jit(solution)/shard_map/ppermute | solution.py:968
  336.0 1.2 copy-start.13
  338.1 28.6 %collective-permute-start.4 = (bf16[2,2,128,512]{3,2,0,1:T(8,128)(2,1)}, bf16[2,2,128,512]{3,2,0,1:T(8,128)(2,1)S(1)}, u32[]{:S(2)}, u32[]{:S(2)}) collective-permute-start(bf16[2,2,128,512]{3,2,0,1:T(8,128)(2,1)} %dynamic-slice_bitcast_fusion), channel_id=1, source_target_pairs={{0,4},{1,5},{2,6},{3,7},{4,0},{5,1},{6,2},{7,3},{8,12},{9,13},{10,... | collective-permute-start | bytes 1572872 | tf_op jit(solution)/shard_map/ppermute | solution.py:968
  342.4 24.4 %collective-permute-start.3 = (bf16[2,2,128,512]{3,2,0,1:T(8,128)(2,1)}, bf16[2,2,128,512]{3,2,0,1:T(8,128)(2,1)}, u32[]{:S(2)}, u32[]{:S(2)}) collective-permute-start(bf16[2,2,128,512]{3,2,0,1:T(8,128)(2,1)} %dynamic-slice_bitcast_fusion.1), channel_id=1, source_target_pairs={{0,2},{1,3},{2,0},{3,1},{4,6},{5,7},{6,4},{7,5},{8,10},{9,11},{10,... | collective-permute-start | bytes 1572872 | tf_op jit(solution)/shard_map/ppermute | solution.py:968
  343.7 23.0 %copy-start.14 = (bf16[2,2,2,128,512]{4,3,0,1,2:T(8,128)(2,1)S(1)}, bf16[2,2,2,128,512]{4,3,0,1,2:T(8,128)(2,1)}, u32[]{:S(2)}) copy-start(bf16[2,2,2,128,512]{4,3,0,1,2:T(8,128)(2,1)} %copy-done.13) | copy-start | bytes 3145732
  368.9 6.5 %copy-start = (bf16[32,4,16,512]{3,2,1,0:T(8,128)(2,1)S(1)}, bf16[32,4,16,512]{3,2,1,0:T(8,128)(2,1)}, u32[]{:S(2)}) copy-start(bf16[32,4,16,512]{3,2,1,0:T(8,128)(2,1)} %get-tuple-element.156) | copy-start | bytes 6291460
  368.9 6.5 %copy-start.1 = (bf16[2048,512]{1,0:T(8,128)(2,1)S(1)}, bf16[2048,512]{1,0:T(8,128)(2,1)}, u32[]{:S(2)}) copy-start(bf16[2048,512]{1,0:T(8,128)(2,1)} %get-tuple-element.157.refs_3_) | copy-start | bytes 6291460
  368.9 6.5 %copy-start.10 = (bf16[512,512]{1,0:T(8,128)(2,1)S(1)}, bf16[512,512]{1,0:T(8,128)(2,1)}, u32[]{:S(2)}) copy-start(bf16[512,512]{1,0:T(8,128)(2,1)} %get-tuple-element.155.refs_1_) | copy-start | bytes 1572868
  375.4 1.4 copy-start.5
  380.2 6.3 %collective-permute-start.5 = (bf16[16,208,512]{2,1,0:T(8,128)(2,1)}, bf16[16,208,512]{2,1,0:T(8,128)(2,1)S(1)}, u32[]{:S(2)}, u32[]{:S(2)}) collective-permute-start(bf16[16,208,512]{2,1,0:T(8,128)(2,1)} %get-tuple-element.169), channel_id=1, source_target_pairs={{0,1},{1,0},{2,3},{3,2},{4,5},{5,4},{6,7},{7,6},{8,9},{9,8},{10,11... | collective-permute-start | bytes 10223624 | tf_op jit(solution)/shard_map/ppermute | solution.py:968
  391.5 19.9 %collective-permute-start.8 = (bf16[2,2,2,96,512]{4,3,0,1,2:T(8,128)(2,1)}, bf16[2,2,2,96,512]{4,3,0,1,2:T(8,128)(2,1)}, u32[]{:S(2)}, u32[]{:S(2)}) collective-permute-start(bf16[2,2,2,96,512]{4,3,0,1,2:T(8,128)(2,1)} %bitcast.197), channel_id=1, source_target_pairs={{0,2},{1,3},{2,0},{3,1},{4,6},{5,7},{6,4},{7,5},{8,10},{9,11},{10,... | collective-permute-start | bytes 2359304 | tf_op jit(solution)/shard_map/ppermute | solution.py:968
  391.6 3.2 copy-start.18
  392.8 23.0 %collective-permute-start.6 = (bf16[2,2,2,112,512]{4,3,0,1,2:T(8,128)(2,1)}, bf16[2,2,2,112,512]{4,3,0,1,2:T(8,128)(2,1)}, u32[]{:S(2)}, u32[]{:S(2)}) collective-permute-start(bf16[2,2,2,112,512]{4,3,0,1,2:T(8,128)(2,1)} %bitcast.196), channel_id=1, source_target_pairs={{0,4},{1,5},{2,6},{3,7},{4,0},{5,1},{6,2},{7,3},{8,12},{9,13},{10,... | collective-permute-start | bytes 2752520 | tf_op jit(solution)/shard_map/ppermute | solution.py:968
  394.8 25.2 %collective-permute-start.12 = (bf16[2,256,512]{2,1,0:T(8,128)(2,1)S(1)}, bf16[2,256,512]{2,1,0:T(8,128)(2,1)S(1)}, u32[]{:S(2)}, u32[]{:S(2)}) collective-permute-start(bf16[2,256,512]{2,1,0:T(8,128)(2,1)S(1)} %copy-done.18), channel_id=1, source_target_pairs={{0,8},{1,9},{2,10},{3,11},{4,12},{5,13},{6,14},{7,15},{8,0},{9,1},... | collective-permute-start | bytes 1572872 | tf_op jit(solution)/shard_map/ppermute | solution.py:968
  413.0 10.8 %collective-permute-start.9 = (bf16[2,2,96,512]{3,2,0,1:T(8,128)(2,1)S(1)}, bf16[2,2,96,512]{3,2,0,1:T(8,128)(2,1)S(1)}, u32[]{:S(2)}, u32[]{:S(2)}) collective-permute-start(bf16[2,2,96,512]{3,2,0,1:T(8,128)(2,1)S(1)} %dynamic-slice_bitcast_fusion.3), channel_id=1, source_target_pairs={{0,4},{1,5},{2,6},{3,7},{4,0},{5,1},{6,2},{7,3},{8,12},{9,13},{10,... | collective-permute-start | bytes 1179656 | tf_op jit(solution)/shard_map/ppermute | solution.py:968
  417.4 11.5 %collective-permute-start.7 = (bf16[2,2,112,512]{3,2,0,1:T(8,128)(2,1)S(1)}, bf16[2,2,112,512]{3,2,0,1:T(8,128)(2,1)S(1)}, u32[]{:S(2)}, u32[]{:S(2)}) collective-permute-start(bf16[2,2,112,512]{3,2,0,1:T(8,128)(2,1)S(1)} %dynamic-slice_bitcast_fusion.2), channel_id=1, source_target_pairs={{0,2},{1,3},{2,0},{3,1},{4,6},{5,7},{6,4},{7,5},{8,10},{9,11},{10,... | collective-permute-start | bytes 1376264 | tf_op jit(solution)/shard_map/ppermute | solution.py:968
  420.2 20.4 %collective-permute-start.13 = (bf16[256,512]{1,0:T(8,128)(2,1)S(1)}, bf16[256,512]{1,0:T(8,128)(2,1)S(1)}, u32[]{:S(2)}, u32[]{:S(2)}) collective-permute-start(bf16[256,512]{1,0:T(8,128)(2,1)S(1)} %dynamic-slice_bitcast_fusion.4), channel_id=1, source_target_pairs={{0,16},{1,17},{2,18},{3,19},{4,20},{5,21},{6,22},{7,23},{8,24},{9,... | collective-permute-start | bytes 786440 | tf_op jit(solution)/shard_map/ppermute | solution.py:968
  429.8 13.0 %collective-permute-start.10 = (bf16[2,208,512]{2,1,0:T(8,128)(2,1)}, bf16[2,208,512]{2,1,0:T(8,128)(2,1)}, u32[]{:S(2)}, u32[]{:S(2)}) collective-permute-start(bf16[2,208,512]{2,1,0:T(8,128)(2,1)} %fusion.15), channel_id=1, source_target_pairs={{0,8},{1,9},{2,10},{3,11},{4,12},{5,13},{6,14},{7,15},{8,0},{9,1},... | collective-permute-start | bytes 1277960 | tf_op jit(solution)/shard_map/ppermute | solution.py:968
  441.2 4.6 copy-start.28
  442.7 3.1 copy-start.16
  442.7 3.1 copy-start.19
  442.7 3.1 copy-start.20
  444.1 9.6 %collective-permute-start.11 = (bf16[208,512]{1,0:T(8,128)(2,1)S(1)}, bf16[208,512]{1,0:T(8,128)(2,1)S(1)}, u32[]{:S(2)}, u32[]{:S(2)}) collective-permute-start(bf16[208,512]{1,0:T(8,128)(2,1)S(1)} %dynamic-slice_bitcast_fusion.5), channel_id=1, source_target_pairs={{0,16},{1,17},{2,18},{3,19},{4,20},{5,21},{6,22},{7,23},{8,24},{9,... | collective-permute-start | bytes 638984 | tf_op jit(solution)/shard_map/ppermute | solution.py:968
  453.7 1.1 copy-start.25
  453.7 1.1 copy-start.26
  453.7 1.7 copy-start.21
  453.8 1.7 copy-start.22
Sparse Core Ops, SparseCore 0:
  11.4 110.4 all-gather.2
